TPU v7x, 32 devices: a whole 2x2x4 slice. The times are simulated.
32 devices in a mesh: wide: 16 (over z, y, x), narrow: 2 (over core).
Axes of the slice: x: 2, y: 2, z: 4, core: 2. Of those that a mesh axis runs over, the one named last changes fastest.
Arguments:
- tokens: bfloat16 [2048, 2048], P('wide', 'narrow'), may hold values from -6 to 6
- expert_ids: int32 [2048, 6], P('wide'), may hold values from 0 to 15, all different within a row; in each aligned block of 128 rows (0 to 127, 128 to 255, ...) at most 54 rows name the same one
- route_gates: float32 [2048, 6], P('wide'), may hold values from 0.05 to 0.6
- expert_gate: bfloat16 [16, 1408, 2048], P('wide', 'narrow'), may hold values from -0.125 to 0.125
- expert_up: bfloat16 [16, 1408, 2048], P('wide', 'narrow'), may hold values from -0.125 to 0.125
- expert_down: bfloat16 [16, 1408, 2048], P('wide', 'narrow'), may hold values from -0.21875 to 0.21875
- shared_gate: bfloat16 [2048, 2816], P('wide', 'narrow'), may hold values from -0.125 to 0.125
- shared_up: bfloat16 [2048, 2816], P('wide', 'narrow'), may hold values from -0.125 to 0.125
- shared_down: bfloat16 [2816, 2048], P('narrow', 'wide'), may hold values from -0.15625 to 0.15625
Outputs:
- mixed: bfloat16 [2048, 2048], P('wide', 'narrow')
Inputs may be any that keep to these rules, and one draw needn't show every extreme that they name: `expert_ids`: each row names 6 different experts. Among the rows of one index of wide no expert is named by more than 54 rows, a bound that some block reaches of them.
All inputs are finite; a program needn't handle non-finite values.
Results may differ from a plain program's by a relative error of at most 0.019.
Values may be sent and summed in bfloat16 or wider, within the bound.
No kernel may reach another device: no remote copies, remote signals or barrier semaphores. Data moves between devices by JAX's collectives and lax.ppermute only.
A program may use at most 64 MiB of HBM per device.

v0:
```python
import functools
import jax
import jax.numpy as jnp
from jax import lax
from jax.experimental import pallas as pl
from jax.experimental.pallas import tpu as pltpu
from jax.sharding import PartitionSpec as P

PLANE = 4
TILE = 256
OUT_TILE = 512


def dot_t(rows, weight):
    return lax.dot_general(rows, weight, (((1,), (1,)), ((), ())), preferred_element_type=jnp.float32)


def layer_kernel(spans, experts, narrow, *refs):
    count = len(spans)
    own, by_x, by_y, far_a, far_b, gates = refs[:6]
    sources = refs[6 : 6 + 3 * count]
    keep_a, send_a, keep_b, send_b = refs[6 + 3 * count : 10 + 3 * count]
    rows, w_gate, w_up, w_down, hidden, sems = refs[10 + 3 * count :]
    held = (w_gate, w_up, w_down)
    copies = [[None] * count for _ in range(3)]
    for kinds in ((0, 1), (2,)):
        for i, (first, size) in enumerate(spans):
            for kind in kinds:
                copy = pltpu.make_async_copy(
                    sources[3 * i + kind], held[kind].at[pl.ds(first, size)], sems.at[3 * i + kind]
                )
                copy.start()
                copies[kind][i] = copy
    step = own.shape[0]
    half = far_a.shape[1]
    rows[0:step, :] = own[...]
    rows[step : 2 * step, :] = by_x[...]
    rows[2 * step : 3 * step, :] = by_y[...]
    rows[3 * step : 4 * step, 0:half] = far_a[...]
    rows[3 * step : 4 * step, half:] = far_b[...]
    ranges = [(e, spans[e * narrow][0], spans[e * narrow + narrow - 1]) for e in range(experts)]
    ranges = [(e, first, last[0] + last[1]) for e, first, last in ranges]
    ranges.append((None, spans[-1][0], spans[-1][0] + spans[-1][1]))
    ready = 0
    for e, first, end in ranges:
        for lower in range(first, end, TILE):
            upper = min(end, lower + TILE)
            while ready < count and spans[ready][0] < upper:
                copies[0][ready].wait()
                copies[1][ready].wait()
                ready += 1
            pre = dot_t(rows[...], w_gate[lower:upper, :])
            value = jax.nn.silu(pre) * dot_t(rows[...], w_up[lower:upper, :])
            if e is not None:
                value = value * gates[:, e : e + 1]
            hidden[:, lower:upper] = value.astype(jnp.bfloat16)
    for copy in copies[2]:
        copy.wait()
    width = rows.shape[1]
    for lower in range(0, width, OUT_TILE):
        upper = min(width, lower + OUT_TILE)
        part = jnp.dot(hidden[...], w_down[:, lower:upper], preferred_element_type=jnp.float32)
        part = part.astype(jnp.bfloat16)
        quarters = [part[k * step : (k + 1) * step] for k in range(PLANE)]
        if lower < half:
            keep_a[0, :, lower:upper] = quarters[0]
            keep_a[1, :, lower:upper] = quarters[2]
            send_a[0, :, lower:upper] = quarters[1]
            send_a[1, :, lower:upper] = quarters[3]
        else:
            keep_b[0, :, lower - half : upper - half] = quarters[0]
            keep_b[1, :, lower - half : upper - half] = quarters[1]
            send_b[0, :, lower - half : upper - half] = quarters[2]
            send_b[1, :, lower - half : upper - half] = quarters[3]


def layer(blocks, gates, pieces, experts, narrow):
    own = blocks[0]
    step, width = own.shape
    half = width // 2
    spans, first = [], 0
    for trio in pieces:
        spans.append((first, trio[0].shape[0]))
        first += trio[0].shape[0]
    total = first
    flat = [w for trio in pieces for w in trio]
    quarter = jax.ShapeDtypeStruct((2, step, half), jnp.bfloat16)
    flops = 6 * PLANE * step * width * total
    return pl.pallas_call(
        functools.partial(layer_kernel, tuple(spans), experts, narrow),
        out_shape=[quarter] * 4,
        in_specs=[pl.BlockSpec(memory_space=pltpu.VMEM)] * 6
        + [pl.BlockSpec(memory_space=pl.ANY)] * len(flat),
        out_specs=[pl.BlockSpec(memory_space=pltpu.VMEM)] * 4,
        scratch_shapes=[
            pltpu.VMEM((PLANE * step, width), jnp.bfloat16),
            pltpu.VMEM((total, width), jnp.bfloat16),
            pltpu.VMEM((total, width), jnp.bfloat16),
            pltpu.VMEM((total, width), jnp.bfloat16),
            pltpu.VMEM((PLANE * step, total), jnp.bfloat16),
            pltpu.SemaphoreType.DMA((3 * len(pieces),)),
        ],
        compiler_params=pltpu.CompilerParams(vmem_limit_bytes=44 * 1024 * 1024),
        cost_estimate=pl.CostEstimate(
            flops=flops, bytes_accessed=6 * total * width, transcendentals=PLANE * step * total
        ),
    )(*blocks, gates, *flat)


def body(
    tokens,
    expert_ids,
    route_gates,
    expert_gate,
    expert_up,
    expert_down,
    shared_gate,
    shared_up,
    shared_down,
):
    wide = lax.axis_size("wide")
    narrow = lax.axis_size("narrow")
    lines = wide // PLANE
    tok_rows = tokens.shape[0]
    own_rows = tok_rows // narrow
    local_experts = expert_gate.shape[0]
    width = expert_gate.shape[2]
    half = width // 2
    experts_all = local_experts * wide
    here = lax.axis_index("wide")
    core = lax.axis_index("narrow")

    def flip(value, bits):
        return lax.ppermute(value, "wide", [(w, w ^ bits) for w in range(wide)])

    def shift(value, by):
        return lax.ppermute(
            value, "wide", [(w, (w + PLANE * by) % wide) for w in range(wide)]
        )

    def turn(value, by):
        return lax.ppermute(value, "narrow", [(c, (c + by) % narrow) for c in range(narrow)])

    mine = lax.all_to_all(tokens, "narrow", split_axis=0, concat_axis=1, tiled=True)

    own_ids = lax.dynamic_slice_in_dim(expert_ids, core * own_rows, own_rows, 0)
    own_gates = lax.dynamic_slice_in_dim(route_gates, core * own_rows, own_rows, 0)
    numbers = jnp.arange(experts_all, dtype=jnp.int32)
    chosen = own_ids.T[:, None, :] == numbers[None, :, None]
    table = jnp.sum(jnp.where(chosen, own_gates.T[:, None, :], 0.0), axis=0)
    table = table.reshape(wide, local_experts * own_rows)
    high = table.astype(jnp.bfloat16)
    low = (table - high.astype(jnp.float32)).astype(jnp.bfloat16)
    coded = jnp.concatenate([high, low], axis=1)

    hidden_local = shared_gate.shape[1]
    units = -(-hidden_local // wide)
    pad = units * wide - hidden_local
    stacked = jnp.stack([shared_gate.T, shared_up.T, shared_down])
    if pad:
        stacked = jnp.pad(stacked, ((0, 0), (0, pad), (0, 0)))
    chunk = stacked.shape[2]
    stacked = jnp.transpose(stacked.reshape(3, wide, units, chunk), (1, 0, 2, 3))
    stacked = stacked.reshape(wide, 3 * units, chunk)
    gate_rows = -(-coded.shape[1] // (8 * chunk)) * 8
    coded = jnp.pad(coded, ((0, 0), (0, gate_rows * chunk - coded.shape[1])))
    stacked = jnp.concatenate([stacked, coded.reshape(wide, gate_rows, chunk)], axis=1)
    recut = lax.all_to_all(stacked, "wide", split_axis=0, concat_axis=0, tiled=True)
    coded = recut[:, 3 * units :].reshape(wide, gate_rows * chunk).astype(jnp.float32)
    size = local_experts * own_rows
    table = (coded[:, :size] + coded[:, size : 2 * size]).reshape(wide, local_experts, own_rows)
    recut = jnp.transpose(recut[:, : 3 * units].reshape(wide, 3, units, chunk), (1, 2, 0, 3))
    recut = recut.reshape(3, units, width)
    shared_set = jnp.concatenate(
        [recut] + [turn(recut, s) for s in range(1, narrow)], axis=1
    )

    order = jnp.arange(wide, dtype=jnp.int32)
    line, place = here // PLANE, here % PLANE
    source = ((line - order // PLANE) % lines) * PLANE + (place ^ (order % PLANE))
    picks = source[:, None] == jnp.arange(wide, dtype=jnp.int32)[None, :]
    gates = jnp.sum(jnp.where(picks[:, :, None, None], table[None], 0.0), axis=1)
    gates = jnp.transpose(gates.reshape(lines, PLANE, local_experts, own_rows), (0, 1, 3, 2))
    gates = gates.reshape(lines, PLANE * own_rows, local_experts)

    pieces = []
    for e in range(local_experts):
        for s in range(narrow):
            trio = (expert_gate[e], expert_up[e], expert_down[e])
            if s:
                trio = tuple(turn(w, s) for w in trio)
            pieces.append(trio)
    pieces.append((shared_set[0], shared_set[1], shared_set[2]))

    lined = [mine] + [shift(mine, d) for d in range(1, lines)]
    results = []
    for d in range(lines):
        block = lined[d]
        by_x = flip(block, 1)
        by_y = flip(block, 2)
        far_a = flip(by_x[:, :half], 2)
        far_b = flip(by_y[:, half:], 1)
        keep_a, send_a, keep_b, send_b = layer(
            (block, by_x, by_y, far_a, far_b), gates[d], pieces, local_experts, narrow
        )
        sum_a = keep_a.astype(jnp.float32) + flip(send_a, 1).astype(jnp.float32)
        sum_b = keep_b.astype(jnp.float32) + flip(send_b, 2).astype(jnp.float32)
        far_a = flip(sum_a[1].astype(jnp.bfloat16), 2)
        far_b = flip(sum_b[1].astype(jnp.bfloat16), 1)
        sum_a = sum_a[0] + far_a.astype(jnp.float32)
        sum_b = sum_b[0] + far_b.astype(jnp.float32)
        results.append(jnp.concatenate([sum_a, sum_b], axis=1))
    out = results[0]
    for d in range(1, lines):
        out = out + shift(results[d].astype(jnp.bfloat16), -d).astype(jnp.float32)
    return lax.all_to_all(
        out.astype(jnp.bfloat16), "narrow", split_axis=1, concat_axis=0, tiled=True
    )


def solution(mesh):
    return jax.shard_map(
        body,
        mesh=mesh,
        in_specs=(
            P("wide", "narrow"),
            P("wide", None),
            P("wide", None),
            P("wide", "narrow", None),
            P("wide", "narrow", None),
            P("wide", "narrow", None),
            P("wide", "narrow"),
            P("wide", "narrow"),
            P("narrow", "wide"),
        ),
        out_specs=P("wide", "narrow"),
        check_vma=False,
    )
```

profile of v0, /device:TPU:0, one launch (start us, length us, event | category | flops | bytes accessed | tf_op | source)
XLA Modules:
  0.0 204.6 jit_solution(15237527610424895132)
XLA Ops:
  0.0 3.6 %all-to-all-start = ((bf16[2,64,1024]{2,1,0:T(8,128)(2,1)}), bf16[2,64,1024]{2,1,0:T(8,128)(2,1)S(1)}, u32[]{:S(2)}, u32[]{:S(2)}) async-start(bf16[2,64,1024]{2,1,0:T(8,128)(2,1)} %bitcast.138), calls=%async_computation | async-start | bytes 524288 | tf_op jit(solution)/shard_map/all_to_all | solution.py:144
  7.3 8.5 %all-to-all-start.1 = ((bf16[16,272,128]{2,1,0:T(8,128)(2,1)}), bf16[16,272,128]{2,1,0:T(8,128)(2,1)}, u32[]{:S(2)}, u32[]{:S(2)}) async-start(bf16[16,272,128]{2,1,0:T(8,128)(2,1)} %pad_maximum_fusion), calls=%async_computation.1 | async-start | bytes 2228224 | tf_op jit(solution)/shard_map/all_to_all | solution.py:168
  15.9 1.9 collective-permute-start.12
  17.8 2.4 %collective-permute-start.22 = (bf16[64,2048]{1,0:T(8,128)(2,1)S(1)}, bf16[64,2048]{1,0:T(8,128)(2,1)}, u32[]{:S(2)}, u32[]{:S(2)}) collective-permute-start(bf16[64,2048]{1,0:T(8,128)(2,1)S(1)} %bitcast.118), channel_id=1, source_target_pairs={{0,16},{2,18},{4,20},{6,22},{8,24},{10,26},{12,28},{14,30},{16,0},... | collective-permute-start | bytes 786440 | tf_op jit(solution)/shard_map/ppermute | solution.py:137
  20.2 1.5 collective-permute-start.32
  21.6 1.5 collective-permute-start
  23.1 1.5 collective-permute-start.1
  24.6 20.4 %collective-permute-done.12.refs_0_ = bf16[64,2048]{1,0:T(8,128)(2,1)S(1)} collective-permute-done((bf16[64,2048]{1,0:T(8,128)(2,1)S(1)}, bf16[64,2048]{1,0:T(8,128)(2,1)S(1)}, u32[]{:S(2)}, u32[]{:S(2)}) %collective-permute-start.12) | collective-permute-done | bytes 262176 | tf_op jit(solution)/shard_map/ppermute | solution.py:137
  45.0 16.2 %collective-permute-done.22.refs_0_ = bf16[64,2048]{1,0:T(8,128)(2,1)} collective-permute-done((bf16[64,2048]{1,0:T(8,128)(2,1)S(1)}, bf16[64,2048]{1,0:T(8,128)(2,1)}, u32[]{:S(2)}, u32[]{:S(2)}) %collective-permute-start.22) | collective-permute-done | bytes 262176 | tf_op jit(solution)/shard_map/ppermute | solution.py:137
  61.7 1.5 collective-permute-start.13
  63.9 1.7 collective-permute-start.14
  66.3 3.8 %collective-permute-done.13.refs_1_ = bf16[64,2048]{1,0:T(8,128)(2,1)} collective-permute-done((bf16[64,2048]{1,0:T(8,128)(2,1)S(1)}, bf16[64,2048]{1,0:T(8,128)(2,1)}, u32[]{:S(2)}, u32[]{:S(2)}) %collective-permute-start.13) | collective-permute-done | bytes 262176 | tf_op jit(solution)/shard_map/ppermute | solution.py:134
  70.1 1.5 collective-permute-start.23
  72.0 1.7 collective-permute-start.24
  73.7 4.1 %collective-permute-done.23.refs_1_ = bf16[64,2048]{1,0:T(8,128)(2,1)} collective-permute-done((bf16[64,2048]{1,0:T(8,128)(2,1)}, bf16[64,2048]{1,0:T(8,128)(2,1)}, u32[]{:S(2)}, u32[]{:S(2)}) %collective-permute-start.23) | collective-permute-done | bytes 262176 | tf_op jit(solution)/shard_map/ppermute | solution.py:134
  77.9 1.5 collective-permute-start.33
  79.5 1.7 collective-permute-start.34
  81.2 1.3 slice.162
  83.7 2.7 %reshape.122 = bf16[3,88,2048]{2,1,0:T(8,128)(2,1)} reshape(bf16[3,88,16,128]{3,2,1,0:T(8,128)(2,1)} %bitcast.129) | data formatting | bytes 2162688 | tf_op jit(solution)/shard_map/reshape | solution.py:173
  87.1 1.6 slice.157
  88.7 1.6 slice.170
  90.2 1.6 slice.171
  91.8 1.6 slice.177
  93.4 1.6 slice.178
  94.9 1.6 slice.184
  96.9 1.6 slice.185
  102.0 1.4 constant_dynamic-update-slice_fusion.1
  104.6 1.3 constant_dynamic-update-slice_fusion
  106.8 1.4 collective-permute-start.2
  110.2 1.4 collective-permute-start.25
  113.2 9.4 %shard_map.92 = (bf16[2,64,1024]{2,1,0:T(8,128)(2,1)S(1)}, bf16[2,64,1024]{2,1,0:T(8,128)(2,1)S(1)}, bf16[2,64,1024]{2,1,0:T(8,128)(2,1)S(1)}, bf16[2,64,1024]{2,1,0:T(8,128)(2,1)S(1)}) custom-call(bf16[64,2048]{1,0:T(8,128)(2,1)S(1)} %copy-done.9, bf16[64,2048]{1,0:T(8,128)(2,1)} %collective-permute-done.13.refs_1_, ...), custom_call_target="tpu_custom_call" | custom-call | flops 4982833152 | bytes 19464192 | tf_op jit(solution)/shard_map/pallas_call | solution.py:89
  124.7 9.4 %shard_map.93 = (bf16[2,64,1024]{2,1,0:T(8,128)(2,1)S(1)}, bf16[2,64,1024]{2,1,0:T(8,128)(2,1)S(1)}, bf16[2,64,1024]{2,1,0:T(8,128)(2,1)S(1)}, bf16[2,64,1024]{2,1,0:T(8,128)(2,1)S(1)}) custom-call(bf16[64,2048]{1,0:T(8,128)(2,1)} %collective-permute-done.22.refs_0_, bf16[64,2048]{1,0:T(8,128)(2,1)} %collective-permute-done.23.refs_1_, ...), custom_call_target="tpu_custom_call" | custom-call | flops 4982833152 | bytes 19464192 | tf_op jit(solution)/shard_map/pallas_call | solution.py:89
  134.2 1.7 collective-permute-start.19
  136.8 9.4 %shard_map.94 = (bf16[2,64,1024]{2,1,0:T(8,128)(2,1)S(1)}, bf16[2,64,1024]{2,1,0:T(8,128)(2,1)S(1)}, bf16[2,64,1024]{2,1,0:T(8,128)(2,1)S(1)}, bf16[2,64,1024]{2,1,0:T(8,128)(2,1)S(1)}) custom-call(bf16[64,2048]{1,0:T(8,128)(2,1)} %collective-permute-done.32.refs_0_, bf16[64,2048]{1,0:T(8,128)(2,1)} %collective-permute-done.33.refs_1_, ...), custom_call_target="tpu_custom_call" | custom-call | flops 4982833152 | bytes 19464192 | tf_op jit(solution)/shard_map/pallas_call | solution.py:89
  147.8 8.3 %shard_map.91 = (bf16[2,64,1024]{2,1,0:T(8,128)(2,1)S(1)}, bf16[2,64,1024]{2,1,0:T(8,128)(2,1)S(1)}, bf16[2,64,1024]{2,1,0:T(8,128)(2,1)S(1)}, bf16[2,64,1024]{2,1,0:T(8,128)(2,1)S(1)}) custom-call(bf16[64,2048]{1,0:T(8,128)(2,1)S(1)} %bitcast.122, bf16[64,2048]{1,0:T(8,128)(2,1)S(1)} %collective-permute-done.refs_1_, bf16[64,2048]{1,0:T(8,128)(2,1)S(1)} %copy-done.4, ...), custom_call_target="tpu_custom_call" | custom-call | flops 4982833152 | bytes 19464192 | tf_op jit(solution)/shard_map/pallas_call | solution.py:89
  156.2 1.7 collective-permute-start.39
  159.8 1.5 collective-permute-start.18
  161.4 1.2 collective-permute-start.20
  162.7 2.8 %collective-permute-done.39 = bf16[2,64,1024]{2,1,0:T(8,128)(2,1)S(1)} collective-permute-done((bf16[2,64,1024]{2,1,0:T(8,128)(2,1)S(1)}, bf16[2,64,1024]{2,1,0:T(8,128)(2,1)S(1)}, u32[]{:S(2)}, u32[]{:S(2)}) %collective-permute-start.39) | collective-permute-done | bytes 262176 | tf_op jit(solution)/shard_map/ppermute | solution.py:134
  165.5 1.7 collective-permute-start.28
  168.3 2.8 %collective-permute-done.10 = bf16[2,64,1024]{2,1,0:T(8,128)(2,1)S(1)} collective-permute-done((bf16[2,64,1024]{2,1,0:T(8,128)(2,1)S(1)}, bf16[2,64,1024]{2,1,0:T(8,128)(2,1)S(1)}, u32[]{:S(2)}, u32[]{:S(2)}) %collective-permute-start.10) | collective-permute-done | bytes 262176 | tf_op jit(solution)/shard_map/ppermute | solution.py:134
  171.1 1.7 collective-permute-start.38
  174.9 1.5 collective-permute-start.9
  176.4 1.2 collective-permute-start.11
  177.6 6.6 %collective-permute-start.21 = (bf16[64,2048]{1,0:T(8,128)(2,1)S(1)}, bf16[64,2048]{1,0:T(8,128)(2,1)S(1)}, u32[]{:S(2)}, u32[]{:S(2)}) collective-permute-start(bf16[64,2048]{1,0:T(8,128)(2,1)S(1)} %pad_maximum_fusion.1), channel_id=1, source_target_pairs={{0,24},{2,26},{4,28},{6,30},{8,0},{10,2},{12,4},{14,6},{16,8},{18,... | collective-permute-start | bytes 786440 | tf_op jit(solution)/shard_map/ppermute | solution.py:137
  185.4 5.1 %collective-permute-done.21 = bf16[64,2048]{1,0:T(8,128)(2,1)S(1)} collective-permute-done((bf16[64,2048]{1,0:T(8,128)(2,1)S(1)}, bf16[64,2048]{1,0:T(8,128)(2,1)S(1)}, u32[]{:S(2)}, u32[]{:S(2)}) %collective-permute-start.21) | collective-permute-done | bytes 262176 | tf_op jit(solution)/shard_map/ppermute | solution.py:137
  190.5 9.4 %collective-permute-done.31 = bf16[64,2048]{1,0:T(8,128)(2,1)S(1)} collective-permute-done((bf16[64,2048]{1,0:T(8,128)(2,1)S(1)}, bf16[64,2048]{1,0:T(8,128)(2,1)S(1)}, u32[]{:S(2)}, u32[]{:S(2)}) %collective-permute-start.31) | collective-permute-done | bytes 262176 | tf_op jit(solution)/shard_map/ppermute | solution.py:137
  200.0 3.9 %all_to_all.43 = bf16[64,2,1024]{2,0,1:T(8,128)(2,1)S(1)} all-to-all(bf16[64,2,1024]{2,0,1:T(8,128)(2,1)S(1)} %bitcast.134), channel_id=1, replica_groups=mesh['wide'=16,'narrow'=2] {'narrow'}, dimensions={1} | all-to-all | bytes 524288 | tf_op jit(solution)/shard_map/all_to_all | solution.py:216
  (150 shorter events, 29.2 us)
Async XLA Ops:
  0.0 7.3 %all-to-all-start = ((bf16[2,64,1024]{2,1,0:T(8,128)(2,1)}), bf16[2,64,1024]{2,1,0:T(8,128)(2,1)S(1)}, u32[]{:S(2)}, u32[]{:S(2)}) async-start(bf16[2,64,1024]{2,1,0:T(8,128)(2,1)} %bitcast.138), calls=%async_computation | async-start | bytes 524288 | tf_op jit(solution)/shard_map/all_to_all | solution.py:144
  6.2 38.8 %copy-start.1 = (bf16[1,704,2048]{2,1,0:T(8,128)(2,1)S(1)}, bf16[1,704,2048]{2,1,0:T(8,128)(2,1)}, u32[]{:S(2)}) copy-start(bf16[1,704,2048]{2,1,0:T(8,128)(2,1)} %param.12) | copy-start | bytes 8650756
  7.3 73.9 %all-to-all-start.1 = ((bf16[16,272,128]{2,1,0:T(8,128)(2,1)}), bf16[16,272,128]{2,1,0:T(8,128)(2,1)}, u32[]{:S(2)}, u32[]{:S(2)}) async-start(bf16[16,272,128]{2,1,0:T(8,128)(2,1)} %pad_maximum_fusion), calls=%async_computation.1 | async-start | bytes 2228224 | tf_op jit(solution)/shard_map/all_to_all | solution.py:168
  15.9 29.1 %collective-permute-start.12 = (bf16[64,2048]{1,0:T(8,128)(2,1)S(1)}, bf16[64,2048]{1,0:T(8,128)(2,1)S(1)}, u32[]{:S(2)}, u32[]{:S(2)}) collective-permute-start(bf16[64,2048]{1,0:T(8,128)(2,1)S(1)} %bitcast.117), channel_id=1, source_target_pairs={{0,8},{2,10},{4,12},{6,14},{8,16},{10,18},{12,20},{14,22},{16,24},... | collective-permute-start | bytes 786440 | tf_op jit(solution)/shard_map/ppermute | solution.py:137
  17.8 43.4 %collective-permute-start.22 = (bf16[64,2048]{1,0:T(8,128)(2,1)S(1)}, bf16[64,2048]{1,0:T(8,128)(2,1)}, u32[]{:S(2)}, u32[]{:S(2)}) collective-permute-start(bf16[64,2048]{1,0:T(8,128)(2,1)S(1)} %bitcast.118), channel_id=1, source_target_pairs={{0,16},{2,18},{4,20},{6,22},{8,24},{10,26},{12,28},{14,30},{16,0},... | collective-permute-start | bytes 786440 | tf_op jit(solution)/shard_map/ppermute | solution.py:137
  20.2 41.1 %collective-permute-start.32 = (bf16[64,2048]{1,0:T(8,128)(2,1)S(1)}, bf16[64,2048]{1,0:T(8,128)(2,1)}, u32[]{:S(2)}, u32[]{:S(2)}) collective-permute-start(bf16[64,2048]{1,0:T(8,128)(2,1)S(1)} %bitcast.119), channel_id=1, source_target_pairs={{0,24},{2,26},{4,28},{6,30},{8,0},{10,2},{12,4},{14,6},{16,8},{18,... | collective-permute-start | bytes 786440 | tf_op jit(solution)/shard_map/ppermute | solution.py:137
  21.6 40.1 %collective-permute-start = (bf16[64,2048]{1,0:T(8,128)(2,1)S(1)}, bf16[64,2048]{1,0:T(8,128)(2,1)S(1)}, u32[]{:S(2)}, u32[]{:S(2)}) collective-permute-start(bf16[64,2048]{1,0:T(8,128)(2,1)S(1)} %bitcast.120), channel_id=1, source_target_pairs={{0,2},{2,0},{4,6},{6,4},{8,10},{10,8},{12,14},{14,12},{16,18},{18,... | collective-permute-start | bytes 786440 | tf_op jit(solution)/shard_map/ppermute | solution.py:134
  23.1 40.1 %collective-permute-start.1 = (bf16[64,2048]{1,0:T(8,128)(2,1)S(1)}, bf16[64,2048]{1,0:T(8,128)(2,1)S(1)}, u32[]{:S(2)}, u32[]{:S(2)}) collective-permute-start(bf16[64,2048]{1,0:T(8,128)(2,1)S(1)} %bitcast.121), channel_id=1, source_target_pairs={{0,4},{2,6},{4,0},{6,2},{8,12},{10,14},{12,8},{14,10},{16,20},{18,... | collective-permute-start | bytes 786440 | tf_op jit(solution)/shard_map/ppermute | solution.py:134
  45.0 65.2 %collective-permute-start.4 = (bf16[704,2048]{1,0:T(8,128)(2,1)S(1)}, bf16[704,2048]{1,0:T(8,128)(2,1)}, u32[]{:S(2)}, u32[]{:S(2)}) collective-permute-start(bf16[704,2048]{1,0:T(8,128)(2,1)S(1)} %bitcast.107), channel_id=1, source_target_pairs={{0,1},{1,0},{2,3},{3,2},{4,5},{5,4},{6,7},{7,6},{8,9},{9,8},{10,11... | collective-permute-start | bytes 8650760 | tf_op jit(solution)/shard_map/ppermute | solution.py:142
  61.2 50.4 %collective-permute-start.5 = (bf16[704,2048]{1,0:T(8,128)(2,1)}, bf16[704,2048]{1,0:T(8,128)(2,1)}, u32[]{:S(2)}, u32[]{:S(2)}) collective-permute-start(bf16[704,2048]{1,0:T(8,128)(2,1)} %bitcast.112), channel_id=1, source_target_pairs={{0,1},{1,0},{2,3},{3,2},{4,5},{5,4},{6,7},{7,6},{8,9},{9,8},{10,11... | collective-permute-start | bytes 8650760 | tf_op jit(solution)/shard_map/ppermute | solution.py:142
  61.2 51.5 %collective-permute-start.6 = (bf16[704,2048]{1,0:T(8,128)(2,1)}, bf16[704,2048]{1,0:T(8,128)(2,1)}, u32[]{:S(2)}, u32[]{:S(2)}) collective-permute-start(bf16[704,2048]{1,0:T(8,128)(2,1)} %bitcast.123), channel_id=1, source_target_pairs={{0,1},{1,0},{2,3},{3,2},{4,5},{5,4},{6,7},{7,6},{8,9},{9,8},{10,11... | collective-permute-start | bytes 8650760 | tf_op jit(solution)/shard_map/ppermute | solution.py:142
  61.7 8.4 %collective-permute-start.13 = (bf16[64,2048]{1,0:T(8,128)(2,1)S(1)}, bf16[64,2048]{1,0:T(8,128)(2,1)}, u32[]{:S(2)}, u32[]{:S(2)}) collective-permute-start(bf16[64,2048]{1,0:T(8,128)(2,1)S(1)} %collective-permute-done.12.refs_0_), channel_id=1, source_target_pairs={{0,2},{2,0},{4,6},{6,4},{8,10},{10,8},{12,14},{14,12},{16,18},{18,... | collective-permute-start | bytes 786440 | tf_op jit(solution)/shard_map/ppermute | solution.py:134
  63.9 8.1 %collective-permute-start.14 = (bf16[64,2048]{1,0:T(8,128)(2,1)S(1)}, bf16[64,2048]{1,0:T(8,128)(2,1)}, u32[]{:S(2)}, u32[]{:S(2)}) collective-permute-start(bf16[64,2048]{1,0:T(8,128)(2,1)S(1)} %collective-permute-done.12.refs_0_), channel_id=1, source_target_pairs={{0,4},{2,6},{4,0},{6,2},{8,12},{10,14},{12,8},{14,10},{16,20},{18,... | collective-permute-start | bytes 786440 | tf_op jit(solution)/shard_map/ppermute | solution.py:134
  70.1 7.8 %collective-permute-start.23 = (bf16[64,2048]{1,0:T(8,128)(2,1)}, bf16[64,2048]{1,0:T(8,128)(2,1)}, u32[]{:S(2)}, u32[]{:S(2)}) collective-permute-start(bf16[64,2048]{1,0:T(8,128)(2,1)} %collective-permute-done.22.refs_0_), channel_id=1, source_target_pairs={{0,2},{2,0},{4,6},{6,4},{8,10},{10,8},{12,14},{14,12},{16,18},{18,... | collective-permute-start | bytes 786440 | tf_op jit(solution)/shard_map/ppermute | solution.py:134
  72.0 7.4 %collective-permute-start.24 = (bf16[64,2048]{1,0:T(8,128)(2,1)}, bf16[64,2048]{1,0:T(8,128)(2,1)}, u32[]{:S(2)}, u32[]{:S(2)}) collective-permute-start(bf16[64,2048]{1,0:T(8,128)(2,1)} %collective-permute-done.22.refs_0_), channel_id=1, source_target_pairs={{0,4},{2,6},{4,0},{6,2},{8,12},{10,14},{12,8},{14,10},{16,20},{18,... | collective-permute-start | bytes 786440 | tf_op jit(solution)/shard_map/ppermute | solution.py:134
  77.9 8.5 %collective-permute-start.33 = (bf16[64,2048]{1,0:T(8,128)(2,1)}, bf16[64,2048]{1,0:T(8,128)(2,1)}, u32[]{:S(2)}, u32[]{:S(2)}) collective-permute-start(bf16[64,2048]{1,0:T(8,128)(2,1)} %collective-permute-done.32.refs_0_), channel_id=1, source_target_pairs={{0,2},{2,0},{4,6},{6,4},{8,10},{10,8},{12,14},{14,12},{16,18},{18,... | collective-permute-start | bytes 786440 | tf_op jit(solution)/shard_map/ppermute | solution.py:134
  79.5 17.0 %collective-permute-start.34 = (bf16[64,2048]{1,0:T(8,128)(2,1)}, bf16[64,2048]{1,0:T(8,128)(2,1)}, u32[]{:S(2)}, u32[]{:S(2)}) collective-permute-start(bf16[64,2048]{1,0:T(8,128)(2,1)} %collective-permute-done.32.refs_0_), channel_id=1, source_target_pairs={{0,4},{2,6},{4,0},{6,2},{8,12},{10,14},{12,8},{14,10},{16,20},{18,... | collective-permute-start | bytes 786440 | tf_op jit(solution)/shard_map/ppermute | solution.py:134
  86.4 17.0 %collective-permute-start.7 = (bf16[3,88,2048]{2,1,0:T(8,128)(2,1)}, bf16[3,88,2048]{2,1,0:T(8,128)(2,1)}, u32[]{:S(2)}, u32[]{:S(2)}) collective-permute-start(bf16[3,88,2048]{2,1,0:T(8,128)(2,1)} %reshape.122), channel_id=1, source_target_pairs={{0,1},{1,0},{2,3},{3,2},{4,5},{5,4},{6,7},{7,6},{8,9},{9,8},{10,11... | collective-permute-start | bytes 3244040 | tf_op jit(solution)/shard_map/ppermute | solution.py:142
  96.5 9.8 %collective-permute-start.15 = (bf16[64,1024]{1,0:T(8,128)(2,1)}, bf16[64,1024]{1,0:T(8,128)(2,1)}, u32[]{:S(2)}, u32[]{:S(2)}) collective-permute-start(bf16[64,1024]{1,0:T(8,128)(2,1)} %slice.170), channel_id=1, source_target_pairs={{0,4},{2,6},{4,0},{6,2},{8,12},{10,14},{12,8},{14,10},{16,20},{18,... | collective-permute-start | bytes 393224 | tf_op jit(solution)/shard_map/ppermute | solution.py:134
  103.4 5.7 %collective-permute-start.16 = (bf16[64,1024]{1,0:T(8,128)(2,1)S(1)}, bf16[64,1024]{1,0:T(8,128)(2,1)S(1)}, u32[]{:S(2)}, u32[]{:S(2)}) collective-permute-start(bf16[64,1024]{1,0:T(8,128)(2,1)S(1)} %copy-done.18), channel_id=1, source_target_pairs={{0,2},{2,0},{4,6},{6,4},{8,10},{10,8},{12,14},{14,12},{16,18},{18,... | collective-permute-start | bytes 393224 | tf_op jit(solution)/shard_map/ppermute | solution.py:134
  106.8 39.4 %collective-permute-start.2 = (bf16[64,1024]{1,0:T(8,128)(2,1)S(1)}, bf16[64,1024]{1,0:T(8,128)(2,1)S(1)}, u32[]{:S(2)}, u32[]{:S(2)}) collective-permute-start(bf16[64,1024]{1,0:T(8,128)(2,1)S(1)} %copy-done.13), channel_id=1, source_target_pairs={{0,4},{2,6},{4,0},{6,2},{8,12},{10,14},{12,8},{14,10},{16,20},{18,... | collective-permute-start | bytes 393224 | tf_op jit(solution)/shard_map/ppermute | solution.py:134
  109.1 37.9 %collective-permute-start.3 = (bf16[64,1024]{1,0:T(8,128)(2,1)S(1)}, bf16[64,1024]{1,0:T(8,128)(2,1)S(1)}, u32[]{:S(2)}, u32[]{:S(2)}) collective-permute-start(bf16[64,1024]{1,0:T(8,128)(2,1)S(1)} %copy-done.12), channel_id=1, source_target_pairs={{0,2},{2,0},{4,6},{6,4},{8,10},{10,8},{12,14},{14,12},{16,18},{18,... | collective-permute-start | bytes 393224 | tf_op jit(solution)/shard_map/ppermute | solution.py:134
  110.2 12.4 %collective-permute-start.25 = (bf16[64,1024]{1,0:T(8,128)(2,1)S(1)}, bf16[64,1024]{1,0:T(8,128)(2,1)S(1)}, u32[]{:S(2)}, u32[]{:S(2)}) collective-permute-start(bf16[64,1024]{1,0:T(8,128)(2,1)S(1)} %copy-done.17), channel_id=1, source_target_pairs={{0,4},{2,6},{4,0},{6,2},{8,12},{10,14},{12,8},{14,10},{16,20},{18,... | collective-permute-start | bytes 393224 | tf_op jit(solution)/shard_map/ppermute | solution.py:134
  111.6 12.2 %collective-permute-start.26 = (bf16[64,1024]{1,0:T(8,128)(2,1)S(1)}, bf16[64,1024]{1,0:T(8,128)(2,1)S(1)}, u32[]{:S(2)}, u32[]{:S(2)}) collective-permute-start(bf16[64,1024]{1,0:T(8,128)(2,1)S(1)} %copy-done.16), channel_id=1, source_target_pairs={{0,2},{2,0},{4,6},{6,4},{8,10},{10,8},{12,14},{14,12},{16,18},{18,... | collective-permute-start | bytes 393224 | tf_op jit(solution)/shard_map/ppermute | solution.py:134
  112.8 21.4 %collective-permute-start.35 = (bf16[64,1024]{1,0:T(8,128)(2,1)S(1)}, bf16[64,1024]{1,0:T(8,128)(2,1)S(1)}, u32[]{:S(2)}, u32[]{:S(2)}) collective-permute-start(bf16[64,1024]{1,0:T(8,128)(2,1)S(1)} %copy-done.14), channel_id=1, source_target_pairs={{0,4},{2,6},{4,0},{6,2},{8,12},{10,14},{12,8},{14,10},{16,20},{18,... | collective-permute-start | bytes 393224 | tf_op jit(solution)/shard_map/ppermute | solution.py:134
  113.2 11.6 %copy-start.6 = (f32[256,1]{1,0:T(8,128)S(1)}, f32[256,1]{1,0:T(8,128)}, u32[]{:S(2)}) copy-start(f32[256,1]{1,0:T(8,128)} %squeeze.85.refs_5_) | copy-start | bytes 3076
  122.6 13.3 %collective-permute-start.36 = (bf16[64,1024]{1,0:T(8,128)(2,1)S(1)}, bf16[64,1024]{1,0:T(8,128)(2,1)S(1)}, u32[]{:S(2)}, u32[]{:S(2)}) collective-permute-start(bf16[64,1024]{1,0:T(8,128)(2,1)S(1)} %copy-done.15), channel_id=1, source_target_pairs={{0,2},{2,0},{4,6},{6,4},{8,10},{10,8},{12,14},{14,12},{16,18},{18,... | collective-permute-start | bytes 393224 | tf_op jit(solution)/shard_map/ppermute | solution.py:134
  123.8 13.0 %copy-start.5 = (f32[256,1]{1,0:T(8,128)S(1)}, f32[256,1]{1,0:T(8,128)}, u32[]{:S(2)}) copy-start(f32[256,1]{1,0:T(8,128)} %squeeze.86.refs_5_) | copy-start | bytes 3076
  123.8 32.3 %collective-permute-start.17 = (bf16[2,64,1024]{2,1,0:T(8,128)(2,1)S(1)}, bf16[2,64,1024]{2,1,0:T(8,128)(2,1)S(1)}, u32[]{:S(2)}, u32[]{:S(2)}) collective-permute-start(bf16[2,64,1024]{2,1,0:T(8,128)(2,1)S(1)} %get-tuple-element.26), channel_id=1, source_target_pairs={{0,2},{2,0},{4,6},{6,4},{8,10},{10,8},{12,14},{14,12},{16,18},{18,... | collective-permute-start | bytes 786440 | tf_op jit(solution)/shard_map/ppermute | solution.py:134
  134.2 23.8 %collective-permute-start.19 = (bf16[2,64,1024]{2,1,0:T(8,128)(2,1)S(1)}, bf16[2,64,1024]{2,1,0:T(8,128)(2,1)S(1)}, u32[]{:S(2)}, u32[]{:S(2)}) collective-permute-start(bf16[2,64,1024]{2,1,0:T(8,128)(2,1)S(1)} %get-tuple-element.28), channel_id=1, source_target_pairs={{0,4},{2,6},{4,0},{6,2},{8,12},{10,14},{12,8},{14,10},{16,20},{18,... | collective-permute-start | bytes 786440 | tf_op jit(solution)/shard_map/ppermute | solution.py:134
  135.9 11.9 %copy-start.4 = (bf16[64,2048]{1,0:T(8,128)(2,1)S(1)}, bf16[64,2048]{1,0:T(8,128)(2,1)}, u32[]{:S(2)}) copy-start(bf16[64,2048]{1,0:T(8,128)(2,1)} %copy-done.3) | copy-start | bytes 786436
  135.9 23.1 %collective-permute-start.27 = (bf16[2,64,1024]{2,1,0:T(8,128)(2,1)S(1)}, bf16[2,64,1024]{2,1,0:T(8,128)(2,1)S(1)}, u32[]{:S(2)}, u32[]{:S(2)}) collective-permute-start(bf16[2,64,1024]{2,1,0:T(8,128)(2,1)S(1)} %get-tuple-element.30), channel_id=1, source_target_pairs={{0,2},{2,0},{4,6},{6,4},{8,10},{10,8},{12,14},{14,12},{16,18},{18,... | collective-permute-start | bytes 786440 | tf_op jit(solution)/shard_map/ppermute | solution.py:134
  146.2 13.6 %collective-permute-start.29 = (bf16[2,64,1024]{2,1,0:T(8,128)(2,1)S(1)}, bf16[2,64,1024]{2,1,0:T(8,128)(2,1)S(1)}, u32[]{:S(2)}, u32[]{:S(2)}) collective-permute-start(bf16[2,64,1024]{2,1,0:T(8,128)(2,1)S(1)} %get-tuple-element.32), channel_id=1, source_target_pairs={{0,4},{2,6},{4,0},{6,2},{8,12},{10,14},{12,8},{14,10},{16,20},{18,... | collective-permute-start | bytes 786440 | tf_op jit(solution)/shard_map/ppermute | solution.py:134
  146.9 14.4 %collective-permute-start.37 = (bf16[2,64,1024]{2,1,0:T(8,128)(2,1)S(1)}, bf16[2,64,1024]{2,1,0:T(8,128)(2,1)S(1)}, u32[]{:S(2)}, u32[]{:S(2)}) collective-permute-start(bf16[2,64,1024]{2,1,0:T(8,128)(2,1)S(1)} %get-tuple-element.34), channel_id=1, source_target_pairs={{0,2},{2,0},{4,6},{6,4},{8,10},{10,8},{12,14},{14,12},{16,18},{18,... | collective-permute-start | bytes 786440 | tf_op jit(solution)/shard_map/ppermute | solution.py:134
  156.2 9.3 %collective-permute-start.39 = (bf16[2,64,1024]{2,1,0:T(8,128)(2,1)S(1)}, bf16[2,64,1024]{2,1,0:T(8,128)(2,1)S(1)}, u32[]{:S(2)}, u32[]{:S(2)}) collective-permute-start(bf16[2,64,1024]{2,1,0:T(8,128)(2,1)S(1)} %get-tuple-element.36), channel_id=1, source_target_pairs={{0,4},{2,6},{4,0},{6,2},{8,12},{10,14},{12,8},{14,10},{16,20},{18,... | collective-permute-start | bytes 786440 | tf_op jit(solution)/shard_map/ppermute | solution.py:134
  158.0 9.2 %collective-permute-start.8 = (bf16[2,64,1024]{2,1,0:T(8,128)(2,1)S(1)}, bf16[2,64,1024]{2,1,0:T(8,128)(2,1)S(1)}, u32[]{:S(2)}, u32[]{:S(2)}) collective-permute-start(bf16[2,64,1024]{2,1,0:T(8,128)(2,1)S(1)} %get-tuple-element.22), channel_id=1, source_target_pairs={{0,2},{2,0},{4,6},{6,4},{8,10},{10,8},{12,14},{14,12},{16,18},{18,... | collective-permute-start | bytes 786440 | tf_op jit(solution)/shard_map/ppermute | solution.py:134
  159.0 12.1 %collective-permute-start.10 = (bf16[2,64,1024]{2,1,0:T(8,128)(2,1)S(1)}, bf16[2,64,1024]{2,1,0:T(8,128)(2,1)S(1)}, u32[]{:S(2)}, u32[]{:S(2)}) collective-permute-start(bf16[2,64,1024]{2,1,0:T(8,128)(2,1)S(1)} %get-tuple-element.24), channel_id=1, source_target_pairs={{0,4},{2,6},{4,0},{6,2},{8,12},{10,14},{12,8},{14,10},{16,20},{18,... | collective-permute-start | bytes 786440 | tf_op jit(solution)/shard_map/ppermute | solution.py:134
  159.8 13.9 %collective-permute-start.18 = (bf16[64,1024]{1,0:T(8,128)(2,1)S(1)}, bf16[64,1024]{1,0:T(8,128)(2,1)S(1)}, u32[]{:S(2)}, u32[]{:S(2)}) collective-permute-start(bf16[64,1024]{1,0:T(8,128)(2,1)S(1)} %fusion.19), channel_id=1, source_target_pairs={{0,4},{2,6},{4,0},{6,2},{8,12},{10,14},{12,8},{14,10},{16,20},{18,... | collective-permute-start | bytes 393224 | tf_op jit(solution)/shard_map/ppermute | solution.py:134
  161.4 13.5 %collective-permute-start.20 = (bf16[64,1024]{1,0:T(8,128)(2,1)S(1)}, bf16[64,1024]{1,0:T(8,128)(2,1)S(1)}, u32[]{:S(2)}, u32[]{:S(2)}) collective-permute-start(bf16[64,1024]{1,0:T(8,128)(2,1)S(1)} %fusion.20), channel_id=1, source_target_pairs={{0,2},{2,0},{4,6},{6,4},{8,10},{10,8},{12,14},{14,12},{16,18},{18,... | collective-permute-start | bytes 393224 | tf_op jit(solution)/shard_map/ppermute | solution.py:134
  165.5 10.9 %collective-permute-start.28 = (bf16[64,1024]{1,0:T(8,128)(2,1)S(1)}, bf16[64,1024]{1,0:T(8,128)(2,1)S(1)}, u32[]{:S(2)}, u32[]{:S(2)}) collective-permute-start(bf16[64,1024]{1,0:T(8,128)(2,1)S(1)} %fusion.21), channel_id=1, source_target_pairs={{0,4},{2,6},{4,0},{6,2},{8,12},{10,14},{12,8},{14,10},{16,20},{18,... | collective-permute-start | bytes 393224 | tf_op jit(solution)/shard_map/ppermute | solution.py:134
  167.2 10.4 %collective-permute-start.30 = (bf16[64,1024]{1,0:T(8,128)(2,1)S(1)}, bf16[64,1024]{1,0:T(8,128)(2,1)S(1)}, u32[]{:S(2)}, u32[]{:S(2)}) collective-permute-start(bf16[64,1024]{1,0:T(8,128)(2,1)S(1)} %fusion.22), channel_id=1, source_target_pairs={{0,2},{2,0},{4,6},{6,4},{8,10},{10,8},{12,14},{14,12},{16,18},{18,... | collective-permute-start | bytes 393224 | tf_op jit(solution)/shard_map/ppermute | solution.py:134
  171.1 13.2 %collective-permute-start.38 = (bf16[64,1024]{1,0:T(8,128)(2,1)S(1)}, bf16[64,1024]{1,0:T(8,128)(2,1)S(1)}, u32[]{:S(2)}, u32[]{:S(2)}) collective-permute-start(bf16[64,1024]{1,0:T(8,128)(2,1)S(1)} %fusion.23), channel_id=1, source_target_pairs={{0,4},{2,6},{4,0},{6,2},{8,12},{10,14},{12,8},{14,10},{16,20},{18,... | collective-permute-start | bytes 393224 | tf_op jit(solution)/shard_map/ppermute | solution.py:134
  173.7 11.5 %collective-permute-start.40 = (bf16[64,1024]{1,0:T(8,128)(2,1)S(1)}, bf16[64,1024]{1,0:T(8,128)(2,1)S(1)}, u32[]{:S(2)}, u32[]{:S(2)}) collective-permute-start(bf16[64,1024]{1,0:T(8,128)(2,1)S(1)} %fusion.24), channel_id=1, source_target_pairs={{0,2},{2,0},{4,6},{6,4},{8,10},{10,8},{12,14},{14,12},{16,18},{18,... | collective-permute-start | bytes 393224 | tf_op jit(solution)/shard_map/ppermute | solution.py:134
  174.9 10.5 %collective-permute-start.9 = (bf16[64,1024]{1,0:T(8,128)(2,1)S(1)}, bf16[64,1024]{1,0:T(8,128)(2,1)S(1)}, u32[]{:S(2)}, u32[]{:S(2)}) collective-permute-start(bf16[64,1024]{1,0:T(8,128)(2,1)S(1)} %fusion.17), channel_id=1, source_target_pairs={{0,4},{2,6},{4,0},{6,2},{8,12},{10,14},{12,8},{14,10},{16,20},{18,... | collective-permute-start | bytes 393224 | tf_op jit(solution)/shard_map/ppermute | solution.py:134
  176.4 9.0 %collective-permute-start.11 = (bf16[64,1024]{1,0:T(8,128)(2,1)S(1)}, bf16[64,1024]{1,0:T(8,128)(2,1)S(1)}, u32[]{:S(2)}, u32[]{:S(2)}) collective-permute-start(bf16[64,1024]{1,0:T(8,128)(2,1)S(1)} %fusion.18), channel_id=1, source_target_pairs={{0,2},{2,0},{4,6},{6,4},{8,10},{10,8},{12,14},{14,12},{16,18},{18,... | collective-permute-start | bytes 393224 | tf_op jit(solution)/shard_map/ppermute | solution.py:134
  177.6 12.8 %collective-permute-start.21 = (bf16[64,2048]{1,0:T(8,128)(2,1)S(1)}, bf16[64,2048]{1,0:T(8,128)(2,1)S(1)}, u32[]{:S(2)}, u32[]{:S(2)}) collective-permute-start(bf16[64,2048]{1,0:T(8,128)(2,1)S(1)} %pad_maximum_fusion.1), channel_id=1, source_target_pairs={{0,24},{2,26},{4,28},{6,30},{8,0},{10,2},{12,4},{14,6},{16,8},{18,... | collective-permute-start | bytes 786440 | tf_op jit(solution)/shard_map/ppermute | solution.py:137
  184.3 15.5 %collective-permute-start.31 = (bf16[64,2048]{1,0:T(8,128)(2,1)S(1)}, bf16[64,2048]{1,0:T(8,128)(2,1)S(1)}, u32[]{:S(2)}, u32[]{:S(2)}) collective-permute-start(bf16[64,2048]{1,0:T(8,128)(2,1)S(1)} %pad_maximum_fusion.2), channel_id=1, source_target_pairs={{0,16},{2,18},{4,20},{6,22},{8,24},{10,26},{12,28},{14,30},{16,0},... | collective-permute-start | bytes 786440 | tf_op jit(solution)/shard_map/ppermute | solution.py:137
  185.2 14.6 %collective-permute-start.41 = (bf16[64,2048]{1,0:T(8,128)(2,1)S(1)}, bf16[64,2048]{1,0:T(8,128)(2,1)S(1)}, u32[]{:S(2)}, u32[]{:S(2)}) collective-permute-start(bf16[64,2048]{1,0:T(8,128)(2,1)S(1)} %pad_maximum_fusion.3), channel_id=1, source_target_pairs={{0,8},{2,10},{4,12},{6,14},{8,16},{10,18},{12,20},{14,22},{16,24},... | collective-permute-start | bytes 786440 | tf_op jit(solution)/shard_map/ppermute | solution.py:137
  (15 other events, 70.0 us)
where the time goes:
time: 205 us
  waiting for transfers between devices  66.9 us (33%)
  starting transfers between devices  65.8 us (32%)
  Pallas kernels  36.6 us (18%)
  local copies, waits for them, and re-layouts  27.5 us (13%)
  blocking collectives  3.94 us (2%)
  other arithmetic  3.21 us (2%)
    ppermute x6, waiting for transfers between devices, shift(): lax.ppermute(value, 'wide', [(w, (w + PLANE * by) % wide) for w in range(...  51.1 us
    ppermute x32, starting transfers between devices, flip(): return lax.ppermute(value, 'wide', [(w, w ^ bits) for w in range(wide)])  39.9 us
    pallas_call x4, Pallas kernels, layer(): pl.pallas_call(functools.partial(layer_kernel, tuple(spans), experts, nar...  36.6 us
    ppermute x32, waiting for transfers between devices, flip(): return lax.ppermute(value, 'wide', [(w, w ^ bits) for w in range(wide)])  15.8 us
    ppermute x6, starting transfers between devices, shift(): lax.ppermute(value, 'wide', [(w, (w + PLANE * by) % wide) for w in range(...  13.3 us
    all_to_all x1, starting transfers between devices, body(): lax.all_to_all(stacked, 'wide', split_axis=0, concat_axis=0, tiled=True)  8.51 us
    slice x4, local copies, waits for them, and re-layouts, body(): far_b = flip(by_y[:, half:], 1)  6.24 us
    unnamed x44, local copies, waits for them, and re-layouts  5.57 us
  transfers between devices with their start and end apart: 44, of which 12 were waited for; matrix products, arithmetic and copies ran while one was open for 14% of the time, Pallas kernels for 18%

commit v1 on v0

v1 whole, which is shorter than its diff:
```python
import functools
import jax
import jax.numpy as jnp
from jax import lax
from jax.experimental import pallas as pl
from jax.experimental.pallas import tpu as pltpu
from jax.sharding import PartitionSpec as P

PLANE = 4
OUT_TILE = 512


def dot_t(rows, weight):
    return lax.dot_general(rows, weight, (((1,), (1,)), ((), ())), preferred_element_type=jnp.float32)


def layer_kernel(plan, *refs):
    spans, experts, narrow, plane, ties = plan
    count = len(spans)
    own, by_x, by_y, far, gates, shared = refs[:6]
    sources = refs[6 : 6 + 3 * (count - 1)]
    refs = refs[6 + 3 * (count - 1) + ties :]
    keep, send, rows, w_gate, w_up, w_down, hidden, sems = refs
    held = (w_gate, w_up, w_down)
    copies = [[None] * count for _ in range(3)]
    for kinds in ((0, 1), (2,)):
        for i, (first, size) in enumerate(spans):
            for kind in kinds:
                source = shared.at[kind] if i == count - 1 else sources[3 * i + kind]
                copy = pltpu.make_async_copy(
                    source, held[kind].at[pl.ds(first, size)], sems.at[3 * i + kind]
                )
                copy.start()
                copies[kind][i] = copy
    step, width = own.shape
    for k, block in enumerate((own, by_x, by_y, far)):
        rows[k * step : (k + 1) * step, :] = block[...]
    for i, (first, size) in enumerate(spans):
        copies[0][i].wait()
        pre = dot_t(w_gate[first : first + size, :], rows[...])
        copies[1][i].wait()
        value = jax.nn.silu(pre) * dot_t(w_up[first : first + size, :], rows[...])
        if i < count - 1:
            expert = i // narrow
            value = value * gates[plane, expert : expert + 1, :]
        hidden[first : first + size, :] = value.astype(jnp.bfloat16)
    for copy in copies[2]:
        copy.wait()
    acts = hidden[...].T
    kept = (0, 2) if plane % 2 == 0 else (0, 1)
    sent = (1, 3) if plane % 2 == 0 else (2, 3)
    for lower in range(0, width, OUT_TILE):
        upper = min(width, lower + OUT_TILE)
        part = jnp.dot(acts, w_down[:, lower:upper], preferred_element_type=jnp.float32)
        part = part.astype(jnp.bfloat16)
        for ref, which in ((keep, kept), (send, sent)):
            for j, k in enumerate(which):
                ref[j, :, lower:upper] = part[k * step : (k + 1) * step]


def layer(blocks, gates, pieces, shared, experts, narrow, plane, after):
    step, width = blocks[0].shape
    spans, first = [], 0
    for size in [trio[0].shape[0] for trio in pieces] + [shared.shape[1]]:
        spans.append((first, size))
        first += size
    total = first
    flat = [w for trio in pieces for w in trio]
    pair = jax.ShapeDtypeStruct((2, step, width), jnp.bfloat16)
    held = pltpu.VMEM((total, width), jnp.bfloat16)
    plan = (tuple(spans), experts, narrow, plane, len(after))
    return pl.pallas_call(
        functools.partial(layer_kernel, plan),
        out_shape=[pair] * 2,
        in_specs=[pl.BlockSpec(memory_space=pltpu.VMEM)] * 5
        + [pl.BlockSpec(memory_space=pl.ANY)] * (1 + len(flat) + len(after)),
        out_specs=[pl.BlockSpec(memory_space=pltpu.VMEM)] * 2,
        scratch_shapes=[
            pltpu.VMEM((PLANE * step, width), jnp.bfloat16),
            held,
            held,
            held,
            pltpu.VMEM((total, PLANE * step), jnp.bfloat16),
            pltpu.SemaphoreType.DMA((3 * len(spans),)),
        ],
        compiler_params=pltpu.CompilerParams(vmem_limit_bytes=44 * 1024 * 1024),
        cost_estimate=pl.CostEstimate(
            flops=6 * PLANE * step * width * total,
            bytes_accessed=6 * total * width,
            transcendentals=PLANE * step * total,
        ),
    )(*blocks, gates, shared, *flat, *after)


def lay_out_kernel(units, *refs):
    parts, out = refs[:-1], refs[-1]
    for s, part in enumerate(parts):
        wide, _, chunk = part.shape
        for kind in range(3):
            for w in range(wide):
                out[kind, s * units : (s + 1) * units, w * chunk : (w + 1) * chunk] = part[
                    w, kind * units : (kind + 1) * units, :
                ]


def lay_out(parts, units, width):
    if parts[0].shape[2] % 128:
        shaped = [p.reshape(p.shape[0], 3, units, p.shape[2]) for p in parts]
        shaped = [jnp.transpose(p, (1, 2, 0, 3)).reshape(3, units, width) for p in shaped]
        return jnp.concatenate(shaped, axis=1)
    return pl.pallas_call(
        functools.partial(lay_out_kernel, units),
        out_shape=jax.ShapeDtypeStruct((3, units * len(parts), width), jnp.bfloat16),
        in_specs=[pl.BlockSpec(memory_space=pltpu.VMEM)] * len(parts),
        out_specs=pl.BlockSpec(memory_space=pltpu.VMEM),
        compiler_params=pltpu.CompilerParams(vmem_limit_bytes=16 * 1024 * 1024),
        cost_estimate=pl.CostEstimate(
            flops=0, bytes_accessed=12 * units * len(parts) * width, transcendentals=0
        ),
    )(*parts)


def body(
    tokens,
    expert_ids,
    route_gates,
    expert_gate,
    expert_up,
    expert_down,
    shared_gate,
    shared_up,
    shared_down,
):
    wide = lax.axis_size("wide")
    narrow = lax.axis_size("narrow")
    lines = wide // PLANE
    tok_rows = tokens.shape[0]
    own_rows = tok_rows // narrow
    local_experts = expert_gate.shape[0]
    width = expert_gate.shape[2]
    experts_all = local_experts * wide
    here = lax.axis_index("wide")
    core = lax.axis_index("narrow")

    def flip(value, bits):
        return lax.ppermute(value, "wide", [(w, w ^ bits) for w in range(wide)])

    def shift(value, by):
        return lax.ppermute(
            value, "wide", [(w, (w + PLANE * by) % wide) for w in range(wide)]
        )

    def turn(value, by):
        return lax.ppermute(value, "narrow", [(c, (c + by) % narrow) for c in range(narrow)])

    mine = lax.all_to_all(tokens, "narrow", split_axis=0, concat_axis=1, tiled=True)

    own_ids = lax.dynamic_slice_in_dim(expert_ids, core * own_rows, own_rows, 0)
    own_gates = lax.dynamic_slice_in_dim(route_gates, core * own_rows, own_rows, 0)
    numbers = jnp.arange(experts_all, dtype=jnp.int32)
    chosen = own_ids.T[:, None, :] == numbers[None, :, None]
    table = jnp.sum(jnp.where(chosen, own_gates.T[:, None, :], 0.0), axis=0)
    table = table.reshape(wide, local_experts * own_rows)
    high = table.astype(jnp.bfloat16)
    low = (table - high.astype(jnp.float32)).astype(jnp.bfloat16)
    coded = jnp.concatenate([high, low], axis=1)

    lined = {0: mine}
    for d in sorted(range(1, lines), key=lambda d: min(d, lines - d)):
        lined[d] = shift(mine, d)

    hidden_local = shared_gate.shape[1]
    units = -(-hidden_local // wide)
    chunk = shared_down.shape[1]
    gate_rows = -(-coded.shape[1] // chunk)
    padded = -(-(units + gate_rows) // 16) * 16
    coded = jnp.pad(coded, ((0, 0), (0, (padded - units) * chunk - coded.shape[1])))
    cut = []
    for weight in (shared_gate.T, shared_up.T, shared_down):
        weight = jnp.pad(weight, ((0, units * wide - hidden_local), (0, 0)))
        cut.append(weight.reshape(wide, units, chunk))
    blank = jnp.zeros((wide, padded - units, chunk), jnp.bfloat16)
    stacked = jnp.concatenate(
        [cut[0], coded.reshape(wide, padded - units, chunk), cut[1], blank, cut[2], blank], axis=1
    )
    if lines > 2:
        stacked, lined[1], lined[lines - 1] = lax.optimization_barrier(
            (stacked, lined[1], lined[lines - 1])
        )
    recut = lax.all_to_all(stacked, "wide", split_axis=0, concat_axis=0, tiled=True)
    shared = lay_out([recut] + [turn(recut, s) for s in range(1, narrow)], padded, width)
    coded = recut[:, units : units + gate_rows].reshape(wide, gate_rows * chunk)
    coded = coded.astype(jnp.float32)
    size = local_experts * own_rows
    table = (coded[:, :size] + coded[:, size : 2 * size]).reshape(wide, local_experts, own_rows)

    order = jnp.arange(wide, dtype=jnp.int32)
    line, place = here // PLANE, here % PLANE
    source = ((line - order // PLANE) % lines) * PLANE + (place ^ (order % PLANE))
    picks = source[:, None] == jnp.arange(wide, dtype=jnp.int32)[None, :]
    gates = jnp.sum(jnp.where(picks[:, :, None, None], table[None], 0.0), axis=1)
    gates = jnp.transpose(gates.reshape(lines, PLANE, local_experts, own_rows), (0, 2, 1, 3))
    gates = gates.reshape(lines, local_experts, PLANE * own_rows)

    pieces = []
    for e in range(local_experts):
        for s in range(narrow):
            trio = (expert_gate[e], expert_up[e], expert_down[e])
            if s:
                trio = tuple(turn(w, s) for w in trio)
            pieces.append(trio)

    placed = {}
    for d, block in lined.items():
        by_x = flip(block, 1)
        by_y = flip(block, 2)
        far = flip(by_x, 2) if d % 2 == 0 else flip(by_y, 1)
        placed[d] = (block, by_x, by_y, far)
    out = None
    passed = []
    far_first = sorted(range(lines), key=lambda d: -min(d, lines - d))
    for n, d in enumerate(far_first):
        after = passed[n - 2 : n - 1] if n >= 2 else []
        keep, send = layer(placed[d], gates, pieces, shared, local_experts, narrow, d, after)
        first, second = (1, 2) if d % 2 == 0 else (2, 1)
        got = flip(send, first).astype(jnp.float32)
        onward = (keep[1].astype(jnp.float32) + got[1]).astype(jnp.bfloat16)
        passed.append(onward)
        total = keep[0].astype(jnp.float32) + got[0] + flip(onward, second).astype(jnp.float32)
        if d:
            total = shift(total.astype(jnp.bfloat16), -d).astype(jnp.float32)
        out = total if out is None else out + total
    return lax.all_to_all(
        out.astype(jnp.bfloat16), "narrow", split_axis=1, concat_axis=0, tiled=True
    )


def solution(mesh):
    return jax.shard_map(
        body,
        mesh=mesh,
        in_specs=(
            P("wide", "narrow"),
            P("wide", None),
            P("wide", None),
            P("wide", "narrow", None),
            P("wide", "narrow", None),
            P("wide", "narrow", None),
            P("wide", "narrow"),
            P("wide", "narrow"),
            P("narrow", "wide"),
        ),
        out_specs=P("wide", "narrow"),
        check_vma=False,
    )
```

time: 205 us -> 192 us (0.937)
  starting transfers between devices: 65.8 us -> 39.2 us
  local copies, waits for them, and re-layouts: 27.5 us -> 6.52 us
  waiting for transfers between devices: 66.9 us -> 86.7 us
  Pallas kernels: 36.6 us -> 48.1 us
  blocking collectives: 3.94 us -> 9.06 us
    all_to_all x1, waiting for transfers between devices: 0.01 us -> 25.6 us  [body(): lax.all_to_all(stacked, 'wide', split_axis=0, concat_axis=0, tiled=True)]
    ppermute x6, waiting for transfers between devices: 51.1 us -> 25.6 us  [shift(): lax.ppermute(value, 'wide', [(w, (w + PLANE * by) % wide) for w in range(...]
    ppermute x32 -> x20, waiting for transfers between devices: 15.8 us -> 35.5 us  [flip(): return lax.ppermute(value, 'wide', [(w, w ^ bits) for w in range(wide)])]
    ppermute x32 -> x20, starting transfers between devices: 39.9 us -> 20.9 us  [flip(): return lax.ppermute(value, 'wide', [(w, w ^ bits) for w in range(wide)])]
    slice x10 -> x0, local copies, waits for them, and re-layouts: 12.9 us -> none  [the longest x4 6.24 us: body(): far_b = flip(by_y[:, half:], 1)]
    pallas_call x4 -> x5, Pallas kernels: 36.6 us -> 48.1 us  [the longest x4 45.7 us: layer(): pl.pallas_call(functools.partial(layer_kernel, plan), out_shape=[pair] *...]
    all_to_all x0 -> x1, blocking collectives: none -> 5.11 us  [body(): lax.all_to_all(tokens, 'narrow', split_axis=0, concat_axis=1, tiled=True)]
    reshape x2 -> x0, local copies, waits for them, and re-layouts: 3.86 us -> none  [the longest x1 2.71 us: body(): recut = recut.reshape(3, units, width)]
  transfers between devices with their start and end apart: 44 -> 31, of which waited for: 12 -> 16; matrix products, arithmetic and copies ran while one was open for 14% -> 3% of each run, Pallas kernels for 18% -> 25%
where the time goes in v1:
time: 192 us
  waiting for transfers between devices  86.7 us (45%)
  Pallas kernels  48.1 us (25%)
  starting transfers between devices  39.2 us (20%)
  blocking collectives  9.06 us (5%)
  local copies, waits for them, and re-layouts  6.52 us (3%)
  other arithmetic  2.18 us (1%)
    pallas_call x4, Pallas kernels, layer(): pl.pallas_call(functools.partial(layer_kernel, plan), out_shape=[pair] *...  45.7 us
    ppermute x20, waiting for transfers between devices, flip(): return lax.ppermute(value, 'wide', [(w, w ^ bits) for w in range(wide)])  35.5 us
    ppermute x6, waiting for transfers between devices, shift(): lax.ppermute(value, 'wide', [(w, (w + PLANE * by) % wide) for w in range(...  25.6 us
    all_to_all x1, waiting for transfers between devices, body(): lax.all_to_all(stacked, 'wide', split_axis=0, concat_axis=0, tiled=True)  25.6 us
    ppermute x20, starting transfers between devices, flip(): return lax.ppermute(value, 'wide', [(w, w ^ bits) for w in range(wide)])  20.9 us
    ppermute x6, starting transfers between devices, shift(): lax.ppermute(value, 'wide', [(w, (w + PLANE * by) % wide) for w in range(...  12 us
    all_to_all x1, starting transfers between devices, body(): lax.all_to_all(stacked, 'wide', split_axis=0, concat_axis=0, tiled=True)  5.72 us
    all_to_all x1, blocking collectives, body(): lax.all_to_all(tokens, 'narrow', split_axis=0, concat_axis=1, tiled=True)  5.11 us
  transfers between devices with their start and end apart: 31, of which 16 were waited for; matrix products, arithmetic and copies ran while one was open for 3% of the time, Pallas kernels for 25%

profile of v1, /device:TPU:0, one launch (start us, length us, event | category | flops | bytes accessed | tf_op | source)
XLA Modules:
  0.0 192.1 jit_solution(16506922531670052627)
XLA Ops:
  0.0 5.1 %all_to_all.43 = bf16[2,64,1024]{2,1,0:T(8,128)(2,1)S(1)} all-to-all(bf16[2,64,1024]{2,1,0:T(8,128)(2,1)} %bitcast.91), channel_id=1, replica_groups=mesh['wide'=16,'narrow'=2] {'narrow'}, dimensions={0} | all-to-all | bytes 524288 | tf_op jit(solution)/shard_map/all_to_all | solution.py:156
  5.1 3.1 %collective-permute-start.4 = (bf16[64,2048]{1,0:T(8,128)(2,1)S(1)}, bf16[64,2048]{1,0:T(8,128)(2,1)}, u32[]{:S(2)}, u32[]{:S(2)}) collective-permute-start(bf16[64,2048]{1,0:T(8,128)(2,1)S(1)} %bitcast.71), channel_id=1, source_target_pairs={{0,8},{2,10},{4,12},{6,14},{8,16},{10,18},{12,20},{14,22},{16,24},... | collective-permute-start | bytes 786440 | tf_op jit(solution)/shard_map/ppermute | solution.py:149
  8.2 2.1 %collective-permute-start.5 = (bf16[64,2048]{1,0:T(8,128)(2,1)S(1)}, bf16[64,2048]{1,0:T(8,128)(2,1)S(1)}, u32[]{:S(2)}, u32[]{:S(2)}) collective-permute-start(bf16[64,2048]{1,0:T(8,128)(2,1)S(1)} %bitcast.72), channel_id=1, source_target_pairs={{0,24},{2,26},{4,28},{6,30},{8,0},{10,2},{12,4},{14,6},{16,8},{18,... | collective-permute-start | bytes 786440 | tf_op jit(solution)/shard_map/ppermute | solution.py:149
  10.4 0.8 dynamic-slice_bitcast_fusion.1
  11.9 1.0 copy-done.5
  12.9 2.0 %constant_dynamic-update-slice_fusion = bf16[16,288,128]{2,1,0:T(8,128)(2,1)} fusion(bf16[16,288,128]{2,1,0:T(8,128)(2,1)} %copy-done.5, bf16[16,88,128]{2,1,0:T(8,128)(2,1)} %bitcast.90), kind=kLoop, calls=%fused_computation.40 | loop fusion | bytes 720896
  15.5 2.0 %collective-permute-done.4.refs_0_ = bf16[64,2048]{1,0:T(8,128)(2,1)} collective-permute-done((bf16[64,2048]{1,0:T(8,128)(2,1)S(1)}, bf16[64,2048]{1,0:T(8,128)(2,1)}, u32[]{:S(2)}, u32[]{:S(2)}) %collective-permute-start.4) | collective-permute-done | bytes 262176 | tf_op jit(solution)/shard_map/ppermute | solution.py:149
  17.5 4.4 %collective-permute-done.5.refs_0_ = bf16[64,2048]{1,0:T(8,128)(2,1)S(1)} collective-permute-done((bf16[64,2048]{1,0:T(8,128)(2,1)S(1)}, bf16[64,2048]{1,0:T(8,128)(2,1)S(1)}, u32[]{:S(2)}, u32[]{:S(2)}) %collective-permute-start.5) | collective-permute-done | bytes 262176 | tf_op jit(solution)/shard_map/ppermute | solution.py:149
  21.9 5.7 %all-to-all-start.1 = ((bf16[16,288,128]{2,1,0:T(8,128)(2,1)}), bf16[16,288,128]{2,1,0:T(8,128)(2,1)}, u32[]{:S(2)}, u32[]{:S(2)}) async-start(bf16[16,288,128]{2,1,0:T(8,128)(2,1)} %broadcast_dynamic-update-slice_fusion.1), calls=%async_computation.1 | async-start | bytes 2359296 | tf_op jit(solution)/shard_map/all_to_all | solution.py:190
  28.3 25.6 %all-to-all-done.1.refs_0_ = bf16[16,288,128]{2,1,0:T(8,128)(2,1)} async-done(((bf16[16,288,128]{2,1,0:T(8,128)(2,1)}), bf16[16,288,128]{2,1,0:T(8,128)(2,1)}, u32[]{:S(2)}, u32[]{:S(2)}) %all-to-all-start.1) | async-done | bytes 1179680 | tf_op jit(solution)/shard_map/all_to_all | solution.py:190
  53.9 3.1 %collective-permute-start = (bf16[64,2048]{1,0:T(8,128)(2,1)S(1)}, bf16[64,2048]{1,0:T(8,128)(2,1)}, u32[]{:S(2)}, u32[]{:S(2)}) collective-permute-start(bf16[64,2048]{1,0:T(8,128)(2,1)S(1)} %bitcast.73), channel_id=1, source_target_pairs={{0,16},{2,18},{4,20},{6,22},{8,24},{10,26},{12,28},{14,30},{16,0},... | collective-permute-start | bytes 786440 | tf_op jit(solution)/shard_map/ppermute | solution.py:149
  57.0 12.7 %collective-permute-done.refs_0_ = bf16[64,2048]{1,0:T(8,128)(2,1)} collective-permute-done((bf16[64,2048]{1,0:T(8,128)(2,1)S(1)}, bf16[64,2048]{1,0:T(8,128)(2,1)}, u32[]{:S(2)}, u32[]{:S(2)}) %collective-permute-start) | collective-permute-done | bytes 262176 | tf_op jit(solution)/shard_map/ppermute | solution.py:149
  69.7 1.5 collective-permute-start.1
  71.2 7.0 %collective-permute-done.1.refs_1_ = bf16[64,2048]{1,0:T(8,128)(2,1)} collective-permute-done((bf16[64,2048]{1,0:T(8,128)(2,1)}, bf16[64,2048]{1,0:T(8,128)(2,1)}, u32[]{:S(2)}, u32[]{:S(2)}) %collective-permute-start.1) | collective-permute-done | bytes 262176 | tf_op jit(solution)/shard_map/ppermute | solution.py:146
  78.1 1.5 collective-permute-start.2
  79.7 0.8 slice_convert_fusion
  80.4 5.2 %collective-permute-done.2.refs_2_ = bf16[64,2048]{1,0:T(8,128)(2,1)S(1)} collective-permute-done((bf16[64,2048]{1,0:T(8,128)(2,1)}, bf16[64,2048]{1,0:T(8,128)(2,1)S(1)}, u32[]{:S(2)}, u32[]{:S(2)}) %collective-permute-start.2) | collective-permute-done | bytes 262176 | tf_op jit(solution)/shard_map/ppermute | solution.py:146
  85.6 0.7 copy-done.3
  86.3 1.2 collective-permute-start.14
  87.6 0.8 collective-permute-start.3
  88.6 2.3 %shard_map.91.refs_5_ = bf16[3,192,2048]{2,1,0:T(8,128)(2,1)S(1)} custom-call(bf16[16,288,128]{2,1,0:T(8,128)(2,1)} %all-to-all-done.1.refs_0_, bf16[16,288,128]{2,1,0:T(8,128)(2,1)} %collective-permute-done.6.refs_1_), custom_call_target="tpu_custom_call" | custom-call | bytes 4718592 | tf_op jit(solution)/shard_map/pallas_call | solution.py:111
  91.0 4.8 %collective-permute-done.14.refs_2_ = bf16[64,2048]{1,0:T(8,128)(2,1)} collective-permute-done((bf16[64,2048]{1,0:T(8,128)(2,1)}, bf16[64,2048]{1,0:T(8,128)(2,1)}, u32[]{:S(2)}, u32[]{:S(2)}) %collective-permute-start.14) | collective-permute-done | bytes 262176 | tf_op jit(solution)/shard_map/ppermute | solution.py:146
  95.8 1.5 collective-permute-start.13
  97.3 1.3 collective-permute-done.3.refs_3_
  98.6 1.5 collective-permute-start.15
  100.1 12.0 %shard_map.92 = (bf16[2,64,2048]{2,1,0:T(8,128)(2,1)S(1)}, bf16[2,64,2048]{2,1,0:T(8,128)(2,1)S(1)}) custom-call(bf16[64,2048]{1,0:T(8,128)(2,1)} %collective-permute-done.refs_0_, bf16[64,2048]{1,0:T(8,128)(2,1)} %collective-permute-done.1.refs_1_, bf16[64,2048]{1,0:T(8,128)(2,1)S(1)} %copy-done.4, bf16[64,2048]{1,0:T(8,128)(2,1)} %collective-permute-done.3.refs_3_, ...), custom_call_target="tpu_custom_call" | custom-call | flops 5033164800 | bytes 19660800 | tf_op jit(solution)/shard_map/pallas_call | solution.py:72
  112.8 1.5 collective-permute-start.25
  114.5 12.1 %shard_map.93 = (bf16[2,64,2048]{2,1,0:T(8,128)(2,1)S(1)}, bf16[2,64,2048]{2,1,0:T(8,128)(2,1)S(1)}) custom-call(bf16[64,2048]{1,0:T(8,128)(2,1)} %collective-permute-done.4.refs_0_, bf16[64,2048]{1,0:T(8,128)(2,1)S(1)} %collective-permute-done.13.refs_1_, bf16[64,2048]{1,0:T(8,128)(2,1)} %collective-permute-done.14.refs_2_, ...), custom_call_target="tpu_custom_call" | custom-call | flops 5033164800 | bytes 19660800 | tf_op jit(solution)/shard_map/pallas_call | solution.py:72
  126.6 1.8 collective-permute-start.16
  128.7 1.2 collective-permute-done.25.refs_1_
  130.3 0.7 collective-permute-start.27
  131.0 1.5 collective-permute-start.21
  132.7 8.9 %collective-permute-done.16 = bf16[2,64,2048]{2,1,0:T(8,128)(2,1)S(1)} collective-permute-done((bf16[2,64,2048]{2,1,0:T(8,128)(2,1)S(1)}, bf16[2,64,2048]{2,1,0:T(8,128)(2,1)S(1)}, u32[]{:S(2)}, u32[]{:S(2)}) %collective-permute-start.16) | collective-permute-done | bytes 524320 | tf_op jit(solution)/shard_map/ppermute | solution.py:146
  141.5 1.7 collective-permute-start.11
  144.1 10.7 %shard_map.94 = (bf16[2,64,2048]{2,1,0:T(8,128)(2,1)S(1)}, bf16[2,64,2048]{2,1,0:T(8,128)(2,1)S(1)}) custom-call(bf16[64,2048]{1,0:T(8,128)(2,1)S(1)} %collective-permute-done.5.refs_0_, bf16[64,2048]{1,0:T(8,128)(2,1)S(1)} %collective-permute-done.19.refs_1_, bf16[64,2048]{1,0:T(8,128)(2,1)S(1)} %collective-permute-done.20.refs_2_, ...), custom_call_target="tpu_custom_call" | custom-call | flops 5033164800 | bytes 19660800 | tf_op jit(solution)/shard_map/pallas_call | solution.py:72
  154.8 1.1 collective-permute-start.22
  155.9 10.9 %shard_map.95 = (bf16[2,64,2048]{2,1,0:T(8,128)(2,1)S(1)}, bf16[2,64,2048]{2,1,0:T(8,128)(2,1)S(1)}) custom-call(bf16[64,2048]{1,0:T(8,128)(2,1)S(1)} %bitcast.76, bf16[64,2048]{1,0:T(8,128)(2,1)S(1)} %collective-permute-done.25.refs_1_, bf16[64,2048]{1,0:T(8,128)(2,1)S(1)} %collective-permute-done.26.refs_2_, ...), custom_call_target="tpu_custom_call" | custom-call | flops 5033164800 | bytes 19660800 | tf_op jit(solution)/shard_map/pallas_call | solution.py:72
  166.8 0.8 collective-permute-start.28
  167.9 3.5 %collective-permute-start.18 = (bf16[64,2048]{1,0:T(8,128)(2,1)S(1)}, bf16[64,2048]{1,0:T(8,128)(2,1)S(1)}, u32[]{:S(2)}, u32[]{:S(2)}) collective-permute-start(bf16[64,2048]{1,0:T(8,128)(2,1)S(1)} %fusion.12), channel_id=1, source_target_pairs={{0,24},{2,26},{4,28},{6,30},{8,0},{10,2},{12,4},{14,6},{16,8},{18,... | collective-permute-start | bytes 786440 | tf_op jit(solution)/shard_map/ppermute | solution.py:149
  171.6 0.6 collective-permute-start.23
  172.2 3.8 %collective-permute-done.28 = bf16[2,64,2048]{2,1,0:T(8,128)(2,1)S(1)} collective-permute-done((bf16[2,64,2048]{2,1,0:T(8,128)(2,1)S(1)}, bf16[2,64,2048]{2,1,0:T(8,128)(2,1)S(1)}, u32[]{:S(2)}, u32[]{:S(2)}) %collective-permute-start.28) | collective-permute-done | bytes 524320 | tf_op jit(solution)/shard_map/ppermute | solution.py:146
  176.2 1.1 collective-permute-start.29
  177.3 1.6 collective-permute-done.23
  179.0 1.7 collective-permute-done.12
  181.0 1.7 collective-permute-done.29
  182.7 4.5 %collective-permute-done.24 = bf16[64,2048]{1,0:T(8,128)(2,1)S(1)} collective-permute-done((bf16[64,2048]{1,0:T(8,128)(2,1)S(1)}, bf16[64,2048]{1,0:T(8,128)(2,1)S(1)}, u32[]{:S(2)}, u32[]{:S(2)}) %collective-permute-start.24) | collective-permute-done | bytes 262176 | tf_op jit(solution)/shard_map/ppermute | solution.py:149
  187.4 3.9 %all_to_all.44 = bf16[64,2,1024]{2,0,1:T(8,128)(2,1)S(1)} all-to-all(bf16[64,2,1024]{2,0,1:T(8,128)(2,1)S(1)} %bitcast.84), channel_id=1, replica_groups=mesh['wide'=16,'narrow'=2] {'narrow'}, dimensions={1} | all-to-all | bytes 524288 | tf_op jit(solution)/shard_map/all_to_all | solution.py:233
  191.4 0.7 copy.33
  (72 shorter events, 6.1 us)
Async XLA Ops:
  0.0 10.3 %copy-start = (f32[128,6]{0,1:T(8,128)S(1)}, f32[128,6]{0,1:T(8,128)}, u32[]{:S(2)}) copy-start(f32[128,6]{0,1:T(8,128)} %param.11) | copy-start | bytes 9220
  0.0 11.3 %copy-start.6 = (bf16[128,1408]{1,0:T(8,128)(2,1)S(1)}, bf16[128,1408]{1,0:T(8,128)(2,1)}, u32[]{:S(2)}) copy-start(bf16[128,1408]{1,0:T(8,128)(2,1)} %param.15) | copy-start | bytes 1081348
  5.1 6.4 %copy-start.7 = (bf16[128,1408]{1,0:T(8,128)(2,1)S(1)}, bf16[128,1408]{1,0:T(8,128)(2,1)}, u32[]{:S(2)}) copy-start(bf16[128,1408]{1,0:T(8,128)(2,1)} %param.16) | copy-start | bytes 1081348
  5.1 12.3 %collective-permute-start.4 = (bf16[64,2048]{1,0:T(8,128)(2,1)S(1)}, bf16[64,2048]{1,0:T(8,128)(2,1)}, u32[]{:S(2)}, u32[]{:S(2)}) collective-permute-start(bf16[64,2048]{1,0:T(8,128)(2,1)S(1)} %bitcast.71), channel_id=1, source_target_pairs={{0,8},{2,10},{4,12},{6,14},{8,16},{10,18},{12,20},{14,22},{16,24},... | collective-permute-start | bytes 786440 | tf_op jit(solution)/shard_map/ppermute | solution.py:149
  8.2 13.7 %collective-permute-start.5 = (bf16[64,2048]{1,0:T(8,128)(2,1)S(1)}, bf16[64,2048]{1,0:T(8,128)(2,1)S(1)}, u32[]{:S(2)}, u32[]{:S(2)}) collective-permute-start(bf16[64,2048]{1,0:T(8,128)(2,1)S(1)} %bitcast.72), channel_id=1, source_target_pairs={{0,24},{2,26},{4,28},{6,30},{8,0},{10,2},{12,4},{14,6},{16,8},{18,... | collective-permute-start | bytes 786440 | tf_op jit(solution)/shard_map/ppermute | solution.py:149
  11.9 1.0 copy-start.5
  12.9 14.7 %copy-start.1 = (bf16[1,704,2048]{2,1,0:T(8,128)(2,1)S(1)}, bf16[1,704,2048]{2,1,0:T(8,128)(2,1)}, u32[]{:S(2)}) copy-start(bf16[1,704,2048]{2,1,0:T(8,128)(2,1)} %param.12) | copy-start | bytes 8650756
  21.9 31.9 %all-to-all-start.1 = ((bf16[16,288,128]{2,1,0:T(8,128)(2,1)}), bf16[16,288,128]{2,1,0:T(8,128)(2,1)}, u32[]{:S(2)}, u32[]{:S(2)}) async-start(bf16[16,288,128]{2,1,0:T(8,128)(2,1)} %broadcast_dynamic-update-slice_fusion.1), calls=%async_computation.1 | async-start | bytes 2359296 | tf_op jit(solution)/shard_map/all_to_all | solution.py:190
  27.7 72.4 %collective-permute-start.7 = (bf16[704,2048]{1,0:T(8,128)(2,1)S(1)}, bf16[704,2048]{1,0:T(8,128)(2,1)}, u32[]{:S(2)}, u32[]{:S(2)}) collective-permute-start(bf16[704,2048]{1,0:T(8,128)(2,1)S(1)} %bitcast.61), channel_id=1, source_target_pairs={{0,1},{1,0},{2,3},{3,2},{4,5},{5,4},{6,7},{7,6},{8,9},{9,8},{10,11... | collective-permute-start | bytes 8650760 | tf_op jit(solution)/shard_map/ppermute | solution.py:154
  27.7 72.4 %collective-permute-start.8 = (bf16[704,2048]{1,0:T(8,128)(2,1)}, bf16[704,2048]{1,0:T(8,128)(2,1)}, u32[]{:S(2)}, u32[]{:S(2)}) collective-permute-start(bf16[704,2048]{1,0:T(8,128)(2,1)} %bitcast.66), channel_id=1, source_target_pairs={{0,1},{1,0},{2,3},{3,2},{4,5},{5,4},{6,7},{7,6},{8,9},{9,8},{10,11... | collective-permute-start | bytes 8650760 | tf_op jit(solution)/shard_map/ppermute | solution.py:154
  28.2 71.9 %collective-permute-start.9 = (bf16[704,2048]{1,0:T(8,128)(2,1)}, bf16[704,2048]{1,0:T(8,128)(2,1)}, u32[]{:S(2)}, u32[]{:S(2)}) collective-permute-start(bf16[704,2048]{1,0:T(8,128)(2,1)} %bitcast.77), channel_id=1, source_target_pairs={{0,1},{1,0},{2,3},{3,2},{4,5},{5,4},{6,7},{7,6},{8,9},{9,8},{10,11... | collective-permute-start | bytes 8650760 | tf_op jit(solution)/shard_map/ppermute | solution.py:154
  53.9 33.7 %collective-permute-start.6 = (bf16[16,288,128]{2,1,0:T(8,128)(2,1)}, bf16[16,288,128]{2,1,0:T(8,128)(2,1)}, u32[]{:S(2)}, u32[]{:S(2)}) collective-permute-start(bf16[16,288,128]{2,1,0:T(8,128)(2,1)} %all-to-all-done.1.refs_0_), channel_id=1, source_target_pairs={{0,1},{1,0},{2,3},{3,2},{4,5},{5,4},{6,7},{7,6},{8,9},{9,8},{10,11... | collective-permute-start | bytes 3538952 | tf_op jit(solution)/shard_map/ppermute | solution.py:154
  53.9 15.8 %collective-permute-start = (bf16[64,2048]{1,0:T(8,128)(2,1)S(1)}, bf16[64,2048]{1,0:T(8,128)(2,1)}, u32[]{:S(2)}, u32[]{:S(2)}) collective-permute-start(bf16[64,2048]{1,0:T(8,128)(2,1)S(1)} %bitcast.73), channel_id=1, source_target_pairs={{0,16},{2,18},{4,20},{6,22},{8,24},{10,26},{12,28},{14,30},{16,0},... | collective-permute-start | bytes 786440 | tf_op jit(solution)/shard_map/ppermute | solution.py:149
  69.7 8.5 %collective-permute-start.1 = (bf16[64,2048]{1,0:T(8,128)(2,1)}, bf16[64,2048]{1,0:T(8,128)(2,1)}, u32[]{:S(2)}, u32[]{:S(2)}) collective-permute-start(bf16[64,2048]{1,0:T(8,128)(2,1)} %collective-permute-done.refs_0_), channel_id=1, source_target_pairs={{0,2},{2,0},{4,6},{6,4},{8,10},{10,8},{12,14},{14,12},{16,18},{18,... | collective-permute-start | bytes 786440 | tf_op jit(solution)/shard_map/ppermute | solution.py:146
  78.1 7.5 %collective-permute-start.2 = (bf16[64,2048]{1,0:T(8,128)(2,1)}, bf16[64,2048]{1,0:T(8,128)(2,1)S(1)}, u32[]{:S(2)}, u32[]{:S(2)}) collective-permute-start(bf16[64,2048]{1,0:T(8,128)(2,1)} %collective-permute-done.refs_0_), channel_id=1, source_target_pairs={{0,4},{2,6},{4,0},{6,2},{8,12},{10,14},{12,8},{14,10},{16,20},{18,... | collective-permute-start | bytes 786440 | tf_op jit(solution)/shard_map/ppermute | solution.py:146
  85.6 0.7 copy-start.3
  86.3 9.5 %collective-permute-start.14 = (bf16[64,2048]{1,0:T(8,128)(2,1)}, bf16[64,2048]{1,0:T(8,128)(2,1)}, u32[]{:S(2)}, u32[]{:S(2)}) collective-permute-start(bf16[64,2048]{1,0:T(8,128)(2,1)} %collective-permute-done.4.refs_0_), channel_id=1, source_target_pairs={{0,4},{2,6},{4,0},{6,2},{8,12},{10,14},{12,8},{14,10},{16,20},{18,... | collective-permute-start | bytes 786440 | tf_op jit(solution)/shard_map/ppermute | solution.py:146
  87.6 11.0 %collective-permute-start.3 = (bf16[64,2048]{1,0:T(8,128)(2,1)}, bf16[64,2048]{1,0:T(8,128)(2,1)}, u32[]{:S(2)}, u32[]{:S(2)}) collective-permute-start(bf16[64,2048]{1,0:T(8,128)(2,1)} %collective-permute-done.1.refs_1_), channel_id=1, source_target_pairs={{0,4},{2,6},{4,0},{6,2},{8,12},{10,14},{12,8},{14,10},{16,20},{18,... | collective-permute-start | bytes 786440 | tf_op jit(solution)/shard_map/ppermute | solution.py:146
  88.6 11.5 %copy-start.2 = (bf16[1,704,2048]{2,1,0:T(8,128)(2,1)S(1)}, bf16[1,704,2048]{2,1,0:T(8,128)(2,1)}, u32[]{:S(2)}) copy-start(bf16[1,704,2048]{2,1,0:T(8,128)(2,1)} %param.13) | copy-start | bytes 8650756
  88.6 11.5 %copy-start.4 = (bf16[64,2048]{1,0:T(8,128)(2,1)S(1)}, bf16[64,2048]{1,0:T(8,128)(2,1)}, u32[]{:S(2)}) copy-start(bf16[64,2048]{1,0:T(8,128)(2,1)} %copy-done.3) | copy-start | bytes 786436
  95.8 18.7 %collective-permute-start.13 = (bf16[64,2048]{1,0:T(8,128)(2,1)}, bf16[64,2048]{1,0:T(8,128)(2,1)S(1)}, u32[]{:S(2)}, u32[]{:S(2)}) collective-permute-start(bf16[64,2048]{1,0:T(8,128)(2,1)} %collective-permute-done.4.refs_0_), channel_id=1, source_target_pairs={{0,2},{2,0},{4,6},{6,4},{8,10},{10,8},{12,14},{14,12},{16,18},{18,... | collective-permute-start | bytes 786440 | tf_op jit(solution)/shard_map/ppermute | solution.py:146
  98.6 15.9 %collective-permute-start.15 = (bf16[64,2048]{1,0:T(8,128)(2,1)}, bf16[64,2048]{1,0:T(8,128)(2,1)S(1)}, u32[]{:S(2)}, u32[]{:S(2)}) collective-permute-start(bf16[64,2048]{1,0:T(8,128)(2,1)} %collective-permute-done.14.refs_2_), channel_id=1, source_target_pairs={{0,2},{2,0},{4,6},{6,4},{8,10},{10,8},{12,14},{14,12},{16,18},{18,... | collective-permute-start | bytes 786440 | tf_op jit(solution)/shard_map/ppermute | solution.py:146
  112.1 18.9 %collective-permute-start.10 = (bf16[2,64,2048]{2,1,0:T(8,128)(2,1)S(1)}, bf16[2,64,2048]{2,1,0:T(8,128)(2,1)S(1)}, u32[]{:S(2)}, u32[]{:S(2)}) collective-permute-start(bf16[2,64,2048]{2,1,0:T(8,128)(2,1)S(1)} %get-tuple-element.18), channel_id=1, source_target_pairs={{0,2},{2,0},{4,6},{6,4},{8,10},{10,8},{12,14},{14,12},{16,18},{18,... | collective-permute-start | bytes 1572872 | tf_op jit(solution)/shard_map/ppermute | solution.py:146
  112.8 17.1 %collective-permute-start.25 = (bf16[64,2048]{1,0:T(8,128)(2,1)S(1)}, bf16[64,2048]{1,0:T(8,128)(2,1)S(1)}, u32[]{:S(2)}, u32[]{:S(2)}) collective-permute-start(bf16[64,2048]{1,0:T(8,128)(2,1)S(1)} %bitcast.74), channel_id=1, source_target_pairs={{0,2},{2,0},{4,6},{6,4},{8,10},{10,8},{12,14},{14,12},{16,18},{18,... | collective-permute-start | bytes 786440 | tf_op jit(solution)/shard_map/ppermute | solution.py:146
  114.2 16.1 %collective-permute-start.20 = (bf16[64,2048]{1,0:T(8,128)(2,1)S(1)}, bf16[64,2048]{1,0:T(8,128)(2,1)S(1)}, u32[]{:S(2)}, u32[]{:S(2)}) collective-permute-start(bf16[64,2048]{1,0:T(8,128)(2,1)S(1)} %collective-permute-done.5.refs_0_), channel_id=1, source_target_pairs={{0,4},{2,6},{4,0},{6,2},{8,12},{10,14},{12,8},{14,10},{16,20},{18,... | collective-permute-start | bytes 786440 | tf_op jit(solution)/shard_map/ppermute | solution.py:146
  126.6 14.9 %collective-permute-start.16 = (bf16[2,64,2048]{2,1,0:T(8,128)(2,1)S(1)}, bf16[2,64,2048]{2,1,0:T(8,128)(2,1)S(1)}, u32[]{:S(2)}, u32[]{:S(2)}) collective-permute-start(bf16[2,64,2048]{2,1,0:T(8,128)(2,1)S(1)} %get-tuple-element.21), channel_id=1, source_target_pairs={{0,4},{2,6},{4,0},{6,2},{8,12},{10,14},{12,8},{14,10},{16,20},{18,... | collective-permute-start | bytes 1572872 | tf_op jit(solution)/shard_map/ppermute | solution.py:146
  128.4 27.5 %collective-permute-start.26 = (bf16[64,2048]{1,0:T(8,128)(2,1)S(1)}, bf16[64,2048]{1,0:T(8,128)(2,1)S(1)}, u32[]{:S(2)}, u32[]{:S(2)}) collective-permute-start(bf16[64,2048]{1,0:T(8,128)(2,1)S(1)} %bitcast.75), channel_id=1, source_target_pairs={{0,4},{2,6},{4,0},{6,2},{8,12},{10,14},{12,8},{14,10},{16,20},{18,... | collective-permute-start | bytes 786440 | tf_op jit(solution)/shard_map/ppermute | solution.py:146
  129.9 13.6 %collective-permute-start.19 = (bf16[64,2048]{1,0:T(8,128)(2,1)S(1)}, bf16[64,2048]{1,0:T(8,128)(2,1)S(1)}, u32[]{:S(2)}, u32[]{:S(2)}) collective-permute-start(bf16[64,2048]{1,0:T(8,128)(2,1)S(1)} %collective-permute-done.5.refs_0_), channel_id=1, source_target_pairs={{0,2},{2,0},{4,6},{6,4},{8,10},{10,8},{12,14},{14,12},{16,18},{18,... | collective-permute-start | bytes 786440 | tf_op jit(solution)/shard_map/ppermute | solution.py:146
  130.3 25.6 %collective-permute-start.27 = (bf16[64,2048]{1,0:T(8,128)(2,1)S(1)}, bf16[64,2048]{1,0:T(8,128)(2,1)S(1)}, u32[]{:S(2)}, u32[]{:S(2)}) collective-permute-start(bf16[64,2048]{1,0:T(8,128)(2,1)S(1)} %collective-permute-done.25.refs_1_), channel_id=1, source_target_pairs={{0,4},{2,6},{4,0},{6,2},{8,12},{10,14},{12,8},{14,10},{16,20},{18,... | collective-permute-start | bytes 786440 | tf_op jit(solution)/shard_map/ppermute | solution.py:146
  131.0 13.1 %collective-permute-start.21 = (bf16[64,2048]{1,0:T(8,128)(2,1)S(1)}, bf16[64,2048]{1,0:T(8,128)(2,1)S(1)}, u32[]{:S(2)}, u32[]{:S(2)}) collective-permute-start(bf16[64,2048]{1,0:T(8,128)(2,1)S(1)} %collective-permute-done.20.refs_2_), channel_id=1, source_target_pairs={{0,2},{2,0},{4,6},{6,4},{8,10},{10,8},{12,14},{14,12},{16,18},{18,... | collective-permute-start | bytes 786440 | tf_op jit(solution)/shard_map/ppermute | solution.py:146
  141.5 26.1 %collective-permute-start.11 = (bf16[64,2048]{1,0:T(8,128)(2,1)S(1)}, bf16[64,2048]{1,0:T(8,128)(2,1)S(1)}, u32[]{:S(2)}, u32[]{:S(2)}) collective-permute-start(bf16[64,2048]{1,0:T(8,128)(2,1)S(1)} %fusion.17.refs_12_), channel_id=1, source_target_pairs={{0,4},{2,6},{4,0},{6,2},{8,12},{10,14},{12,8},{14,10},{16,20},{18,... | collective-permute-start | bytes 786440 | tf_op jit(solution)/shard_map/ppermute | solution.py:146
  143.5 24.3 %collective-permute-start.17 = (bf16[64,2048]{1,0:T(8,128)(2,1)S(1)}, bf16[64,2048]{1,0:T(8,128)(2,1)S(1)}, u32[]{:S(2)}, u32[]{:S(2)}) collective-permute-start(bf16[64,2048]{1,0:T(8,128)(2,1)S(1)} %fusion.18.refs_12_), channel_id=1, source_target_pairs={{0,2},{2,0},{4,6},{6,4},{8,10},{10,8},{12,14},{14,12},{16,18},{18,... | collective-permute-start | bytes 786440 | tf_op jit(solution)/shard_map/ppermute | solution.py:146
  154.8 16.6 %collective-permute-start.22 = (bf16[2,64,2048]{2,1,0:T(8,128)(2,1)S(1)}, bf16[2,64,2048]{2,1,0:T(8,128)(2,1)S(1)}, u32[]{:S(2)}, u32[]{:S(2)}) collective-permute-start(bf16[2,64,2048]{2,1,0:T(8,128)(2,1)S(1)} %get-tuple-element.24), channel_id=1, source_target_pairs={{0,4},{2,6},{4,0},{6,2},{8,12},{10,14},{12,8},{14,10},{16,20},{18,... | collective-permute-start | bytes 1572872 | tf_op jit(solution)/shard_map/ppermute | solution.py:146
  166.8 9.2 %collective-permute-start.28 = (bf16[2,64,2048]{2,1,0:T(8,128)(2,1)S(1)}, bf16[2,64,2048]{2,1,0:T(8,128)(2,1)S(1)}, u32[]{:S(2)}, u32[]{:S(2)}) collective-permute-start(bf16[2,64,2048]{2,1,0:T(8,128)(2,1)S(1)} %get-tuple-element.26), channel_id=1, source_target_pairs={{0,2},{2,0},{4,6},{6,4},{8,10},{10,8},{12,14},{14,12},{16,18},{18,... | collective-permute-start | bytes 1572872 | tf_op jit(solution)/shard_map/ppermute | solution.py:146
  167.7 13.1 %collective-permute-start.12 = (bf16[64,2048]{1,0:T(8,128)(2,1)S(1)}, bf16[64,2048]{1,0:T(8,128)(2,1)S(1)}, u32[]{:S(2)}, u32[]{:S(2)}) collective-permute-start(bf16[64,2048]{1,0:T(8,128)(2,1)S(1)} %fusion.16), channel_id=1, source_target_pairs={{0,16},{2,18},{4,20},{6,22},{8,24},{10,26},{12,28},{14,30},{16,0},... | collective-permute-start | bytes 786440 | tf_op jit(solution)/shard_map/ppermute | solution.py:149
  167.9 13.1 %collective-permute-start.18 = (bf16[64,2048]{1,0:T(8,128)(2,1)S(1)}, bf16[64,2048]{1,0:T(8,128)(2,1)S(1)}, u32[]{:S(2)}, u32[]{:S(2)}) collective-permute-start(bf16[64,2048]{1,0:T(8,128)(2,1)S(1)} %fusion.12), channel_id=1, source_target_pairs={{0,24},{2,26},{4,28},{6,30},{8,0},{10,2},{12,4},{14,6},{16,8},{18,... | collective-permute-start | bytes 786440 | tf_op jit(solution)/shard_map/ppermute | solution.py:149
  171.6 7.3 %collective-permute-start.23 = (bf16[64,2048]{1,0:T(8,128)(2,1)S(1)}, bf16[64,2048]{1,0:T(8,128)(2,1)S(1)}, u32[]{:S(2)}, u32[]{:S(2)}) collective-permute-start(bf16[64,2048]{1,0:T(8,128)(2,1)S(1)} %fusion.19), channel_id=1, source_target_pairs={{0,2},{2,0},{4,6},{6,4},{8,10},{10,8},{12,14},{14,12},{16,18},{18,... | collective-permute-start | bytes 786440 | tf_op jit(solution)/shard_map/ppermute | solution.py:146
  176.2 6.4 %collective-permute-start.29 = (bf16[64,2048]{1,0:T(8,128)(2,1)S(1)}, bf16[64,2048]{1,0:T(8,128)(2,1)S(1)}, u32[]{:S(2)}, u32[]{:S(2)}) collective-permute-start(bf16[64,2048]{1,0:T(8,128)(2,1)S(1)} %fusion.20), channel_id=1, source_target_pairs={{0,4},{2,6},{4,0},{6,2},{8,12},{10,14},{12,8},{14,10},{16,20},{18,... | collective-permute-start | bytes 786440 | tf_op jit(solution)/shard_map/ppermute | solution.py:146
  179.0 8.2 %collective-permute-start.24 = (bf16[64,2048]{1,0:T(8,128)(2,1)S(1)}, bf16[64,2048]{1,0:T(8,128)(2,1)S(1)}, u32[]{:S(2)}, u32[]{:S(2)}) collective-permute-start(bf16[64,2048]{1,0:T(8,128)(2,1)S(1)} %fusion.8), channel_id=1, source_target_pairs={{0,8},{2,10},{4,12},{6,14},{8,16},{10,18},{12,20},{14,22},{16,24},... | collective-permute-start | bytes 786440 | tf_op jit(solution)/shard_map/ppermute | solution.py:149

commit v2 on v1

--- a/solution.py
+++ b/solution.py
@@ -7,6 +7,7 @@
 from jax.sharding import PartitionSpec as P
 
 PLANE = 4
+TILE = 256
 OUT_TILE = 512
 
 
@@ -21,37 +22,61 @@
     sources = refs[6 : 6 + 3 * (count - 1)]
     refs = refs[6 + 3 * (count - 1) + ties :]
     keep, send, rows, w_gate, w_up, w_down, hidden, sems = refs
-    held = (w_gate, w_up, w_down)
-    copies = [[None] * count for _ in range(3)]
-    for kinds in ((0, 1), (2,)):
+    step, width = own.shape
+    blocks = width // OUT_TILE
+
+    def source(i, kind):
+        return shared.at[kind] if i == count - 1 else sources[3 * i + kind]
+
+    def launch(src, dst, index):
+        copy = pltpu.make_async_copy(src, dst, sems.at[index])
+        copy.start()
+        return copy
+
+    copies = []
+    for i, (first, size) in enumerate(spans):
+        for kind, held in ((0, w_gate), (1, w_up)):
+            copies.append(launch(source(i, kind), held.at[pl.ds(first, size)], 2 * i + kind))
+    down_copies = []
+    for n in range(blocks):
+        columns = pl.ds(n * OUT_TILE, OUT_TILE)
         for i, (first, size) in enumerate(spans):
-            for kind in kinds:
-                source = shared.at[kind] if i == count - 1 else sources[3 * i + kind]
-                copy = pltpu.make_async_copy(
-                    source, held[kind].at[pl.ds(first, size)], sems.at[3 * i + kind]
+            down_copies.append(
+                launch(
+                    source(i, 2).at[:, columns],
+                    w_down.at[pl.ds(first, size), columns],
+                    2 * count + n * count + i,
                 )
-                copy.start()
-                copies[kind][i] = copy
-    step, width = own.shape
+            )
     for k, block in enumerate((own, by_x, by_y, far)):
         rows[k * step : (k + 1) * step, :] = block[...]
-    for i, (first, size) in enumerate(spans):
-        copies[0][i].wait()
-        pre = dot_t(w_gate[first : first + size, :], rows[...])
-        copies[1][i].wait()
-        value = jax.nn.silu(pre) * dot_t(w_up[first : first + size, :], rows[...])
-        if i < count - 1:
-            expert = i // narrow
-            value = value * gates[plane, expert : expert + 1, :]
-        hidden[first : first + size, :] = value.astype(jnp.bfloat16)
-    for copy in copies[2]:
-        copy.wait()
-    acts = hidden[...].T
+    columns = []
+    for e in range(experts):
+        line = gates[plane, e : e + 1, :]
+        columns.append(jnp.broadcast_to(line, (128, line.shape[1])).T[:, 0:1])
+    ranges = [(e, spans[e * narrow][0], spans[e * narrow + narrow - 1]) for e in range(experts)]
+    ranges = [(e, first, last[0] + last[1]) for e, first, last in ranges]
+    ranges.append((None, spans[-1][0], spans[-1][0] + spans[-1][1]))
+    ready = 0
+    for e, first, end in ranges:
+        for lower in range(first, end, TILE):
+            upper = min(end, lower + TILE)
+            while ready < count and spans[ready][0] < upper:
+                copies[2 * ready].wait()
+                copies[2 * ready + 1].wait()
+                ready += 1
+            pre = dot_t(rows[...], w_gate[lower:upper, :])
+            value = jax.nn.silu(pre) * dot_t(rows[...], w_up[lower:upper, :])
+            if e is not None:
+                value = value * columns[e]
+            hidden[:, lower:upper] = value.astype(jnp.bfloat16)
     kept = (0, 2) if plane % 2 == 0 else (0, 1)
     sent = (1, 3) if plane % 2 == 0 else (2, 3)
-    for lower in range(0, width, OUT_TILE):
-        upper = min(width, lower + OUT_TILE)
-        part = jnp.dot(acts, w_down[:, lower:upper], preferred_element_type=jnp.float32)
+    for n in range(blocks):
+        lower, upper = n * OUT_TILE, (n + 1) * OUT_TILE
+        for copy in down_copies[n * count : (n + 1) * count]:
+            copy.wait()
+        part = jnp.dot(hidden[...], w_down[:, lower:upper], preferred_element_type=jnp.float32)
         part = part.astype(jnp.bfloat16)
         for ref, which in ((keep, kept), (send, sent)):
             for j, k in enumerate(which):
@@ -80,8 +105,8 @@
             held,
             held,
             held,
-            pltpu.VMEM((total, PLANE * step), jnp.bfloat16),
-            pltpu.SemaphoreType.DMA((3 * len(spans),)),
+            pltpu.VMEM((PLANE * step, total), jnp.bfloat16),
+            pltpu.SemaphoreType.DMA(((2 + width // OUT_TILE) * len(spans),)),
         ],
         compiler_params=pltpu.CompilerParams(vmem_limit_bytes=44 * 1024 * 1024),
         cost_estimate=pl.CostEstimate(
@@ -165,10 +190,6 @@
     low = (table - high.astype(jnp.float32)).astype(jnp.bfloat16)
     coded = jnp.concatenate([high, low], axis=1)
 
-    lined = {0: mine}
-    for d in sorted(range(1, lines), key=lambda d: min(d, lines - d)):
-        lined[d] = shift(mine, d)
-
     hidden_local = shared_gate.shape[1]
     units = -(-hidden_local // wide)
     chunk = shared_down.shape[1]
@@ -183,11 +204,39 @@
     stacked = jnp.concatenate(
         [cut[0], coded.reshape(wide, padded - units, chunk), cut[1], blank, cut[2], blank], axis=1
     )
-    if lines > 2:
-        stacked, lined[1], lined[lines - 1] = lax.optimization_barrier(
-            (stacked, lined[1], lined[lines - 1])
-        )
+
+    pieces = []
+    for e in range(local_experts):
+        for s in range(narrow):
+            trio = (expert_gate[e], expert_up[e], expert_down[e])
+            pieces.append(tuple(turn(w, s) for w in trio) if s else trio)
+
+    near = sorted({1, lines - 1} - {0, lines})
+    rest = [d for d in range(1, lines) if d not in near]
+
+    def diagonal(d):
+        return flip(by_x[d], 2) if d % 2 == 0 else flip(by_y[d], 1)
+
+    lined, by_x, by_y, far = {0: mine}, {}, {}, {}
+    for d in near:
+        lined[d] = shift(mine, d)
+    by_x[0], by_y[0] = flip(mine, 1), flip(mine, 2)
+    lined, by_x, by_y, stacked = lax.optimization_barrier((lined, by_x, by_y, stacked))
+    for d in rest:
+        lined[d] = shift(lined[0], d)
+    for d in near:
+        by_x[d], by_y[d] = flip(lined[d], 1), flip(lined[d], 2)
+    lined, by_x, by_y, stacked = lax.optimization_barrier((lined, by_x, by_y, stacked))
     recut = lax.all_to_all(stacked, "wide", split_axis=0, concat_axis=0, tiled=True)
+    for d in near:
+        far[d] = diagonal(d)
+    for d in rest:
+        by_x[d], by_y[d] = flip(lined[d], 1), flip(lined[d], 2)
+    recut, lined, by_x, by_y, far, pieces = lax.optimization_barrier(
+        (recut, lined, by_x, by_y, far, pieces)
+    )
+    for d in rest + [0]:
+        far[d] = diagonal(d)
     shared = lay_out([recut] + [turn(recut, s) for s in range(1, narrow)], padded, width)
     coded = recut[:, units : units + gate_rows].reshape(wide, gate_rows * chunk)
     coded = coded.astype(jnp.float32)
@@ -202,26 +251,12 @@
     gates = jnp.transpose(gates.reshape(lines, PLANE, local_experts, own_rows), (0, 2, 1, 3))
     gates = gates.reshape(lines, local_experts, PLANE * own_rows)
 
-    pieces = []
-    for e in range(local_experts):
-        for s in range(narrow):
-            trio = (expert_gate[e], expert_up[e], expert_down[e])
-            if s:
-                trio = tuple(turn(w, s) for w in trio)
-            pieces.append(trio)
-
-    placed = {}
-    for d, block in lined.items():
-        by_x = flip(block, 1)
-        by_y = flip(block, 2)
-        far = flip(by_x, 2) if d % 2 == 0 else flip(by_y, 1)
-        placed[d] = (block, by_x, by_y, far)
     out = None
     passed = []
-    far_first = sorted(range(lines), key=lambda d: -min(d, lines - d))
-    for n, d in enumerate(far_first):
+    for n, d in enumerate(near + rest + [0]):
         after = passed[n - 2 : n - 1] if n >= 2 else []
-        keep, send = layer(placed[d], gates, pieces, shared, local_experts, narrow, d, after)
+        blocks = (lined[d], by_x[d], by_y[d], far[d])
+        keep, send = layer(blocks, gates, pieces, shared, local_experts, narrow, d, after)
         first, second = (1, 2) if d % 2 == 0 else (2, 1)
         got = flip(send, first).astype(jnp.float32)
         onward = (keep[1].astype(jnp.float32) + got[1]).astype(jnp.bfloat16)

time: 192 us -> 188 us (0.979)
  waiting for transfers between devices: 86.7 us -> 73.5 us
  local copies, waits for them, and re-layouts: 6.52 us -> 15.6 us
  Pallas kernels: 48.1 us -> 43.6 us
  starting transfers between devices: 39.2 us -> 42.9 us
    all_to_all x1, waiting for transfers between devices: 25.6 us -> 0.01 us  [body(): lax.all_to_all(stacked, 'wide', split_axis=0, concat_axis=0, tiled=True)]
    ppermute x20, waiting for transfers between devices: 35.5 us -> 57.1 us  [flip(): return lax.ppermute(value, 'wide', [(w, w ^ bits) for w in range(wide)])]
    ppermute x6, waiting for transfers between devices: 25.6 us -> 14.4 us  [shift(): lax.ppermute(value, 'wide', [(w, (w + PLANE * by) % wide) for w in range(...]
    unnamed x23 -> x35, local copies, waits for them, and re-layouts: 4.52 us -> 11.2 us
    pallas_call x4, Pallas kernels: 45.7 us -> 41.3 us  [layer(): pl.pallas_call(functools.partial(layer_kernel, plan), out_shape=[pair] *...]
    ppermute x20, starting transfers between devices: 20.9 us -> 24.1 us  [flip(): return lax.ppermute(value, 'wide', [(w, w ^ bits) for w in range(wide)])]
    transpose x2, local copies, waits for them, and re-layouts: 0.45 us -> 2.78 us
    ppermute x4, waiting for transfers between devices: 0.01 us -> 2.02 us  [turn(): lax.ppermute(value, 'narrow', [(c, (c + by) % narrow) for c in range(narr...]
  transfers between devices with their start and end apart: 31 -> 31, of which waited for: 16 -> 16; matrix products, arithmetic and copies ran while one was open for 3% -> 7% of each run, Pallas kernels for 25% -> 17%
where the time goes in v2:
time: 188 us; the launch traced here: 187 us
  waiting for transfers between devices  73.5 us (39%)
  Pallas kernels  43.6 us (23%)
  starting transfers between devices  42.9 us (23%)
  local copies, waits for them, and re-layouts  15.6 us (8%)
  blocking collectives  9.06 us (5%)
  other arithmetic  2.18 us (1%)
    ppermute x20, waiting for transfers between devices, flip(): return lax.ppermute(value, 'wide', [(w, w ^ bits) for w in range(wide)])  57.1 us
    pallas_call x4, Pallas kernels, layer(): pl.pallas_call(functools.partial(layer_kernel, plan), out_shape=[pair] *...  41.3 us
    ppermute x20, starting transfers between devices, flip(): return lax.ppermute(value, 'wide', [(w, w ^ bits) for w in range(wide)])  24.1 us
    ppermute x6, waiting for transfers between devices, shift(): lax.ppermute(value, 'wide', [(w, (w + PLANE * by) % wide) for w in range(...  14.4 us
    ppermute x6, starting transfers between devices, shift(): lax.ppermute(value, 'wide', [(w, (w + PLANE * by) % wide) for w in range(...  13.8 us
    unnamed x35, local copies, waits for them, and re-layouts  11.2 us
    all_to_all x1, blocking collectives, body(): lax.all_to_all(tokens, 'narrow', split_axis=0, concat_axis=1, tiled=True)  5.11 us
    all_to_all x1, starting transfers between devices, body(): lax.all_to_all(stacked, 'wide', split_axis=0, concat_axis=0, tiled=True)  4.38 us
  transfers between devices with their start and end apart: 31, of which 16 were waited for; matrix products, arithmetic and copies ran while one was open for 7% of the time, Pallas kernels for 17%

profile of v2, /device:TPU:0, one launch (start us, length us, event | category | flops | bytes accessed | tf_op | source)
XLA Modules:
  0.0 187.1 jit_solution(10862513129500588891)
XLA Ops:
  0.0 5.1 %all_to_all.43 = bf16[2,64,1024]{2,1,0:T(8,128)(2,1)S(1)} all-to-all(bf16[2,64,1024]{2,1,0:T(8,128)(2,1)} %bitcast.91), channel_id=1, replica_groups=mesh['wide'=16,'narrow'=2] {'narrow'}, dimensions={0} | all-to-all | bytes 524288 | tf_op jit(solution)/shard_map/all_to_all | solution.py:181
  5.1 3.1 %collective-permute-start = (bf16[64,2048]{1,0:T(8,128)(2,1)S(1)}, bf16[64,2048]{1,0:T(8,128)(2,1)}, u32[]{:S(2)}, u32[]{:S(2)}) collective-permute-start(bf16[64,2048]{1,0:T(8,128)(2,1)S(1)} %bitcast.71), channel_id=1, source_target_pairs={{0,8},{2,10},{4,12},{6,14},{8,16},{10,18},{12,20},{14,22},{16,24},... | collective-permute-start | bytes 786440 | tf_op jit(solution)/shard_map/ppermute | solution.py:174
  8.2 2.1 %collective-permute-start.1 = (bf16[64,2048]{1,0:T(8,128)(2,1)S(1)}, bf16[64,2048]{1,0:T(8,128)(2,1)}, u32[]{:S(2)}, u32[]{:S(2)}) collective-permute-start(bf16[64,2048]{1,0:T(8,128)(2,1)S(1)} %bitcast.72), channel_id=1, source_target_pairs={{0,24},{2,26},{4,28},{6,30},{8,0},{10,2},{12,4},{14,6},{16,8},{18,... | collective-permute-start | bytes 786440 | tf_op jit(solution)/shard_map/ppermute | solution.py:174
  10.3 1.6 collective-permute-start.2
  12.0 1.5 collective-permute-start.3
  14.4 0.9 copy.19
  15.3 2.0 %constant_dynamic-update-slice_fusion.3 = bf16[16,288,128]{2,1,0:T(8,128)(2,1)} fusion(bf16[16,88,128]{2,1,0:T(8,128)(2,1)} %bitcast.83), kind=kLoop, calls=%fused_computation.43 | loop fusion | bytes 720896
  17.3 1.9 %copy.20 = bf16[1408,128]{1,0:T(8,128)(2,1)} copy(bf16[1408,128]{0,1:T(8,128)(2,1)} %bitcast.89) | data formatting | bytes 720896 | tf_op jit(solution)/shard_map/transpose | solution.py:200
  19.8 1.8 constant_dynamic-update-slice_fusion.1
  22.2 1.8 constant_dynamic-update-slice_fusion
  25.8 1.5 collective-permute-start.6
  27.3 6.9 %collective-permute-done.5.refs_1_ = bf16[64,2048]{1,0:T(8,128)(2,1)S(1)} collective-permute-done((bf16[64,2048]{1,0:T(8,128)(2,1)}, bf16[64,2048]{1,0:T(8,128)(2,1)S(1)}, u32[]{:S(2)}, u32[]{:S(2)}) %collective-permute-start.5) | collective-permute-done | bytes 262176 | tf_op jit(solution)/shard_map/ppermute | solution.py:171
  35.4 2.5 %collective-permute-done.6.refs_1_ = bf16[64,2048]{1,0:T(8,128)(2,1)S(1)} collective-permute-done((bf16[64,2048]{1,0:T(8,128)(2,1)}, bf16[64,2048]{1,0:T(8,128)(2,1)S(1)}, u32[]{:S(2)}, u32[]{:S(2)}) %collective-permute-start.6) | collective-permute-done | bytes 262176 | tf_op jit(solution)/shard_map/ppermute | solution.py:171
  39.2 4.2 %collective-permute-done.7.refs_2_ = bf16[64,2048]{1,0:T(8,128)(2,1)} collective-permute-done((bf16[64,2048]{1,0:T(8,128)(2,1)}, bf16[64,2048]{1,0:T(8,128)(2,1)}, u32[]{:S(2)}, u32[]{:S(2)}) %collective-permute-start.7) | collective-permute-done | bytes 262176 | tf_op jit(solution)/shard_map/ppermute | solution.py:171
  43.4 1.1 collective-permute-start.4
  44.5 2.7 %collective-permute-done.8.refs_2_ = bf16[64,2048]{1,0:T(8,128)(2,1)} collective-permute-done((bf16[64,2048]{1,0:T(8,128)(2,1)}, bf16[64,2048]{1,0:T(8,128)(2,1)}, u32[]{:S(2)}, u32[]{:S(2)}) %collective-permute-start.8) | collective-permute-done | bytes 262176 | tf_op jit(solution)/shard_map/ppermute | solution.py:171
  47.2 5.8 %collective-permute-done.4.refs_0_ = bf16[64,2048]{1,0:T(8,128)(2,1)} collective-permute-done((bf16[64,2048]{1,0:T(8,128)(2,1)S(1)}, bf16[64,2048]{1,0:T(8,128)(2,1)}, u32[]{:S(2)}, u32[]{:S(2)}) %collective-permute-start.4) | collective-permute-done | bytes 262176 | tf_op jit(solution)/shard_map/ppermute | solution.py:174
  53.0 4.4 %all-to-all-start.1 = ((bf16[16,288,128]{2,1,0:T(8,128)(2,1)}), bf16[16,288,128]{2,1,0:T(8,128)(2,1)}, u32[]{:S(2)}, u32[]{:S(2)}) async-start(bf16[16,288,128]{2,1,0:T(8,128)(2,1)} %broadcast_dynamic-update-slice_fusion.1), calls=%async_computation.1 | async-start | bytes 2359296 | tf_op jit(solution)/shard_map/all_to_all | solution.py:230
  57.4 1.8 collective-permute-start.10
  59.2 1.5 collective-permute-start.11
  60.7 8.8 %collective-permute-done.10.refs_2_ = bf16[64,2048]{1,0:T(8,128)(2,1)S(1)} collective-permute-done((bf16[64,2048]{1,0:T(8,128)(2,1)}, bf16[64,2048]{1,0:T(8,128)(2,1)S(1)}, u32[]{:S(2)}, u32[]{:S(2)}) %collective-permute-start.10) | collective-permute-done | bytes 262176 | tf_op jit(solution)/shard_map/ppermute | solution.py:171
  70.2 3.2 %collective-permute-start.12 = (bf16[64,2048]{1,0:T(8,128)(2,1)}, bf16[64,2048]{1,0:T(8,128)(2,1)S(1)}, u32[]{:S(2)}, u32[]{:S(2)}) collective-permute-start(bf16[64,2048]{1,0:T(8,128)(2,1)} %collective-permute-done.8.refs_2_), channel_id=1, source_target_pairs={{0,2},{2,0},{4,6},{6,4},{8,10},{10,8},{12,14},{14,12},{16,18},{18,... | collective-permute-start | bytes 786440 | tf_op jit(solution)/shard_map/ppermute | solution.py:171
  74.1 8.1 %collective-permute-done.12.refs_3_ = bf16[64,2048]{1,0:T(8,128)(2,1)S(1)} collective-permute-done((bf16[64,2048]{1,0:T(8,128)(2,1)}, bf16[64,2048]{1,0:T(8,128)(2,1)S(1)}, u32[]{:S(2)}, u32[]{:S(2)}) %collective-permute-start.12) | collective-permute-done | bytes 262176 | tf_op jit(solution)/shard_map/ppermute | solution.py:171
  82.9 2.2 %collective-permute-done.9.refs_1_ = bf16[64,2048]{1,0:T(8,128)(2,1)} collective-permute-done((bf16[64,2048]{1,0:T(8,128)(2,1)}, bf16[64,2048]{1,0:T(8,128)(2,1)}, u32[]{:S(2)}, u32[]{:S(2)}) %collective-permute-start.9) | collective-permute-done | bytes 262176 | tf_op jit(solution)/shard_map/ppermute | solution.py:171
  86.4 2.0 %collective-permute-done.16.refs_1_ = bf16[16,288,128]{2,1,0:T(8,128)(2,1)} collective-permute-done((bf16[16,288,128]{2,1,0:T(8,128)(2,1)}, bf16[16,288,128]{2,1,0:T(8,128)(2,1)}, u32[]{:S(2)}, u32[]{:S(2)}) %collective-permute-start.16) | collective-permute-done | bytes 1179680 | tf_op jit(solution)/shard_map/ppermute | solution.py:179
  88.4 2.3 %shard_map.91.refs_5_ = bf16[3,192,2048]{2,1,0:T(8,128)(2,1)S(1)} custom-call(bf16[16,288,128]{2,1,0:T(8,128)(2,1)} %all-to-all-done.1.refs_0_, bf16[16,288,128]{2,1,0:T(8,128)(2,1)} %collective-permute-done.16.refs_1_), custom_call_target="tpu_custom_call" | custom-call | bytes 4718592 | tf_op jit(solution)/shard_map/pallas_call | solution.py:136
  90.9 10.0 %shard_map.92 = (bf16[2,64,2048]{2,1,0:T(8,128)(2,1)S(1)}, bf16[2,64,2048]{2,1,0:T(8,128)(2,1)S(1)}) custom-call(bf16[64,2048]{1,0:T(8,128)(2,1)} %collective-permute-done.refs_0_, bf16[64,2048]{1,0:T(8,128)(2,1)S(1)} %copy-done.6, bf16[64,2048]{1,0:T(8,128)(2,1)} %collective-permute-done.7.refs_2_, bf16[64,2048]{1,0:T(8,128)(2,1)S(1)} %copy-done.12, ...), custom_call_target="tpu_custom_call" | custom-call | flops 5033164800 | bytes 19660800 | tf_op jit(solution)/shard_map/pallas_call | solution.py:97
  100.9 1.2 collective-permute-start.17
  102.1 9.9 %shard_map.93 = (bf16[2,64,2048]{2,1,0:T(8,128)(2,1)S(1)}, bf16[2,64,2048]{2,1,0:T(8,128)(2,1)S(1)}) custom-call(bf16[64,2048]{1,0:T(8,128)(2,1)} %collective-permute-done.1.refs_0_, bf16[64,2048]{1,0:T(8,128)(2,1)S(1)} %copy-done.8, bf16[64,2048]{1,0:T(8,128)(2,1)} %collective-permute-done.8.refs_2_, bf16[64,2048]{1,0:T(8,128)(2,1)S(1)} %copy-done.10, ...), custom_call_target="tpu_custom_call" | custom-call | flops 5033164800 | bytes 19660800 | tf_op jit(solution)/shard_map/pallas_call | solution.py:97
  112.1 1.0 collective-permute-start.20
  113.1 1.1 collective-permute-start.23
  114.2 0.9 collective-permute-start.27
  115.5 1.7 collective-permute-start.18
  117.1 9.9 %collective-permute-done.20 = bf16[2,64,2048]{2,1,0:T(8,128)(2,1)S(1)} collective-permute-done((bf16[2,64,2048]{2,1,0:T(8,128)(2,1)S(1)}, bf16[2,64,2048]{2,1,0:T(8,128)(2,1)S(1)}, u32[]{:S(2)}, u32[]{:S(2)}) %collective-permute-start.20) | collective-permute-done | bytes 524320 | tf_op jit(solution)/shard_map/ppermute | solution.py:171
  127.1 1.2 collective-permute-start.21
  128.3 4.2 %collective-permute-done.23.refs_3_ = bf16[64,2048]{1,0:T(8,128)(2,1)S(1)} collective-permute-done((bf16[64,2048]{1,0:T(8,128)(2,1)}, bf16[64,2048]{1,0:T(8,128)(2,1)S(1)}, u32[]{:S(2)}, u32[]{:S(2)}) %collective-permute-start.23) | collective-permute-done | bytes 262176 | tf_op jit(solution)/shard_map/ppermute | solution.py:171
  132.6 10.8 %shard_map.94 = (bf16[2,64,2048]{2,1,0:T(8,128)(2,1)S(1)}, bf16[2,64,2048]{2,1,0:T(8,128)(2,1)S(1)}) custom-call(bf16[64,2048]{1,0:T(8,128)(2,1)} %collective-permute-done.4.refs_0_, bf16[64,2048]{1,0:T(8,128)(2,1)} %collective-permute-done.9.refs_1_, bf16[64,2048]{1,0:T(8,128)(2,1)S(1)} %copy-done.4, bf16[64,2048]{1,0:T(8,128)(2,1)S(1)} %collective-permute-done.23.refs_3_, ...), custom_call_target="tpu_custom_call" | custom-call | flops 5033164800 | bytes 19660800 | tf_op jit(solution)/shard_map/pallas_call | solution.py:97
  143.4 1.2 collective-permute-start.24
  144.6 10.5 %shard_map.95 = (bf16[2,64,2048]{2,1,0:T(8,128)(2,1)S(1)}, bf16[2,64,2048]{2,1,0:T(8,128)(2,1)S(1)}) custom-call(bf16[64,2048]{1,0:T(8,128)(2,1)S(1)} %bitcast.76, bf16[64,2048]{1,0:T(8,128)(2,1)S(1)} %collective-permute-done.2.refs_1_, bf16[64,2048]{1,0:T(8,128)(2,1)} %collective-permute-done.3.refs_2_, ...), custom_call_target="tpu_custom_call" | custom-call | flops 5033164800 | bytes 19660800 | tf_op jit(solution)/shard_map/pallas_call | solution.py:97
  155.1 0.9 collective-permute-start.28
  156.2 4.8 %collective-permute-start.19 = (bf16[64,2048]{1,0:T(8,128)(2,1)S(1)}, bf16[64,2048]{1,0:T(8,128)(2,1)S(1)}, u32[]{:S(2)}, u32[]{:S(2)}) collective-permute-start(bf16[64,2048]{1,0:T(8,128)(2,1)S(1)} %fusion.16), channel_id=1, source_target_pairs={{0,24},{2,26},{4,28},{6,30},{8,0},{10,2},{12,4},{14,6},{16,8},{18,... | collective-permute-start | bytes 786440 | tf_op jit(solution)/shard_map/ppermute | solution.py:174
  161.3 0.9 collective-permute-start.25
  162.2 5.0 %collective-permute-done.28 = bf16[2,64,2048]{2,1,0:T(8,128)(2,1)S(1)} collective-permute-done((bf16[2,64,2048]{2,1,0:T(8,128)(2,1)S(1)}, bf16[2,64,2048]{2,1,0:T(8,128)(2,1)S(1)}, u32[]{:S(2)}, u32[]{:S(2)}) %collective-permute-start.28) | collective-permute-done | bytes 524320 | tf_op jit(solution)/shard_map/ppermute | solution.py:171
  167.4 1.2 collective-permute-start.29
  168.8 2.7 %collective-permute-start.26 = (bf16[64,2048]{1,0:T(8,128)(2,1)S(1)}, bf16[64,2048]{1,0:T(8,128)(2,1)S(1)}, u32[]{:S(2)}, u32[]{:S(2)}) collective-permute-start(bf16[64,2048]{1,0:T(8,128)(2,1)S(1)} %fusion.8), channel_id=1, source_target_pairs={{0,16},{2,18},{4,20},{6,22},{8,24},{10,26},{12,28},{14,30},{16,0},... | collective-permute-start | bytes 786440 | tf_op jit(solution)/shard_map/ppermute | solution.py:174
  171.6 2.2 %collective-permute-done.29 = bf16[64,2048]{1,0:T(8,128)(2,1)S(1)} collective-permute-done((bf16[64,2048]{1,0:T(8,128)(2,1)S(1)}, bf16[64,2048]{1,0:T(8,128)(2,1)S(1)}, u32[]{:S(2)}, u32[]{:S(2)}) %collective-permute-start.29) | collective-permute-done | bytes 262176 | tf_op jit(solution)/shard_map/ppermute | solution.py:171
  173.8 8.4 %collective-permute-done.26 = bf16[64,2048]{1,0:T(8,128)(2,1)S(1)} collective-permute-done((bf16[64,2048]{1,0:T(8,128)(2,1)S(1)}, bf16[64,2048]{1,0:T(8,128)(2,1)S(1)}, u32[]{:S(2)}, u32[]{:S(2)}) %collective-permute-start.26) | collective-permute-done | bytes 262176 | tf_op jit(solution)/shard_map/ppermute | solution.py:174
  182.5 3.9 %all_to_all.44 = bf16[64,2,1024]{2,0,1:T(8,128)(2,1)S(1)} all-to-all(bf16[64,2,1024]{2,0,1:T(8,128)(2,1)S(1)} %bitcast.84), channel_id=1, replica_groups=mesh['wide'=16,'narrow'=2] {'narrow'}, dimensions={1} | all-to-all | bytes 524288 | tf_op jit(solution)/shard_map/all_to_all | solution.py:268
  (84 shorter events, 12.1 us)
Async XLA Ops:
  0.0 13.5 %copy-start = (f32[128,6]{0,1:T(8,128)S(1)}, f32[128,6]{0,1:T(8,128)}, u32[]{:S(2)}) copy-start(f32[128,6]{0,1:T(8,128)} %param.11) | copy-start | bytes 9220
  0.0 14.4 %copy-start.13 = (bf16[128,1408]{1,0:T(8,128)(2,1)S(1)}, bf16[128,1408]{1,0:T(8,128)(2,1)}, u32[]{:S(2)}) copy-start(bf16[128,1408]{1,0:T(8,128)(2,1)} %param.15) | copy-start | bytes 1081348
  5.1 19.5 %collective-permute-start = (bf16[64,2048]{1,0:T(8,128)(2,1)S(1)}, bf16[64,2048]{1,0:T(8,128)(2,1)}, u32[]{:S(2)}, u32[]{:S(2)}) collective-permute-start(bf16[64,2048]{1,0:T(8,128)(2,1)S(1)} %bitcast.71), channel_id=1, source_target_pairs={{0,8},{2,10},{4,12},{6,14},{8,16},{10,18},{12,20},{14,22},{16,24},... | collective-permute-start | bytes 786440 | tf_op jit(solution)/shard_map/ppermute | solution.py:174
  8.2 16.5 %collective-permute-start.1 = (bf16[64,2048]{1,0:T(8,128)(2,1)S(1)}, bf16[64,2048]{1,0:T(8,128)(2,1)}, u32[]{:S(2)}, u32[]{:S(2)}) collective-permute-start(bf16[64,2048]{1,0:T(8,128)(2,1)S(1)} %bitcast.72), channel_id=1, source_target_pairs={{0,24},{2,26},{4,28},{6,30},{8,0},{10,2},{12,4},{14,6},{16,8},{18,... | collective-permute-start | bytes 786440 | tf_op jit(solution)/shard_map/ppermute | solution.py:174
  10.3 14.4 %collective-permute-start.2 = (bf16[64,2048]{1,0:T(8,128)(2,1)S(1)}, bf16[64,2048]{1,0:T(8,128)(2,1)S(1)}, u32[]{:S(2)}, u32[]{:S(2)}) collective-permute-start(bf16[64,2048]{1,0:T(8,128)(2,1)S(1)} %bitcast.73), channel_id=1, source_target_pairs={{0,2},{2,0},{4,6},{6,4},{8,10},{10,8},{12,14},{14,12},{16,18},{18,... | collective-permute-start | bytes 786440 | tf_op jit(solution)/shard_map/ppermute | solution.py:171
  12.0 12.7 %collective-permute-start.3 = (bf16[64,2048]{1,0:T(8,128)(2,1)S(1)}, bf16[64,2048]{1,0:T(8,128)(2,1)}, u32[]{:S(2)}, u32[]{:S(2)}) collective-permute-start(bf16[64,2048]{1,0:T(8,128)(2,1)S(1)} %bitcast.74), channel_id=1, source_target_pairs={{0,4},{2,6},{4,0},{6,2},{8,12},{10,14},{12,8},{14,10},{16,20},{18,... | collective-permute-start | bytes 786440 | tf_op jit(solution)/shard_map/ppermute | solution.py:171
  15.3 9.9 %copy-start.1 = (bf16[1,704,2048]{2,1,0:T(8,128)(2,1)S(1)}, bf16[1,704,2048]{2,1,0:T(8,128)(2,1)}, u32[]{:S(2)}) copy-start(bf16[1,704,2048]{2,1,0:T(8,128)(2,1)} %param.12) | copy-start | bytes 8650756
  24.7 9.5 %collective-permute-start.5 = (bf16[64,2048]{1,0:T(8,128)(2,1)}, bf16[64,2048]{1,0:T(8,128)(2,1)S(1)}, u32[]{:S(2)}, u32[]{:S(2)}) collective-permute-start(bf16[64,2048]{1,0:T(8,128)(2,1)} %collective-permute-done.refs_0_), channel_id=1, source_target_pairs={{0,2},{2,0},{4,6},{6,4},{8,10},{10,8},{12,14},{14,12},{16,18},{18,... | collective-permute-start | bytes 786440 | tf_op jit(solution)/shard_map/ppermute | solution.py:171
  25.3 59.8 %collective-permute-start.13 = (bf16[704,2048]{1,0:T(8,128)(2,1)S(1)}, bf16[704,2048]{1,0:T(8,128)(2,1)}, u32[]{:S(2)}, u32[]{:S(2)}) collective-permute-start(bf16[704,2048]{1,0:T(8,128)(2,1)S(1)} %bitcast.61), channel_id=1, source_target_pairs={{0,1},{1,0},{2,3},{3,2},{4,5},{5,4},{6,7},{7,6},{8,9},{9,8},{10,11... | collective-permute-start | bytes 8650760 | tf_op jit(solution)/shard_map/ppermute | solution.py:179
  25.3 59.8 %collective-permute-start.14 = (bf16[704,2048]{1,0:T(8,128)(2,1)}, bf16[704,2048]{1,0:T(8,128)(2,1)}, u32[]{:S(2)}, u32[]{:S(2)}) collective-permute-start(bf16[704,2048]{1,0:T(8,128)(2,1)} %bitcast.66), channel_id=1, source_target_pairs={{0,1},{1,0},{2,3},{3,2},{4,5},{5,4},{6,7},{7,6},{8,9},{9,8},{10,11... | collective-permute-start | bytes 8650760 | tf_op jit(solution)/shard_map/ppermute | solution.py:179
  25.8 59.3 %collective-permute-start.15 = (bf16[704,2048]{1,0:T(8,128)(2,1)}, bf16[704,2048]{1,0:T(8,128)(2,1)}, u32[]{:S(2)}, u32[]{:S(2)}) collective-permute-start(bf16[704,2048]{1,0:T(8,128)(2,1)} %bitcast.77), channel_id=1, source_target_pairs={{0,1},{1,0},{2,3},{3,2},{4,5},{5,4},{6,7},{7,6},{8,9},{9,8},{10,11... | collective-permute-start | bytes 8650760 | tf_op jit(solution)/shard_map/ppermute | solution.py:179
  25.8 12.1 %collective-permute-start.6 = (bf16[64,2048]{1,0:T(8,128)(2,1)}, bf16[64,2048]{1,0:T(8,128)(2,1)S(1)}, u32[]{:S(2)}, u32[]{:S(2)}) collective-permute-start(bf16[64,2048]{1,0:T(8,128)(2,1)} %collective-permute-done.1.refs_0_), channel_id=1, source_target_pairs={{0,2},{2,0},{4,6},{6,4},{8,10},{10,8},{12,14},{14,12},{16,18},{18,... | collective-permute-start | bytes 786440 | tf_op jit(solution)/shard_map/ppermute | solution.py:171
  34.2 0.7 copy-start.5
  34.9 8.5 %collective-permute-start.7 = (bf16[64,2048]{1,0:T(8,128)(2,1)}, bf16[64,2048]{1,0:T(8,128)(2,1)}, u32[]{:S(2)}, u32[]{:S(2)}) collective-permute-start(bf16[64,2048]{1,0:T(8,128)(2,1)} %collective-permute-done.refs_0_), channel_id=1, source_target_pairs={{0,4},{2,6},{4,0},{6,2},{8,12},{10,14},{12,8},{14,10},{16,20},{18,... | collective-permute-start | bytes 786440 | tf_op jit(solution)/shard_map/ppermute | solution.py:171
  37.9 0.7 copy-start.7
  38.6 8.6 %collective-permute-start.8 = (bf16[64,2048]{1,0:T(8,128)(2,1)}, bf16[64,2048]{1,0:T(8,128)(2,1)}, u32[]{:S(2)}, u32[]{:S(2)}) collective-permute-start(bf16[64,2048]{1,0:T(8,128)(2,1)} %collective-permute-done.1.refs_0_), channel_id=1, source_target_pairs={{0,4},{2,6},{4,0},{6,2},{8,12},{10,14},{12,8},{14,10},{16,20},{18,... | collective-permute-start | bytes 786440 | tf_op jit(solution)/shard_map/ppermute | solution.py:171
  43.4 9.6 %collective-permute-start.4 = (bf16[64,2048]{1,0:T(8,128)(2,1)S(1)}, bf16[64,2048]{1,0:T(8,128)(2,1)}, u32[]{:S(2)}, u32[]{:S(2)}) collective-permute-start(bf16[64,2048]{1,0:T(8,128)(2,1)S(1)} %bitcast.75), channel_id=1, source_target_pairs={{0,16},{2,18},{4,20},{6,22},{8,24},{10,26},{12,28},{14,30},{16,0},... | collective-permute-start | bytes 786440 | tf_op jit(solution)/shard_map/ppermute | solution.py:174
  53.0 32.1 %all-to-all-start.1 = ((bf16[16,288,128]{2,1,0:T(8,128)(2,1)}), bf16[16,288,128]{2,1,0:T(8,128)(2,1)}, u32[]{:S(2)}, u32[]{:S(2)}) async-start(bf16[16,288,128]{2,1,0:T(8,128)(2,1)} %broadcast_dynamic-update-slice_fusion.1), calls=%async_computation.1 | async-start | bytes 2359296 | tf_op jit(solution)/shard_map/all_to_all | solution.py:230
  57.4 12.0 %collective-permute-start.10 = (bf16[64,2048]{1,0:T(8,128)(2,1)}, bf16[64,2048]{1,0:T(8,128)(2,1)S(1)}, u32[]{:S(2)}, u32[]{:S(2)}) collective-permute-start(bf16[64,2048]{1,0:T(8,128)(2,1)} %collective-permute-done.4.refs_0_), channel_id=1, source_target_pairs={{0,4},{2,6},{4,0},{6,2},{8,12},{10,14},{12,8},{14,10},{16,20},{18,... | collective-permute-start | bytes 786440 | tf_op jit(solution)/shard_map/ppermute | solution.py:171
  59.2 14.2 %collective-permute-start.11 = (bf16[64,2048]{1,0:T(8,128)(2,1)}, bf16[64,2048]{1,0:T(8,128)(2,1)S(1)}, u32[]{:S(2)}, u32[]{:S(2)}) collective-permute-start(bf16[64,2048]{1,0:T(8,128)(2,1)} %collective-permute-done.7.refs_2_), channel_id=1, source_target_pairs={{0,2},{2,0},{4,6},{6,4},{8,10},{10,8},{12,14},{14,12},{16,18},{18,... | collective-permute-start | bytes 786440 | tf_op jit(solution)/shard_map/ppermute | solution.py:171
  69.5 0.7 copy-start.3
  70.2 12.0 %collective-permute-start.12 = (bf16[64,2048]{1,0:T(8,128)(2,1)}, bf16[64,2048]{1,0:T(8,128)(2,1)S(1)}, u32[]{:S(2)}, u32[]{:S(2)}) collective-permute-start(bf16[64,2048]{1,0:T(8,128)(2,1)} %collective-permute-done.8.refs_2_), channel_id=1, source_target_pairs={{0,2},{2,0},{4,6},{6,4},{8,10},{10,8},{12,14},{14,12},{16,18},{18,... | collective-permute-start | bytes 786440 | tf_op jit(solution)/shard_map/ppermute | solution.py:171
  73.4 0.7 copy-start.11
  74.1 11.0 %collective-permute-start.9 = (bf16[64,2048]{1,0:T(8,128)(2,1)}, bf16[64,2048]{1,0:T(8,128)(2,1)}, u32[]{:S(2)}, u32[]{:S(2)}) collective-permute-start(bf16[64,2048]{1,0:T(8,128)(2,1)} %collective-permute-done.4.refs_0_), channel_id=1, source_target_pairs={{0,2},{2,0},{4,6},{6,4},{8,10},{10,8},{12,14},{14,12},{16,18},{18,... | collective-permute-start | bytes 786440 | tf_op jit(solution)/shard_map/ppermute | solution.py:171
  82.2 0.7 copy-start.9
  85.2 3.3 %collective-permute-start.16 = (bf16[16,288,128]{2,1,0:T(8,128)(2,1)}, bf16[16,288,128]{2,1,0:T(8,128)(2,1)}, u32[]{:S(2)}, u32[]{:S(2)}) collective-permute-start(bf16[16,288,128]{2,1,0:T(8,128)(2,1)} %all-to-all-done.1.refs_0_), channel_id=1, source_target_pairs={{0,1},{1,0},{2,3},{3,2},{4,5},{5,4},{6,7},{7,6},{8,9},{9,8},{10,11... | collective-permute-start | bytes 3538952 | tf_op jit(solution)/shard_map/ppermute | solution.py:179
  86.4 4.4 %copy-start.6 = (bf16[64,2048]{1,0:T(8,128)(2,1)S(1)}, bf16[64,2048]{1,0:T(8,128)(2,1)}, u32[]{:S(2)}) copy-start(bf16[64,2048]{1,0:T(8,128)(2,1)} %copy-done.5) | copy-start | bytes 786436
  86.4 4.4 %copy-start.12 = (bf16[64,2048]{1,0:T(8,128)(2,1)S(1)}, bf16[64,2048]{1,0:T(8,128)(2,1)}, u32[]{:S(2)}) copy-start(bf16[64,2048]{1,0:T(8,128)(2,1)} %copy-done.11) | copy-start | bytes 786436
  88.4 2.5 %copy-start.2 = (bf16[1,704,2048]{2,1,0:T(8,128)(2,1)S(1)}, bf16[1,704,2048]{2,1,0:T(8,128)(2,1)}, u32[]{:S(2)}) copy-start(bf16[1,704,2048]{2,1,0:T(8,128)(2,1)} %param.13) | copy-start | bytes 8650756
  90.9 11.2 %copy-start.8 = (bf16[64,2048]{1,0:T(8,128)(2,1)S(1)}, bf16[64,2048]{1,0:T(8,128)(2,1)}, u32[]{:S(2)}) copy-start(bf16[64,2048]{1,0:T(8,128)(2,1)} %copy-done.7) | copy-start | bytes 786436
  90.9 11.2 %copy-start.10 = (bf16[64,2048]{1,0:T(8,128)(2,1)S(1)}, bf16[64,2048]{1,0:T(8,128)(2,1)}, u32[]{:S(2)}) copy-start(bf16[64,2048]{1,0:T(8,128)(2,1)} %copy-done.9) | copy-start | bytes 786436
  100.9 14.3 %collective-permute-start.17 = (bf16[2,64,2048]{2,1,0:T(8,128)(2,1)S(1)}, bf16[2,64,2048]{2,1,0:T(8,128)(2,1)S(1)}, u32[]{:S(2)}, u32[]{:S(2)}) collective-permute-start(bf16[2,64,2048]{2,1,0:T(8,128)(2,1)S(1)} %get-tuple-element.80), channel_id=1, source_target_pairs={{0,4},{2,6},{4,0},{6,2},{8,12},{10,14},{12,8},{14,10},{16,20},{18,... | collective-permute-start | bytes 1572872 | tf_op jit(solution)/shard_map/ppermute | solution.py:171
  112.1 14.9 %collective-permute-start.20 = (bf16[2,64,2048]{2,1,0:T(8,128)(2,1)S(1)}, bf16[2,64,2048]{2,1,0:T(8,128)(2,1)S(1)}, u32[]{:S(2)}, u32[]{:S(2)}) collective-permute-start(bf16[2,64,2048]{2,1,0:T(8,128)(2,1)S(1)} %get-tuple-element.86), channel_id=1, source_target_pairs={{0,4},{2,6},{4,0},{6,2},{8,12},{10,14},{12,8},{14,10},{16,20},{18,... | collective-permute-start | bytes 1572872 | tf_op jit(solution)/shard_map/ppermute | solution.py:171
  113.1 19.5 %collective-permute-start.23 = (bf16[64,2048]{1,0:T(8,128)(2,1)}, bf16[64,2048]{1,0:T(8,128)(2,1)S(1)}, u32[]{:S(2)}, u32[]{:S(2)}) collective-permute-start(bf16[64,2048]{1,0:T(8,128)(2,1)} %collective-permute-done.9.refs_1_), channel_id=1, source_target_pairs={{0,4},{2,6},{4,0},{6,2},{8,12},{10,14},{12,8},{14,10},{16,20},{18,... | collective-permute-start | bytes 786440 | tf_op jit(solution)/shard_map/ppermute | solution.py:171
  114.2 30.4 %collective-permute-start.27 = (bf16[64,2048]{1,0:T(8,128)(2,1)S(1)}, bf16[64,2048]{1,0:T(8,128)(2,1)S(1)}, u32[]{:S(2)}, u32[]{:S(2)}) collective-permute-start(bf16[64,2048]{1,0:T(8,128)(2,1)S(1)} %collective-permute-done.2.refs_1_), channel_id=1, source_target_pairs={{0,4},{2,6},{4,0},{6,2},{8,12},{10,14},{12,8},{14,10},{16,20},{18,... | collective-permute-start | bytes 786440 | tf_op jit(solution)/shard_map/ppermute | solution.py:171
  115.5 17.1 %copy-start.4 = (bf16[64,2048]{1,0:T(8,128)(2,1)S(1)}, bf16[64,2048]{1,0:T(8,128)(2,1)}, u32[]{:S(2)}) copy-start(bf16[64,2048]{1,0:T(8,128)(2,1)} %copy-done.3) | copy-start | bytes 786436
  115.5 40.6 %collective-permute-start.18 = (bf16[64,2048]{1,0:T(8,128)(2,1)S(1)}, bf16[64,2048]{1,0:T(8,128)(2,1)S(1)}, u32[]{:S(2)}, u32[]{:S(2)}) collective-permute-start(bf16[64,2048]{1,0:T(8,128)(2,1)S(1)} %fusion.17.refs_12_), channel_id=1, source_target_pairs={{0,2},{2,0},{4,6},{6,4},{8,10},{10,8},{12,14},{14,12},{16,18},{18,... | collective-permute-start | bytes 786440 | tf_op jit(solution)/shard_map/ppermute | solution.py:171
  127.1 33.9 %collective-permute-start.21 = (bf16[64,2048]{1,0:T(8,128)(2,1)S(1)}, bf16[64,2048]{1,0:T(8,128)(2,1)S(1)}, u32[]{:S(2)}, u32[]{:S(2)}) collective-permute-start(bf16[64,2048]{1,0:T(8,128)(2,1)S(1)} %fusion.18.refs_12_), channel_id=1, source_target_pairs={{0,2},{2,0},{4,6},{6,4},{8,10},{10,8},{12,14},{14,12},{16,18},{18,... | collective-permute-start | bytes 786440 | tf_op jit(solution)/shard_map/ppermute | solution.py:171
  143.4 17.8 %collective-permute-start.24 = (bf16[2,64,2048]{2,1,0:T(8,128)(2,1)S(1)}, bf16[2,64,2048]{2,1,0:T(8,128)(2,1)S(1)}, u32[]{:S(2)}, u32[]{:S(2)}) collective-permute-start(bf16[2,64,2048]{2,1,0:T(8,128)(2,1)S(1)} %get-tuple-element.91), channel_id=1, source_target_pairs={{0,2},{2,0},{4,6},{6,4},{8,10},{10,8},{12,14},{14,12},{16,18},{18,... | collective-permute-start | bytes 1572872 | tf_op jit(solution)/shard_map/ppermute | solution.py:171
  155.1 12.1 %collective-permute-start.28 = (bf16[2,64,2048]{2,1,0:T(8,128)(2,1)S(1)}, bf16[2,64,2048]{2,1,0:T(8,128)(2,1)S(1)}, u32[]{:S(2)}, u32[]{:S(2)}) collective-permute-start(bf16[2,64,2048]{2,1,0:T(8,128)(2,1)S(1)} %get-tuple-element.96), channel_id=1, source_target_pairs={{0,2},{2,0},{4,6},{6,4},{8,10},{10,8},{12,14},{14,12},{16,18},{18,... | collective-permute-start | bytes 1572872 | tf_op jit(solution)/shard_map/ppermute | solution.py:171
  156.2 15.3 %collective-permute-start.19 = (bf16[64,2048]{1,0:T(8,128)(2,1)S(1)}, bf16[64,2048]{1,0:T(8,128)(2,1)S(1)}, u32[]{:S(2)}, u32[]{:S(2)}) collective-permute-start(bf16[64,2048]{1,0:T(8,128)(2,1)S(1)} %fusion.16), channel_id=1, source_target_pairs={{0,24},{2,26},{4,28},{6,30},{8,0},{10,2},{12,4},{14,6},{16,8},{18,... | collective-permute-start | bytes 786440 | tf_op jit(solution)/shard_map/ppermute | solution.py:174
  161.1 10.5 %collective-permute-start.22 = (bf16[64,2048]{1,0:T(8,128)(2,1)S(1)}, bf16[64,2048]{1,0:T(8,128)(2,1)S(1)}, u32[]{:S(2)}, u32[]{:S(2)}) collective-permute-start(bf16[64,2048]{1,0:T(8,128)(2,1)S(1)} %fusion.12), channel_id=1, source_target_pairs={{0,8},{2,10},{4,12},{6,14},{8,16},{10,18},{12,20},{14,22},{16,24},... | collective-permute-start | bytes 786440 | tf_op jit(solution)/shard_map/ppermute | solution.py:174
  161.3 7.3 %collective-permute-start.25 = (bf16[64,2048]{1,0:T(8,128)(2,1)S(1)}, bf16[64,2048]{1,0:T(8,128)(2,1)S(1)}, u32[]{:S(2)}, u32[]{:S(2)}) collective-permute-start(bf16[64,2048]{1,0:T(8,128)(2,1)S(1)} %fusion.19), channel_id=1, source_target_pairs={{0,4},{2,6},{4,0},{6,2},{8,12},{10,14},{12,8},{14,10},{16,20},{18,... | collective-permute-start | bytes 786440 | tf_op jit(solution)/shard_map/ppermute | solution.py:171
  167.4 6.4 %collective-permute-start.29 = (bf16[64,2048]{1,0:T(8,128)(2,1)S(1)}, bf16[64,2048]{1,0:T(8,128)(2,1)S(1)}, u32[]{:S(2)}, u32[]{:S(2)}) collective-permute-start(bf16[64,2048]{1,0:T(8,128)(2,1)S(1)} %fusion.20), channel_id=1, source_target_pairs={{0,4},{2,6},{4,0},{6,2},{8,12},{10,14},{12,8},{14,10},{16,20},{18,... | collective-permute-start | bytes 786440 | tf_op jit(solution)/shard_map/ppermute | solution.py:171
  168.8 13.5 %collective-permute-start.26 = (bf16[64,2048]{1,0:T(8,128)(2,1)S(1)}, bf16[64,2048]{1,0:T(8,128)(2,1)S(1)}, u32[]{:S(2)}, u32[]{:S(2)}) collective-permute-start(bf16[64,2048]{1,0:T(8,128)(2,1)S(1)} %fusion.8), channel_id=1, source_target_pairs={{0,16},{2,18},{4,20},{6,22},{8,24},{10,26},{12,28},{14,30},{16,0},... | collective-permute-start | bytes 786440 | tf_op jit(solution)/shard_map/ppermute | solution.py:174

commit v3 on v2

v3 whole, which is shorter than its diff:
```python
import functools
import jax
import jax.numpy as jnp
from jax import lax
from jax.experimental import pallas as pl
from jax.experimental.pallas import tpu as pltpu
from jax.sharding import PartitionSpec as P

PLANE = 4
TILE = 256
OUT_TILE = 512


def dot_t(rows, weight):
    return lax.dot_general(rows, weight, (((1,), (1,)), ((), ())), preferred_element_type=jnp.float32)


def launch(copies, sems, src, dst):
    copy = pltpu.make_async_copy(src, dst, sems.at[len(copies)])
    copy.start()
    copies.append(copy)


def row_chunks(count):
    size = count // 4 if count % 64 == 0 else count
    return [(first, size) for first in range(0, count, size)]


def layer_kernel(plan, *refs):
    experts, planes, ties = plan
    blocks = [refs[4 * i : 4 * i + 4] for i in range(len(planes))]
    refs = refs[4 * len(planes) :]
    gates, shared = refs[:2]
    weights = [refs[2 + 3 * e : 5 + 3 * e] for e in range(experts)]
    refs = refs[2 + 3 * experts + ties :]
    outs = [refs[2 * i : 2 * i + 2] for i in range(len(planes))]
    rows, w_gate, w_up, w_down, hidden, sems = refs[2 * len(planes) :]
    step, width = blocks[0][0].shape
    count, units = weights[0][0].shape[0], shared.shape[1]
    base = experts * count
    chunks = [
        (e, e * count + first, size) for e in range(experts) for first, size in row_chunks(count)
    ]
    chunks.append((None, base, units))
    copies = []
    for e, first, size in chunks:
        for kind, held in ((0, w_gate), (1, w_up)):
            if e is None:
                source = shared.at[kind]
            else:
                source = weights[e][kind].at[pl.ds(first - e * count, size)]
            launch(copies, sems, source, held.at[pl.ds(first, size)])
    head = len(copies)
    for lower in range(0, width, OUT_TILE):
        columns = pl.ds(lower, OUT_TILE)
        for e in range(experts):
            part = w_down.at[pl.ds(e * count, count), columns]
            launch(copies, sems, weights[e][2].at[:, columns], part)
        launch(copies, sems, shared.at[2].at[:, columns], w_down.at[pl.ds(base, units), columns])
    for k, block in enumerate([block for plane in blocks for block in plane]):
        rows[k * step : (k + 1) * step, :] = block[...]
    columns = []
    for e in range(experts):
        parts = []
        for plane in planes:
            line = gates[plane, e : e + 1, :]
            parts.append(jnp.broadcast_to(line, (128, line.shape[1])).T[:, 0:1])
        columns.append(jnp.concatenate(parts, axis=0))
    ready = 0
    ranges = [(e, e * count, (e + 1) * count) for e in range(experts)]
    for e, first, end in ranges + [(None, base, base + units)]:
        for lower in range(first, end, TILE):
            upper = min(end, lower + TILE)
            while ready < len(chunks) and chunks[ready][1] < upper:
                copies[2 * ready].wait()
                copies[2 * ready + 1].wait()
                ready += 1
            pre = dot_t(rows[...], w_gate[lower:upper, :])
            value = jax.nn.silu(pre) * dot_t(rows[...], w_up[lower:upper, :])
            if e is not None:
                value = value * columns[e]
            hidden[:, lower:upper] = value.astype(jnp.bfloat16)
    for n in range(width // OUT_TILE):
        lower, upper = n * OUT_TILE, (n + 1) * OUT_TILE
        for copy in copies[head + n * (experts + 1) : head + (n + 1) * (experts + 1)]:
            copy.wait()
        part = jnp.dot(hidden[...], w_down[:, lower:upper], preferred_element_type=jnp.float32)
        part = part.astype(jnp.bfloat16)
        for i, (keep, send) in enumerate(outs):
            kept, sent = ((0, 2), (1, 3)) if i % 2 == 0 else ((0, 1), (2, 3))
            for ref, which in ((keep, kept), (send, sent)):
                for j, k in enumerate(which):
                    first = (PLANE * i + k) * step
                    ref[j, :, lower:upper] = part[first : first + step]


def layer(blocks, gates, trios, shared, planes, after):
    step, width = blocks[0][0].shape
    experts, units = len(trios), shared.shape[1]
    count = trios[0][0].shape[0]
    total = experts * count + units
    depth = len(planes) * PLANE * step
    pair = jax.ShapeDtypeStruct((2, step, width), jnp.bfloat16)
    held = pltpu.VMEM((total, width), jnp.bfloat16)
    sems = 2 * (experts * len(row_chunks(count)) + 1) + (width // OUT_TILE) * (experts + 1)
    inputs = [block for plane in blocks for block in plane]
    out = pl.pallas_call(
        functools.partial(layer_kernel, (experts, tuple(planes), len(after))),
        out_shape=[pair] * (2 * len(planes)),
        in_specs=[pl.BlockSpec(memory_space=pltpu.VMEM)] * (len(inputs) + 1)
        + [pl.BlockSpec(memory_space=pl.ANY)] * (1 + 3 * experts + len(after)),
        out_specs=[pl.BlockSpec(memory_space=pltpu.VMEM)] * (2 * len(planes)),
        scratch_shapes=[
            pltpu.VMEM((depth, width), jnp.bfloat16),
            held,
            held,
            held,
            pltpu.VMEM((depth, total), jnp.bfloat16),
            pltpu.SemaphoreType.DMA((sems,)),
        ],
        compiler_params=pltpu.CompilerParams(vmem_limit_bytes=60 * 1024 * 1024),
        cost_estimate=pl.CostEstimate(
            flops=6 * depth * width * total,
            bytes_accessed=6 * total * width,
            transcendentals=depth * total,
        ),
    )(*inputs, gates, shared, *[w for trio in trios for w in trio], *after)
    return [(out[2 * i], out[2 * i + 1]) for i in range(len(planes))]


def cut_kernel(units, padded, gate, up, down, coded, out):
    wide, chunk = out.shape[0], out.shape[2]
    gate_t, up_t = gate[...].T, up[...].T
    blank = jnp.zeros((padded - units, chunk), jnp.bfloat16)
    for w in range(wide):
        part = slice(w * units, (w + 1) * units)
        out[w, 0:units, :] = gate_t[part]
        out[w, units:padded, :] = coded[w]
        out[w, padded : padded + units, :] = up_t[part]
        out[w, padded + units : 2 * padded, :] = blank
        out[w, 2 * padded : 2 * padded + units, :] = down[part, :]
        out[w, 2 * padded + units : 3 * padded, :] = blank


def cut(gate, up, down, coded, units, padded):
    wide, chunk = coded.shape[0], down.shape[1]
    coded = coded.reshape(wide, padded - units, chunk)
    if chunk % 128 == 0 and units % 8 == 0 and units * wide == gate.shape[1]:
        return pl.pallas_call(
            functools.partial(cut_kernel, units, padded),
            out_shape=jax.ShapeDtypeStruct((wide, 3 * padded, chunk), jnp.bfloat16),
            in_specs=[pl.BlockSpec(memory_space=pltpu.VMEM)] * 4,
            out_specs=pl.BlockSpec(memory_space=pltpu.VMEM),
            compiler_params=pltpu.CompilerParams(vmem_limit_bytes=60 * 1024 * 1024),
            cost_estimate=pl.CostEstimate(
                flops=0, bytes_accessed=16 * down.size, transcendentals=0
            ),
        )(gate, up, down, coded)
    parts = []
    blank = jnp.zeros((wide, padded - units, chunk), jnp.bfloat16)
    for weight, tail in ((gate.T, coded), (up.T, blank), (down, blank)):
        weight = jnp.pad(weight, ((0, units * wide - weight.shape[0]), (0, 0)))
        parts += [weight.reshape(wide, units, chunk), tail]
    return jnp.concatenate(parts, axis=1)


def lay_out_kernel(units, *refs):
    parts, out = refs[:-1], refs[-1]
    for s, part in enumerate(parts):
        wide, _, chunk = part.shape
        for kind in range(3):
            for w in range(wide):
                out[kind, s * units : (s + 1) * units, w * chunk : (w + 1) * chunk] = part[
                    w, kind * units : (kind + 1) * units, :
                ]


def lay_out(parts, units, width):
    if parts[0].shape[2] % 128:
        shaped = [p.reshape(p.shape[0], 3, units, p.shape[2]) for p in parts]
        shaped = [jnp.transpose(p, (1, 2, 0, 3)).reshape(3, units, width) for p in shaped]
        return jnp.concatenate(shaped, axis=1)
    return pl.pallas_call(
        functools.partial(lay_out_kernel, units),
        out_shape=jax.ShapeDtypeStruct((3, units * len(parts), width), jnp.bfloat16),
        in_specs=[pl.BlockSpec(memory_space=pltpu.VMEM)] * len(parts),
        out_specs=pl.BlockSpec(memory_space=pltpu.VMEM),
        compiler_params=pltpu.CompilerParams(vmem_limit_bytes=60 * 1024 * 1024),
        cost_estimate=pl.CostEstimate(
            flops=0, bytes_accessed=12 * units * len(parts) * width, transcendentals=0
        ),
    )(*parts)


def body(
    tokens,
    expert_ids,
    route_gates,
    expert_gate,
    expert_up,
    expert_down,
    shared_gate,
    shared_up,
    shared_down,
):
    wide = lax.axis_size("wide")
    narrow = lax.axis_size("narrow")
    lines = wide // PLANE
    tok_rows = tokens.shape[0]
    own_rows = tok_rows // narrow
    local_experts = expert_gate.shape[0]
    width = expert_gate.shape[2]
    experts_all = local_experts * wide
    here = lax.axis_index("wide")
    core = lax.axis_index("narrow")

    def flip(value, bits):
        return lax.ppermute(value, "wide", [(w, w ^ bits) for w in range(wide)])

    def shift(value, by):
        return lax.ppermute(
            value, "wide", [(w, (w + PLANE * by) % wide) for w in range(wide)]
        )

    def turn(value, by):
        return lax.ppermute(value, "narrow", [(c, (c + by) % narrow) for c in range(narrow)])

    mine = lax.all_to_all(tokens, "narrow", split_axis=0, concat_axis=1, tiled=True)

    own_ids = lax.dynamic_slice_in_dim(expert_ids, core * own_rows, own_rows, 0)
    own_gates = lax.dynamic_slice_in_dim(route_gates, core * own_rows, own_rows, 0)
    numbers = jnp.arange(experts_all, dtype=jnp.int32)
    chosen = own_ids.T[:, None, :] == numbers[None, :, None]
    table = jnp.sum(jnp.where(chosen, own_gates.T[:, None, :], 0.0), axis=0)
    table = table.reshape(wide, local_experts * own_rows)
    high = table.astype(jnp.bfloat16)
    low = (table - high.astype(jnp.float32)).astype(jnp.bfloat16)
    coded = jnp.concatenate([high, low], axis=1)

    hidden_local = shared_gate.shape[1]
    units = -(-hidden_local // wide)
    chunk = shared_down.shape[1]
    gate_rows = -(-coded.shape[1] // chunk)
    padded = -(-(units + gate_rows) // 16) * 16
    coded = jnp.pad(coded, ((0, 0), (0, (padded - units) * chunk - coded.shape[1])))
    stacked = cut(shared_gate, shared_up, shared_down, coded, units, padded)

    near = sorted({1, lines - 1} - {0, lines})
    rest = [d for d in range(1, lines) if d not in near]
    planes = rest + near + [0]
    x_first = {d: n % 2 == 0 for n, d in enumerate(planes)}
    lined, by_x, by_y = {0: mine}, {}, {}
    for d in near:
        lined[d] = shift(mine, d)
    by_x[0], by_y[0] = flip(mine, 1), flip(mine, 2)
    experts = (expert_gate, expert_up, expert_down)
    lined, by_x, by_y, stacked, experts = lax.optimization_barrier(
        (lined, by_x, by_y, stacked, experts)
    )
    trios = [
        tuple(lax.all_gather(weight[e], "narrow", axis=0, tiled=True) for weight in experts)
        for e in range(local_experts)
    ]
    for d in rest:
        lined[d] = shift(lined[0], d)
    for d in near:
        by_x[d], by_y[d] = flip(lined[d], 1), flip(lined[d], 2)
    lined, by_x, by_y, stacked = lax.optimization_barrier((lined, by_x, by_y, stacked))
    recut = lax.all_to_all(stacked, "wide", split_axis=0, concat_axis=0, tiled=True)
    for d in rest:
        by_x[d], by_y[d] = flip(lined[d], 1), flip(lined[d], 2)
    blocks = {}
    for d in [0] + near + rest:
        far = flip(by_x[d], 2) if x_first[d] else flip(by_y[d], 1)
        blocks[d] = (lined[d], by_x[d], by_y[d], far)
    recut, blocks = lax.optimization_barrier((recut, blocks))
    shared = lay_out([recut] + [turn(recut, s) for s in range(1, narrow)], padded, width)
    coded = recut[:, units : units + gate_rows].reshape(wide, gate_rows * chunk)
    coded = coded.astype(jnp.float32)
    size = local_experts * own_rows
    table = (coded[:, :size] + coded[:, size : 2 * size]).reshape(wide, local_experts, own_rows)

    order = jnp.arange(wide, dtype=jnp.int32)
    line, place = here // PLANE, here % PLANE
    source = ((line - order // PLANE) % lines) * PLANE + (place ^ (order % PLANE))
    picks = source[:, None] == jnp.arange(wide, dtype=jnp.int32)[None, :]
    gates = jnp.sum(jnp.where(picks[:, :, None, None], table[None], 0.0), axis=1)
    gates = jnp.transpose(gates.reshape(lines, PLANE, local_experts, own_rows), (0, 2, 1, 3))
    gates = gates.reshape(lines, local_experts, PLANE * own_rows)

    def collect(out, group, waiting):
        for d, (onward, total) in zip(group, waiting):
            total = total + flip(onward, 2 if x_first[d] else 1).astype(jnp.float32)
            if d:
                total = shift(total.astype(jnp.bfloat16), -d).astype(jnp.float32)
            out = total if out is None else out + total
        return out

    out, after, waiting = None, [], []
    for i in range(0, lines, 2):
        group = planes[i : i + 2]
        parts = layer([blocks[d] for d in group], gates, trios, shared, group, after)
        after = [parts[0][0]]
        parts, waiting = lax.optimization_barrier((parts, waiting))
        coming = []
        for d, (keep, send) in zip(group, parts):
            got = flip(send, 1 if x_first[d] else 2).astype(jnp.float32)
            onward = (keep[1].astype(jnp.float32) + got[1]).astype(jnp.bfloat16)
            coming.append((onward, keep[0].astype(jnp.float32) + got[0]))
        out = collect(out, planes[i - 2 : i], waiting) if i else out
        waiting = coming
    out = collect(out, planes[-2:], waiting)
    return lax.all_to_all(
        out.astype(jnp.bfloat16), "narrow", split_axis=1, concat_axis=0, tiled=True
    )


def solution(mesh):
    return jax.shard_map(
        body,
        mesh=mesh,
        in_specs=(
            P("wide", "narrow"),
            P("wide", None),
            P("wide", None),
            P("wide", "narrow", None),
            P("wide", "narrow", None),
            P("wide", "narrow", None),
            P("wide", "narrow"),
            P("wide", "narrow"),
            P("narrow", "wide"),
        ),
        out_specs=P("wide", "narrow"),
        check_vma=False,
    )
```

time: 188 us -> 182 us (0.968)
  between operations: 0.3 us -> 13.4 us
  local copies, waits for them, and re-layouts: 15.6 us -> 6.84 us
  waiting for transfers between devices: 73.5 us -> 66.2 us
    ppermute x20, waiting for transfers between devices: 57.1 us -> 41.7 us  [flip(): return lax.ppermute(value, 'wide', [(w, w ^ bits) for w in range(wide)])]
    ppermute x6, waiting for transfers between devices: 14.4 us -> 21.3 us  [shift(): lax.ppermute(value, 'wide', [(w, (w + PLANE * by) % wide) for w in range(...]
    unnamed x35 -> x50, local copies, waits for them, and re-layouts: 11.2 us -> 5.28 us
    pallas_call x4 -> x3, Pallas kernels: 41.3 us -> 38.3 us  [the longest x2 35.8 us: layer(): pl.pallas_call(functools.partial(layer_kernel, (experts, tuple(planes), l...]
    transpose x2 -> x0, local copies, waits for them, and re-layouts: 2.78 us -> none
  transfers between devices with their start and end apart: 31 -> 31, of which waited for: 16 -> 12; matrix products, arithmetic and copies ran while one was open for 7% -> 2% of each run, Pallas kernels for 17% -> 13%
where the time goes in v3:
time: 182 us; the launch traced here: 181 us
  waiting for transfers between devices  66.2 us (36%)
  starting transfers between devices  42.4 us (23%)
  Pallas kernels  41.9 us (23%)
  between operations  13.4 us (7%)
  blocking collectives  9.06 us (5%)
  local copies, waits for them, and re-layouts  6.84 us (4%)
    ppermute x20, waiting for transfers between devices, flip(): return lax.ppermute(value, 'wide', [(w, w ^ bits) for w in range(wide)])  41.7 us
    pallas_call x2, Pallas kernels, layer(): pl.pallas_call(functools.partial(layer_kernel, (experts, tuple(planes), l...  35.8 us
    ppermute x20, starting transfers between devices, flip(): return lax.ppermute(value, 'wide', [(w, w ^ bits) for w in range(wide)])  22.6 us
    ppermute x6, waiting for transfers between devices, shift(): lax.ppermute(value, 'wide', [(w, (w + PLANE * by) % wide) for w in range(...  21.3 us
    ppermute x6, starting transfers between devices, shift(): lax.ppermute(value, 'wide', [(w, (w + PLANE * by) % wide) for w in range(...  13.8 us
    all_to_all x1, starting transfers between devices, body(): lax.all_to_all(stacked, 'wide', split_axis=0, concat_axis=0, tiled=True)  5.96 us
    unnamed x50, local copies, waits for them, and re-layouts  5.28 us
    all_to_all x1, blocking collectives, body(): lax.all_to_all(tokens, 'narrow', split_axis=0, concat_axis=1, tiled=True)  5.11 us
  transfers between devices with their start and end apart: 31, of which 12 were waited for; matrix products, arithmetic and copies ran while one was open for 2% of the time, Pallas kernels for 13%

profile of v3, /device:TPU:0, one launch (start us, length us, event | category | flops | bytes accessed | tf_op | source)
XLA Modules:
  0.0 181.4 jit_solution(7586403899421726869)
XLA Ops:
  6.5 5.1 %all_to_all.43 = bf16[2,64,1024]{2,1,0:T(8,128)(2,1)S(1)} all-to-all(bf16[2,64,1024]{2,1,0:T(8,128)(2,1)} %bitcast.52), channel_id=1, replica_groups=mesh['wide'=16,'narrow'=2] {'narrow'}, dimensions={0} | all-to-all | bytes 524288 | tf_op jit(solution)/shard_map/all_to_all | solution.py:228
  11.7 3.1 %collective-permute-start = (bf16[64,2048]{1,0:T(8,128)(2,1)S(1)}, bf16[64,2048]{1,0:T(8,128)(2,1)S(1)}, u32[]{:S(2)}, u32[]{:S(2)}) collective-permute-start(bf16[64,2048]{1,0:T(8,128)(2,1)S(1)} %bitcast.53), channel_id=1, source_target_pairs={{0,8},{2,10},{4,12},{6,14},{8,16},{10,18},{12,20},{14,22},{16,24},... | collective-permute-start | bytes 786440 | tf_op jit(solution)/shard_map/ppermute | solution.py:221
  14.8 2.1 %collective-permute-start.1 = (bf16[64,2048]{1,0:T(8,128)(2,1)S(1)}, bf16[64,2048]{1,0:T(8,128)(2,1)S(1)}, u32[]{:S(2)}, u32[]{:S(2)}) collective-permute-start(bf16[64,2048]{1,0:T(8,128)(2,1)S(1)} %bitcast.54), channel_id=1, source_target_pairs={{0,24},{2,26},{4,28},{6,30},{8,0},{10,2},{12,4},{14,6},{16,8},{18,... | collective-permute-start | bytes 786440 | tf_op jit(solution)/shard_map/ppermute | solution.py:221
  16.9 1.6 collective-permute-start.2
  18.5 1.5 collective-permute-start.3
  20.1 0.8 dynamic-slice_bitcast_fusion.1
  21.0 0.6 copy.18
  21.6 2.5 %shard_map.91 = bf16[16,288,128]{2,1,0:T(8,128)(2,1)} custom-call(bf16[128,1408]{1,0:T(8,128)(2,1)} %gate.1, bf16[128,1408]{1,0:T(8,128)(2,1)} %up.1, bf16[1408,128]{1,0:T(8,128)(2,1)} %down.1, bf16[16,8,128]{2,1,0:T(8,128)(2,1)} %bitcast.59), custom_call_target="tpu_custom_call" | custom-call | bytes 2883584 | tf_op jit(solution)/shard_map/pallas_call | solution.py:149
  24.0 4.4 %collective-permute-done.1.refs_0_ = bf16[64,2048]{1,0:T(8,128)(2,1)S(1)} collective-permute-done((bf16[64,2048]{1,0:T(8,128)(2,1)S(1)}, bf16[64,2048]{1,0:T(8,128)(2,1)S(1)}, u32[]{:S(2)}, u32[]{:S(2)}) %collective-permute-start.1) | collective-permute-done | bytes 262176 | tf_op jit(solution)/shard_map/ppermute | solution.py:221
  28.6 0.7 all-gather.9.cloned.1.call-update
  29.3 0.7 all-gather.11.cloned.1.call-update
  30.0 1.4 collective-permute-start.4
  31.4 1.5 collective-permute-start.5
  33.4 1.5 collective-permute-start.7
  35.5 8.8 %collective-permute-done.4.refs_0_ = bf16[64,2048]{1,0:T(8,128)(2,1)S(1)} collective-permute-done((bf16[64,2048]{1,0:T(8,128)(2,1)S(1)}, bf16[64,2048]{1,0:T(8,128)(2,1)S(1)}, u32[]{:S(2)}, u32[]{:S(2)}) %collective-permute-start.4) | collective-permute-done | bytes 262176 | tf_op jit(solution)/shard_map/ppermute | solution.py:221
  44.4 1.5 collective-permute-done.8.refs_2_
  45.9 0.7 copy-done.15
  46.6 6.0 %all-to-all-start.1 = ((bf16[16,288,128]{2,1,0:T(8,128)(2,1)}), bf16[16,288,128]{2,1,0:T(8,128)(2,1)S(1)}, u32[]{:S(2)}, u32[]{:S(2)}) async-start(bf16[16,288,128]{2,1,0:T(8,128)(2,1)} %shard_map.91), calls=%async_computation.1 | async-start | bytes 2359296 | tf_op jit(solution)/shard_map/all_to_all | solution.py:269
  52.6 1.9 %collective-permute-start.11 = (bf16[64,2048]{1,0:T(8,128)(2,1)S(1)}, bf16[64,2048]{1,0:T(8,128)(2,1)S(1)}, u32[]{:S(2)}, u32[]{:S(2)}) collective-permute-start(bf16[64,2048]{1,0:T(8,128)(2,1)S(1)} %collective-permute-done.4.refs_0_), channel_id=1, source_target_pairs={{0,2},{2,0},{4,6},{6,4},{8,10},{10,8},{12,14},{14,12},{16,18},{18,... | collective-permute-start | bytes 786440 | tf_op jit(solution)/shard_map/ppermute | solution.py:218
  54.5 1.5 collective-permute-start.12
  56.6 1.5 collective-permute-start.10
  58.6 12.6 %collective-permute-done.11.refs_1_ = bf16[64,2048]{1,0:T(8,128)(2,1)S(1)} collective-permute-done((bf16[64,2048]{1,0:T(8,128)(2,1)S(1)}, bf16[64,2048]{1,0:T(8,128)(2,1)S(1)}, u32[]{:S(2)}, u32[]{:S(2)}) %collective-permute-start.11) | collective-permute-done | bytes 262176 | tf_op jit(solution)/shard_map/ppermute | solution.py:218
  71.2 1.9 %collective-permute-start.13 = (bf16[64,2048]{1,0:T(8,128)(2,1)S(1)}, bf16[64,2048]{1,0:T(8,128)(2,1)}, u32[]{:S(2)}, u32[]{:S(2)}) collective-permute-start(bf16[64,2048]{1,0:T(8,128)(2,1)S(1)} %collective-permute-done.11.refs_1_), channel_id=1, source_target_pairs={{0,4},{2,6},{4,0},{6,2},{8,12},{10,14},{12,8},{14,10},{16,20},{18,... | collective-permute-start | bytes 786440 | tf_op jit(solution)/shard_map/ppermute | solution.py:218
  73.1 6.9 %collective-permute-done.9.refs_7_ = bf16[64,2048]{1,0:T(8,128)(2,1)S(1)} collective-permute-done((bf16[64,2048]{1,0:T(8,128)(2,1)S(1)}, bf16[64,2048]{1,0:T(8,128)(2,1)S(1)}, u32[]{:S(2)}, u32[]{:S(2)}) %collective-permute-start.9) | collective-permute-done | bytes 262176 | tf_op jit(solution)/shard_map/ppermute | solution.py:218
  80.0 2.8 %collective-permute-done.10.refs_7_ = bf16[64,2048]{1,0:T(8,128)(2,1)S(1)} collective-permute-done((bf16[64,2048]{1,0:T(8,128)(2,1)S(1)}, bf16[64,2048]{1,0:T(8,128)(2,1)S(1)}, u32[]{:S(2)}, u32[]{:S(2)}) %collective-permute-start.10) | collective-permute-done | bytes 262176 | tf_op jit(solution)/shard_map/ppermute | solution.py:218
  82.8 0.7 copy-done.23
  83.6 0.7 copy-done.20
  84.6 0.7 reshape_transpose_reshape.3.refs_8_
  85.3 1.8 %collective-permute-done.15.refs_1_ = bf16[16,288,128]{2,1,0:T(8,128)(2,1)S(1)} collective-permute-done((bf16[16,288,128]{2,1,0:T(8,128)(2,1)S(1)}, bf16[16,288,128]{2,1,0:T(8,128)(2,1)S(1)}, u32[]{:S(2)}, u32[]{:S(2)}) %collective-permute-start.15) | collective-permute-done | bytes 1179680 | tf_op jit(solution)/shard_map/ppermute | solution.py:226
  87.1 1.0 copy-done.2
  88.2 3.6 %shard_map.92.refs_9_ = bf16[3,192,2048]{2,1,0:T(8,128)(2,1)} custom-call(bf16[16,288,128]{2,1,0:T(8,128)(2,1)} %copy-done.1, bf16[16,288,128]{2,1,0:T(8,128)(2,1)} %copy-done.2), custom_call_target="tpu_custom_call" | custom-call | bytes 4718592 | tf_op jit(solution)/shard_map/pallas_call | solution.py:183
  91.8 17.8 %shard_map.93 = (bf16[2,64,2048]{2,1,0:T(8,128)(2,1)}, bf16[2,64,2048]{2,1,0:T(8,128)(2,1)}, bf16[2,64,2048]{2,1,0:T(8,128)(2,1)}, bf16[2,64,2048]{2,1,0:T(8,128)(2,1)}) custom-call(bf16[64,2048]{1,0:T(8,128)(2,1)} %copy-done.16, bf16[64,2048]{1,0:T(8,128)(2,1)} %copy-done.21, bf16[64,2048]{1,0:T(8,128)(2,1)} %copy-done.22, ...), custom_call_target="tpu_custom_call" | custom-call | flops 10066329600 | bytes 19660800 | tf_op jit(solution)/shard_map/pallas_call | solution.py:107
  110.0 1.7 collective-permute-start.17
  111.7 18.0 %shard_map.94 = (bf16[2,64,2048]{2,1,0:T(8,128)(2,1)}, bf16[2,64,2048]{2,1,0:T(8,128)(2,1)}, bf16[2,64,2048]{2,1,0:T(8,128)(2,1)}, bf16[2,64,2048]{2,1,0:T(8,128)(2,1)}) custom-call(bf16[64,2048]{1,0:T(8,128)(2,1)} %copy-done.10, bf16[64,2048]{1,0:T(8,128)(2,1)} %copy-done.14, bf16[64,2048]{1,0:T(8,128)(2,1)} %copy-done.15, bf16[64,2048]{1,0:T(8,128)(2,1)} %copy-done.20, ...), custom_call_target="tpu_custom_call" | custom-call | flops 10066329600 | bytes 19660800 | tf_op jit(solution)/shard_map/pallas_call | solution.py:107
  130.1 0.6 copy-done.4
  130.9 1.5 collective-permute-start.20
  133.3 1.7 collective-permute-start.18
  135.0 5.2 %collective-permute-done.20 = bf16[64,2048]{1,0:T(8,128)(2,1)S(1)} collective-permute-done((bf16[64,2048]{1,0:T(8,128)(2,1)S(1)}, bf16[64,2048]{1,0:T(8,128)(2,1)S(1)}, u32[]{:S(2)}, u32[]{:S(2)}) %collective-permute-start.20) | collective-permute-done | bytes 262176 | tf_op jit(solution)/shard_map/ppermute | solution.py:218
  140.2 3.3 %collective-permute-start.21 = (bf16[64,2048]{1,0:T(8,128)(2,1)S(1)}, bf16[64,2048]{1,0:T(8,128)(2,1)S(1)}, u32[]{:S(2)}, u32[]{:S(2)}) collective-permute-start(bf16[64,2048]{1,0:T(8,128)(2,1)S(1)} %add_convert_fusion), channel_id=1, source_target_pairs={{0,24},{2,26},{4,28},{6,30},{8,0},{10,2},{12,4},{14,6},{16,8},{18,... | collective-permute-start | bytes 786440 | tf_op jit(solution)/shard_map/ppermute | solution.py:221
  143.6 7.6 %collective-permute-done.18 = bf16[64,2048]{1,0:T(8,128)(2,1)S(1)} collective-permute-done((bf16[64,2048]{1,0:T(8,128)(2,1)S(1)}, bf16[64,2048]{1,0:T(8,128)(2,1)S(1)}, u32[]{:S(2)}, u32[]{:S(2)}) %collective-permute-start.18) | collective-permute-done | bytes 262176 | tf_op jit(solution)/shard_map/ppermute | solution.py:218
  151.2 2.4 %collective-permute-start.19 = (bf16[64,2048]{1,0:T(8,128)(2,1)S(1)}, bf16[64,2048]{1,0:T(8,128)(2,1)S(1)}, u32[]{:S(2)}, u32[]{:S(2)}) collective-permute-start(bf16[64,2048]{1,0:T(8,128)(2,1)S(1)} %add_convert_fusion.1), channel_id=1, source_target_pairs={{0,16},{2,18},{4,20},{6,22},{8,24},{10,26},{12,28},{14,30},{16,0},... | collective-permute-start | bytes 786440 | tf_op jit(solution)/shard_map/ppermute | solution.py:221
  153.8 0.6 collective-permute-start.23
  154.6 0.6 collective-permute-start.26
  155.3 5.0 %collective-permute-done.23 = bf16[64,2048]{1,0:T(8,128)(2,1)S(1)} collective-permute-done((bf16[64,2048]{1,0:T(8,128)(2,1)S(1)}, bf16[64,2048]{1,0:T(8,128)(2,1)S(1)}, u32[]{:S(2)}, u32[]{:S(2)}) %collective-permute-start.23) | collective-permute-done | bytes 262176 | tf_op jit(solution)/shard_map/ppermute | solution.py:218
  160.4 1.5 collective-permute-start.24
  161.9 8.1 %collective-permute-done.19 = bf16[64,2048]{1,0:T(8,128)(2,1)S(1)} collective-permute-done((bf16[64,2048]{1,0:T(8,128)(2,1)S(1)}, bf16[64,2048]{1,0:T(8,128)(2,1)S(1)}, u32[]{:S(2)}, u32[]{:S(2)}) %collective-permute-start.19) | collective-permute-done | bytes 262176 | tf_op jit(solution)/shard_map/ppermute | solution.py:221
  170.2 3.9 %all_to_all.44 = bf16[64,2,1024]{2,0,1:T(8,128)(2,1)S(1)} all-to-all(bf16[64,2,1024]{2,0,1:T(8,128)(2,1)S(1)} %bitcast.48), channel_id=1, replica_groups=mesh['wide'=16,'narrow'=2] {'narrow'}, dimensions={1} | all-to-all | bytes 524288 | tf_op jit(solution)/shard_map/all_to_all | solution.py:313
  174.2 0.7 copy.22
  (98 shorter events, 5.5 us)
Async XLA Ops:
  6.5 13.5 %copy-start = (f32[128,6]{0,1:T(8,128)S(1)}, f32[128,6]{0,1:T(8,128)}, u32[]{:S(2)}) copy-start(f32[128,6]{0,1:T(8,128)} %param.11) | copy-start | bytes 9220
  6.5 85.2 %all-gather.7.cloned.1.call-start = ((), (), s32[]{:S(2)}) async-start(), calls=%async_computation.3 | async-start | bytes 8650752 | tf_op jit(solution)/shard_map/all_gather | solution.py:261
  11.7 18.3 %copy-start.7 = (bf16[2,8,8,1024]{3,2,0,1:T(8,128)(2,1)}, bf16[2,8,8,1024]{3,2,0,1:T(8,128)(2,1)S(1)}, u32[]{:S(2)}) copy-start(bf16[2,8,8,1024]{3,2,0,1:T(8,128)(2,1)S(1)} %copy.17) | copy-start | bytes 786436
  11.7 12.4 %collective-permute-start = (bf16[64,2048]{1,0:T(8,128)(2,1)S(1)}, bf16[64,2048]{1,0:T(8,128)(2,1)S(1)}, u32[]{:S(2)}, u32[]{:S(2)}) collective-permute-start(bf16[64,2048]{1,0:T(8,128)(2,1)S(1)} %bitcast.53), channel_id=1, source_target_pairs={{0,8},{2,10},{4,12},{6,14},{8,16},{10,18},{12,20},{14,22},{16,24},... | collective-permute-start | bytes 786440 | tf_op jit(solution)/shard_map/ppermute | solution.py:221
  14.8 13.7 %collective-permute-start.1 = (bf16[64,2048]{1,0:T(8,128)(2,1)S(1)}, bf16[64,2048]{1,0:T(8,128)(2,1)S(1)}, u32[]{:S(2)}, u32[]{:S(2)}) collective-permute-start(bf16[64,2048]{1,0:T(8,128)(2,1)S(1)} %bitcast.54), channel_id=1, source_target_pairs={{0,24},{2,26},{4,28},{6,30},{8,0},{10,2},{12,4},{14,6},{16,8},{18,... | collective-permute-start | bytes 786440 | tf_op jit(solution)/shard_map/ppermute | solution.py:221
  16.9 11.6 %collective-permute-start.2 = (bf16[64,2048]{1,0:T(8,128)(2,1)S(1)}, bf16[64,2048]{1,0:T(8,128)(2,1)S(1)}, u32[]{:S(2)}, u32[]{:S(2)}) collective-permute-start(bf16[64,2048]{1,0:T(8,128)(2,1)S(1)} %bitcast.55), channel_id=1, source_target_pairs={{0,2},{2,0},{4,6},{6,4},{8,10},{10,8},{12,14},{14,12},{16,18},{18,... | collective-permute-start | bytes 786440 | tf_op jit(solution)/shard_map/ppermute | solution.py:218
  18.5 10.0 %collective-permute-start.3 = (bf16[64,2048]{1,0:T(8,128)(2,1)S(1)}, bf16[64,2048]{1,0:T(8,128)(2,1)S(1)}, u32[]{:S(2)}, u32[]{:S(2)}) collective-permute-start(bf16[64,2048]{1,0:T(8,128)(2,1)S(1)} %bitcast.56), channel_id=1, source_target_pairs={{0,4},{2,6},{4,0},{6,2},{8,12},{10,14},{12,8},{14,10},{16,20},{18,... | collective-permute-start | bytes 786440 | tf_op jit(solution)/shard_map/ppermute | solution.py:218
  24.0 9.4 %copy-start.13 = (bf16[64,2048]{1,0:T(8,128)(2,1)}, bf16[64,2048]{1,0:T(8,128)(2,1)S(1)}, u32[]{:S(2)}) copy-start(bf16[64,2048]{1,0:T(8,128)(2,1)S(1)} %collective-permute-done.refs_4_) | copy-start | bytes 786436
  28.5 6.5 %copy-start.10 = (bf16[64,2048]{1,0:T(8,128)(2,1)}, bf16[64,2048]{1,0:T(8,128)(2,1)S(1)}, u32[]{:S(2)}) copy-start(bf16[64,2048]{1,0:T(8,128)(2,1)S(1)} %collective-permute-done.1.refs_0_) | copy-start | bytes 786436
  28.5 27.5 %copy-start.12 = (bf16[64,2048]{1,0:T(8,128)(2,1)}, bf16[64,2048]{1,0:T(8,128)(2,1)S(1)}, u32[]{:S(2)}) copy-start(bf16[64,2048]{1,0:T(8,128)(2,1)S(1)} %collective-permute-done.3.refs_6_) | copy-start | bytes 786436
  28.5 63.3 %all-gather.9.cloned.1.call-start = ((), (), s32[]{:S(2)}) async-start(), calls=%async_computation.4 | async-start | bytes 8650752 | tf_op jit(solution)/shard_map/all_gather | solution.py:261
  29.3 62.5 %all-gather.11.cloned.1.call-start = ((), (), s32[]{:S(2)}) async-start(), calls=%async_computation.5 | async-start | bytes 8650752 | tf_op jit(solution)/shard_map/all_gather | solution.py:261
  30.0 14.2 %collective-permute-start.4 = (bf16[64,2048]{1,0:T(8,128)(2,1)S(1)}, bf16[64,2048]{1,0:T(8,128)(2,1)S(1)}, u32[]{:S(2)}, u32[]{:S(2)}) collective-permute-start(bf16[64,2048]{1,0:T(8,128)(2,1)S(1)} %bitcast.57), channel_id=1, source_target_pairs={{0,16},{2,18},{4,20},{6,22},{8,24},{10,26},{12,28},{14,30},{16,0},... | collective-permute-start | bytes 786440 | tf_op jit(solution)/shard_map/ppermute | solution.py:221
  31.4 12.9 %collective-permute-start.5 = (bf16[64,2048]{1,0:T(8,128)(2,1)S(1)}, bf16[64,2048]{1,0:T(8,128)(2,1)S(1)}, u32[]{:S(2)}, u32[]{:S(2)}) collective-permute-start(bf16[64,2048]{1,0:T(8,128)(2,1)S(1)} %collective-permute-done.refs_4_), channel_id=1, source_target_pairs={{0,2},{2,0},{4,6},{6,4},{8,10},{10,8},{12,14},{14,12},{16,18},{18,... | collective-permute-start | bytes 786440 | tf_op jit(solution)/shard_map/ppermute | solution.py:218
  32.9 11.6 %collective-permute-start.6 = (bf16[64,2048]{1,0:T(8,128)(2,1)S(1)}, bf16[64,2048]{1,0:T(8,128)(2,1)S(1)}, u32[]{:S(2)}, u32[]{:S(2)}) collective-permute-start(bf16[64,2048]{1,0:T(8,128)(2,1)S(1)} %collective-permute-done.1.refs_0_), channel_id=1, source_target_pairs={{0,2},{2,0},{4,6},{6,4},{8,10},{10,8},{12,14},{14,12},{16,18},{18,... | collective-permute-start | bytes 786440 | tf_op jit(solution)/shard_map/ppermute | solution.py:218
  33.4 11.0 %collective-permute-start.7 = (bf16[64,2048]{1,0:T(8,128)(2,1)S(1)}, bf16[64,2048]{1,0:T(8,128)(2,1)S(1)}, u32[]{:S(2)}, u32[]{:S(2)}) collective-permute-start(bf16[64,2048]{1,0:T(8,128)(2,1)S(1)} %collective-permute-done.refs_4_), channel_id=1, source_target_pairs={{0,4},{2,6},{4,0},{6,2},{8,12},{10,14},{12,8},{14,10},{16,20},{18,... | collective-permute-start | bytes 786440 | tf_op jit(solution)/shard_map/ppermute | solution.py:218
  34.9 11.0 %collective-permute-start.8 = (bf16[64,2048]{1,0:T(8,128)(2,1)S(1)}, bf16[64,2048]{1,0:T(8,128)(2,1)S(1)}, u32[]{:S(2)}, u32[]{:S(2)}) collective-permute-start(bf16[64,2048]{1,0:T(8,128)(2,1)S(1)} %collective-permute-done.1.refs_0_), channel_id=1, source_target_pairs={{0,4},{2,6},{4,0},{6,2},{8,12},{10,14},{12,8},{14,10},{16,20},{18,... | collective-permute-start | bytes 786440 | tf_op jit(solution)/shard_map/ppermute | solution.py:218
  44.2 39.3 %copy-start.16 = (bf16[64,2048]{1,0:T(8,128)(2,1)}, bf16[64,2048]{1,0:T(8,128)(2,1)S(1)}, u32[]{:S(2)}) copy-start(bf16[64,2048]{1,0:T(8,128)(2,1)S(1)} %collective-permute-done.4.refs_0_) | copy-start | bytes 786436
  44.3 1.7 copy-start.17
  44.4 47.3 %copy-start.14 = (bf16[64,2048]{1,0:T(8,128)(2,1)}, bf16[64,2048]{1,0:T(8,128)(2,1)S(1)}, u32[]{:S(2)}) copy-start(bf16[64,2048]{1,0:T(8,128)(2,1)S(1)} %collective-permute-done.6.refs_1_) | copy-start | bytes 786436
  44.4 39.1 %copy-start.18 = (bf16[64,2048]{1,0:T(8,128)(2,1)}, bf16[64,2048]{1,0:T(8,128)(2,1)S(1)}, u32[]{:S(2)}) copy-start(bf16[64,2048]{1,0:T(8,128)(2,1)S(1)} %collective-permute-done.7.refs_6_) | copy-start | bytes 786436
  46.6 37.6 %all-to-all-start.1 = ((bf16[16,288,128]{2,1,0:T(8,128)(2,1)}), bf16[16,288,128]{2,1,0:T(8,128)(2,1)S(1)}, u32[]{:S(2)}, u32[]{:S(2)}) async-start(bf16[16,288,128]{2,1,0:T(8,128)(2,1)} %shard_map.91), calls=%async_computation.1 | async-start | bytes 2359296 | tf_op jit(solution)/shard_map/all_to_all | solution.py:269
  52.6 18.6 %collective-permute-start.11 = (bf16[64,2048]{1,0:T(8,128)(2,1)S(1)}, bf16[64,2048]{1,0:T(8,128)(2,1)S(1)}, u32[]{:S(2)}, u32[]{:S(2)}) collective-permute-start(bf16[64,2048]{1,0:T(8,128)(2,1)S(1)} %collective-permute-done.4.refs_0_), channel_id=1, source_target_pairs={{0,2},{2,0},{4,6},{6,4},{8,10},{10,8},{12,14},{14,12},{16,18},{18,... | collective-permute-start | bytes 786440 | tf_op jit(solution)/shard_map/ppermute | solution.py:218
  54.5 28.2 %collective-permute-start.12 = (bf16[64,2048]{1,0:T(8,128)(2,1)S(1)}, bf16[64,2048]{1,0:T(8,128)(2,1)S(1)}, u32[]{:S(2)}, u32[]{:S(2)}) collective-permute-start(bf16[64,2048]{1,0:T(8,128)(2,1)S(1)} %collective-permute-done.4.refs_0_), channel_id=1, source_target_pairs={{0,4},{2,6},{4,0},{6,2},{8,12},{10,14},{12,8},{14,10},{16,20},{18,... | collective-permute-start | bytes 786440 | tf_op jit(solution)/shard_map/ppermute | solution.py:218
  56.0 24.0 %collective-permute-start.9 = (bf16[64,2048]{1,0:T(8,128)(2,1)S(1)}, bf16[64,2048]{1,0:T(8,128)(2,1)S(1)}, u32[]{:S(2)}, u32[]{:S(2)}) collective-permute-start(bf16[64,2048]{1,0:T(8,128)(2,1)S(1)} %collective-permute-done.3.refs_6_), channel_id=1, source_target_pairs={{0,2},{2,0},{4,6},{6,4},{8,10},{10,8},{12,14},{14,12},{16,18},{18,... | collective-permute-start | bytes 786440 | tf_op jit(solution)/shard_map/ppermute | solution.py:218
  56.6 26.2 %collective-permute-start.10 = (bf16[64,2048]{1,0:T(8,128)(2,1)S(1)}, bf16[64,2048]{1,0:T(8,128)(2,1)S(1)}, u32[]{:S(2)}, u32[]{:S(2)}) collective-permute-start(bf16[64,2048]{1,0:T(8,128)(2,1)S(1)} %collective-permute-done.7.refs_6_), channel_id=1, source_target_pairs={{0,2},{2,0},{4,6},{6,4},{8,10},{10,8},{12,14},{14,12},{16,18},{18,... | collective-permute-start | bytes 786440 | tf_op jit(solution)/shard_map/ppermute | solution.py:218
  58.0 24.8 %collective-permute-start.14 = (bf16[64,2048]{1,0:T(8,128)(2,1)S(1)}, bf16[64,2048]{1,0:T(8,128)(2,1)S(1)}, u32[]{:S(2)}, u32[]{:S(2)}) collective-permute-start(bf16[64,2048]{1,0:T(8,128)(2,1)S(1)} %collective-permute-done.6.refs_1_), channel_id=1, source_target_pairs={{0,4},{2,6},{4,0},{6,2},{8,12},{10,14},{12,8},{14,10},{16,20},{18,... | collective-permute-start | bytes 786440 | tf_op jit(solution)/shard_map/ppermute | solution.py:218
  71.2 12.4 %copy-start.21 = (bf16[64,2048]{1,0:T(8,128)(2,1)}, bf16[64,2048]{1,0:T(8,128)(2,1)S(1)}, u32[]{:S(2)}) copy-start(bf16[64,2048]{1,0:T(8,128)(2,1)S(1)} %collective-permute-done.11.refs_1_) | copy-start | bytes 786436
  71.2 12.4 %collective-permute-start.13 = (bf16[64,2048]{1,0:T(8,128)(2,1)S(1)}, bf16[64,2048]{1,0:T(8,128)(2,1)}, u32[]{:S(2)}, u32[]{:S(2)}) collective-permute-start(bf16[64,2048]{1,0:T(8,128)(2,1)S(1)} %collective-permute-done.11.refs_1_), channel_id=1, source_target_pairs={{0,4},{2,6},{4,0},{6,2},{8,12},{10,14},{12,8},{14,10},{16,20},{18,... | collective-permute-start | bytes 786440 | tf_op jit(solution)/shard_map/ppermute | solution.py:218
  80.0 29.6 %copy-start.19 = (bf16[64,2048]{1,0:T(8,128)(2,1)}, bf16[64,2048]{1,0:T(8,128)(2,1)S(1)}, u32[]{:S(2)}) copy-start(bf16[64,2048]{1,0:T(8,128)(2,1)S(1)} %collective-permute-done.9.refs_7_) | copy-start | bytes 786436
  84.3 2.9 %copy-start.1 = (bf16[16,288,128]{2,1,0:T(8,128)(2,1)}, bf16[16,288,128]{2,1,0:T(8,128)(2,1)S(1)}, u32[]{:S(2)}) copy-start(bf16[16,288,128]{2,1,0:T(8,128)(2,1)S(1)} %all-to-all-done.1.refs_0_) | copy-start | bytes 3538948
  84.3 2.8 %collective-permute-start.15 = (bf16[16,288,128]{2,1,0:T(8,128)(2,1)S(1)}, bf16[16,288,128]{2,1,0:T(8,128)(2,1)S(1)}, u32[]{:S(2)}, u32[]{:S(2)}) collective-permute-start(bf16[16,288,128]{2,1,0:T(8,128)(2,1)S(1)} %all-to-all-done.1.refs_0_), channel_id=1, source_target_pairs={{0,1},{1,0},{2,3},{3,2},{4,5},{5,4},{6,7},{7,6},{8,9},{9,8},{10,11... | collective-permute-start | bytes 3538952 | tf_op jit(solution)/shard_map/ppermute | solution.py:226
  109.6 20.1 %collective-permute-start.16 = (bf16[2,64,2048]{2,1,0:T(8,128)(2,1)}, bf16[2,64,2048]{2,1,0:T(8,128)(2,1)S(1)}, u32[]{:S(2)}, u32[]{:S(2)}) collective-permute-start(bf16[2,64,2048]{2,1,0:T(8,128)(2,1)} %get-tuple-element.102), channel_id=1, source_target_pairs={{0,2},{2,0},{4,6},{6,4},{8,10},{10,8},{12,14},{14,12},{16,18},{18,... | collective-permute-start | bytes 1572872 | tf_op jit(solution)/shard_map/ppermute | solution.py:218
  110.0 20.0 %collective-permute-start.17 = (bf16[2,64,2048]{2,1,0:T(8,128)(2,1)}, bf16[2,64,2048]{2,1,0:T(8,128)(2,1)S(1)}, u32[]{:S(2)}, u32[]{:S(2)}) collective-permute-start(bf16[2,64,2048]{2,1,0:T(8,128)(2,1)} %get-tuple-element.104), channel_id=1, source_target_pairs={{0,4},{2,6},{4,0},{6,2},{8,12},{10,14},{12,8},{14,10},{16,20},{18,... | collective-permute-start | bytes 1572872 | tf_op jit(solution)/shard_map/ppermute | solution.py:218
  111.7 18.1 %copy-start.5 = (bf16[2,64,2048]{2,1,0:T(8,128)(2,1)S(1)}, bf16[2,64,2048]{2,1,0:T(8,128)(2,1)}, u32[]{:S(2)}) copy-start(bf16[2,64,2048]{2,1,0:T(8,128)(2,1)} %get-tuple-element.96.refs_13_) | copy-start | bytes 1572868
  129.9 2.6 %copy-start.8 = (bf16[2,64,2048]{2,1,0:T(8,128)(2,1)S(1)}, bf16[2,64,2048]{2,1,0:T(8,128)(2,1)}, u32[]{:S(2)}) copy-start(bf16[2,64,2048]{2,1,0:T(8,128)(2,1)} %get-tuple-element.112) | copy-start | bytes 1572868
  129.9 3.1 %copy-start.9 = (bf16[2,64,2048]{2,1,0:T(8,128)(2,1)S(1)}, bf16[2,64,2048]{2,1,0:T(8,128)(2,1)}, u32[]{:S(2)}) copy-start(bf16[2,64,2048]{2,1,0:T(8,128)(2,1)} %get-tuple-element.110) | copy-start | bytes 1572868
  130.8 23.0 %copy-start.3 = (bf16[2,64,2048]{2,1,0:T(8,128)(2,1)S(1)}, bf16[2,64,2048]{2,1,0:T(8,128)(2,1)}, u32[]{:S(2)}) copy-start(bf16[2,64,2048]{2,1,0:T(8,128)(2,1)} %get-tuple-element.109) | copy-start | bytes 1572868
  130.9 9.3 %collective-permute-start.20 = (bf16[64,2048]{1,0:T(8,128)(2,1)S(1)}, bf16[64,2048]{1,0:T(8,128)(2,1)S(1)}, u32[]{:S(2)}, u32[]{:S(2)}) collective-permute-start(bf16[64,2048]{1,0:T(8,128)(2,1)S(1)} %get-tuple-element.108), channel_id=1, source_target_pairs={{0,2},{2,0},{4,6},{6,4},{8,10},{10,8},{12,14},{14,12},{16,18},{18,... | collective-permute-start | bytes 786440 | tf_op jit(solution)/shard_map/ppermute | solution.py:218
  132.4 22.1 %collective-permute-start.25 = (bf16[2,64,2048]{2,1,0:T(8,128)(2,1)S(1)}, bf16[2,64,2048]{2,1,0:T(8,128)(2,1)S(1)}, u32[]{:S(2)}, u32[]{:S(2)}) collective-permute-start(bf16[2,64,2048]{2,1,0:T(8,128)(2,1)S(1)} %copy-done.8), channel_id=1, source_target_pairs={{0,4},{2,6},{4,0},{6,2},{8,12},{10,14},{12,8},{14,10},{16,20},{18,... | collective-permute-start | bytes 1572872 | tf_op jit(solution)/shard_map/ppermute | solution.py:218
  133.0 20.7 %collective-permute-start.22 = (bf16[2,64,2048]{2,1,0:T(8,128)(2,1)S(1)}, bf16[2,64,2048]{2,1,0:T(8,128)(2,1)S(1)}, u32[]{:S(2)}, u32[]{:S(2)}) collective-permute-start(bf16[2,64,2048]{2,1,0:T(8,128)(2,1)S(1)} %copy-done.9), channel_id=1, source_target_pairs={{0,2},{2,0},{4,6},{6,4},{8,10},{10,8},{12,14},{14,12},{16,18},{18,... | collective-permute-start | bytes 1572872 | tf_op jit(solution)/shard_map/ppermute | solution.py:218
  133.3 17.9 %collective-permute-start.18 = (bf16[64,2048]{1,0:T(8,128)(2,1)S(1)}, bf16[64,2048]{1,0:T(8,128)(2,1)S(1)}, u32[]{:S(2)}, u32[]{:S(2)}) collective-permute-start(bf16[64,2048]{1,0:T(8,128)(2,1)S(1)} %get-tuple-element.106), channel_id=1, source_target_pairs={{0,4},{2,6},{4,0},{6,2},{8,12},{10,14},{12,8},{14,10},{16,20},{18,... | collective-permute-start | bytes 786440 | tf_op jit(solution)/shard_map/ppermute | solution.py:218
  140.2 14.3 %copy-start.6 = (bf16[2,64,2048]{2,1,0:T(8,128)(2,1)S(1)}, bf16[2,64,2048]{2,1,0:T(8,128)(2,1)}, u32[]{:S(2)}) copy-start(bf16[2,64,2048]{2,1,0:T(8,128)(2,1)} %get-tuple-element.111) | copy-start | bytes 1572868
  140.2 21.7 %collective-permute-start.21 = (bf16[64,2048]{1,0:T(8,128)(2,1)S(1)}, bf16[64,2048]{1,0:T(8,128)(2,1)S(1)}, u32[]{:S(2)}, u32[]{:S(2)}) collective-permute-start(bf16[64,2048]{1,0:T(8,128)(2,1)S(1)} %add_convert_fusion), channel_id=1, source_target_pairs={{0,24},{2,26},{4,28},{6,30},{8,0},{10,2},{12,4},{14,6},{16,8},{18,... | collective-permute-start | bytes 786440 | tf_op jit(solution)/shard_map/ppermute | solution.py:221
  151.2 18.8 %collective-permute-start.19 = (bf16[64,2048]{1,0:T(8,128)(2,1)S(1)}, bf16[64,2048]{1,0:T(8,128)(2,1)S(1)}, u32[]{:S(2)}, u32[]{:S(2)}) collective-permute-start(bf16[64,2048]{1,0:T(8,128)(2,1)S(1)} %add_convert_fusion.1), channel_id=1, source_target_pairs={{0,16},{2,18},{4,20},{6,22},{8,24},{10,26},{12,28},{14,30},{16,0},... | collective-permute-start | bytes 786440 | tf_op jit(solution)/shard_map/ppermute | solution.py:221
  153.8 6.4 %collective-permute-start.23 = (bf16[64,2048]{1,0:T(8,128)(2,1)S(1)}, bf16[64,2048]{1,0:T(8,128)(2,1)S(1)}, u32[]{:S(2)}, u32[]{:S(2)}) collective-permute-start(bf16[64,2048]{1,0:T(8,128)(2,1)S(1)} %fusion.15), channel_id=1, source_target_pairs={{0,4},{2,6},{4,0},{6,2},{8,12},{10,14},{12,8},{14,10},{16,20},{18,... | collective-permute-start | bytes 786440 | tf_op jit(solution)/shard_map/ppermute | solution.py:218
  154.6 15.4 %collective-permute-start.26 = (bf16[64,2048]{1,0:T(8,128)(2,1)S(1)}, bf16[64,2048]{1,0:T(8,128)(2,1)S(1)}, u32[]{:S(2)}, u32[]{:S(2)}) collective-permute-start(bf16[64,2048]{1,0:T(8,128)(2,1)S(1)} %fusion.16), channel_id=1, source_target_pairs={{0,2},{2,0},{4,6},{6,4},{8,10},{10,8},{12,14},{14,12},{16,18},{18,... | collective-permute-start | bytes 786440 | tf_op jit(solution)/shard_map/ppermute | solution.py:218
  160.4 9.6 %collective-permute-start.24 = (bf16[64,2048]{1,0:T(8,128)(2,1)S(1)}, bf16[64,2048]{1,0:T(8,128)(2,1)S(1)}, u32[]{:S(2)}, u32[]{:S(2)}) collective-permute-start(bf16[64,2048]{1,0:T(8,128)(2,1)S(1)} %fusion.8), channel_id=1, source_target_pairs={{0,8},{2,10},{4,12},{6,14},{8,16},{10,18},{12,20},{14,22},{16,24},... | collective-permute-start | bytes 786440 | tf_op jit(solution)/shard_map/ppermute | solution.py:221
  (7 other events, 5.8 us)
Sparse Core Ops, SparseCore 0:
  28.6 15.9 all-gather.6
  46.2 17.1 all-gather.8
  64.9 17.1 all-gather.10
